TPU v7x, 256 devices: a whole 4x4x8 slice. The times are simulated.
256 devices in a mesh: grp: 4 (over x), dev: 64 (over z, y, core).
Axes of the slice: x: 4, y: 4, z: 8, core: 2. Of those that a mesh axis runs over, the one named last changes fastest.
Arguments:
- filt_mean: float32 [512, 256], P(('grp', 'dev')), may hold values from -6 to 6
- filt_cov: float32 [512, 256, 256], P(('grp', 'dev')), may hold values from -6 to 10, as said below
- noise_cov: float32 [512, 256, 256], P(('grp', 'dev')), may hold values from -1.25 to 1.25, as said below
- transition: float32 [256, 256], replicated, may hold values from -1 to 1
Outputs:
- smooth_mean: float32 [512, 256], P(('grp', 'dev'))
- smooth_cov: float32 [512, 256, 256], P(('grp', 'dev'))
Inputs may be any that keep to these rules, and one draw needn't show every extreme that they name: Each filt_cov[t] is symmetric positive definite. Each noise_cov[t] is symmetric positive definite.
All inputs are finite; a program needn't handle non-finite values.
Results may differ from a plain program's by a relative error of at most 0.0003.
Values sent between devices are 32-bit elements; how exact they have to be, the bound alone decides.
No kernel may reach another device: no remote copies, remote signals or barrier semaphores. Data moves between devices by JAX's collectives and lax.ppermute only.
A program may use at most 256 MiB of HBM per device.

v0:
```python
import jax
import jax.numpy as jnp
from jax import lax
from jax.sharding import PartitionSpec as P


def carried_in(part, axis, combine, identity):
    count = lax.axis_size(axis)
    place = lax.axis_index(axis)
    ahead = count - 1 - place
    gathered = jax.tree.map(lambda a: lax.all_gather(a, axis), part)
    state = jax.tree.map(lambda a, e: jnp.zeros_like(a) + jnp.asarray(e, a.dtype), part, identity)

    def one(turn, state):
        source = count - 1 - turn
        return combine(
            state, jax.tree.map(lambda a: lax.dynamic_index_in_dim(a, source, 0, False), gathered)
        )

    return lax.fori_loop(0, ahead, one, state)


def product(left, right):
    return jnp.matmul(left, right, precision=lax.Precision.HIGHEST)


def chol_solve(factor, rhs):
    middle = lax.linalg.triangular_solve(factor, rhs, left_side=True, lower=True)
    return lax.linalg.triangular_solve(factor, middle, left_side=True, lower=True, transpose_a=True)


def flipped(matrix):
    return jnp.swapaxes(matrix, -1, -2)


def apply_vec(matrix, vector):
    return product(matrix, vector[..., None])[..., 0]


def compose(earlier, follower):
    gain_a, off_a, rem_a = earlier
    gain_b, off_b, rem_b = follower
    gain_ab = product(gain_a, gain_b)
    off_ab = apply_vec(gain_a, off_b) + off_a
    rem_ab = product(product(gain_a, rem_b), flipped(gain_a)) + rem_a
    return (gain_ab, off_ab, rem_ab)


def joined(higher, lower):
    return compose(lower, higher)


def local(filt_mean, filt_cov, noise_cov, transition):
    local_steps, state_width = filt_mean.shape
    moved = product(transition, filt_cov)
    predicted = product(moved, transition.T) + noise_cov
    factor = jnp.linalg.cholesky(predicted)
    solved = chol_solve(factor, moved)
    position = lax.axis_index(("grp", "dev"))
    final_device = position == lax.axis_size(("grp", "dev")) - 1
    local_index = lax.broadcasted_iota(jnp.int32, (local_steps,), 0)
    keep_mask = jnp.where(final_device & (local_index == local_steps - 1), 0.0, 1.0).astype(
        jnp.float32
    )
    solved = solved * keep_mask[:, None, None]
    gain_mat = flipped(solved)
    offset = filt_mean - apply_vec(gain_mat, apply_vec(transition, filt_mean))
    remainder = filt_cov - product(gain_mat, moved)
    unit_matrix = jnp.eye(state_width, dtype=jnp.float32)
    blank_vec = jnp.zeros((state_width,), jnp.float32)
    blank_mat = jnp.zeros((state_width, state_width), jnp.float32)
    identity = (unit_matrix, blank_vec, blank_mat)

    def fold_step(running, element):
        merged = compose(element, running)
        return (merged, merged)

    summary, cumulative = lax.scan(fold_step, identity, (gain_mat, offset, remainder), reverse=True)
    sum_gain, sum_off, sum_rem = summary
    remote = carried_in((sum_gain, sum_off, sum_rem), ("grp", "dev"), joined, identity)
    remote_off = remote[1]
    remote_rem = remote[2]
    cum_gain, cum_off, cum_rem = cumulative
    smooth_mean = cum_off + apply_vec(cum_gain, remote_off)
    smooth_cov = product(product(cum_gain, remote_rem), flipped(cum_gain)) + cum_rem
    return (smooth_mean, smooth_cov)


def solution(mesh):
    in_specs = (
        P(("grp", "dev"), None),
        P(("grp", "dev"), None, None),
        P(("grp", "dev"), None, None),
        P(),
    )
    out_specs = (P(("grp", "dev"), None), P(("grp", "dev"), None, None))
    return jax.shard_map(local, mesh=mesh, in_specs=in_specs, out_specs=out_specs, check_vma=False)
```

profile of v0, /device:TPU:0, one launch (start us, length us, event | category | flops | bytes accessed | tf_op | source)
XLA Modules:
  0.0 1621.5 jit_solution(9943722599999074122)
XLA Ops:
  8.7 1.7 convolution_bitcast_fusion
  11.3 23.5 %custom-call.18 = f32[2,128,128]{2,1,0:T(8,128)S(1)} custom-call(f32[2,128,128]{2,1,0:T(8,128)S(1)} %cholesky.119), custom_call_target="Cholesky" | custom-call | tf_op jit(solution)/shard_map/jit(cholesky)/cholesky | solution.py:57
  34.7 19.7 %custom-call.19 = f32[2,1,128,128]{2,3,1,0:T(8,128)S(1)} custom-call(f32[2,1,128,128]{3,2,1,0:T(8,128)S(1)} %select_bitcast_fusion), custom_call_target="InvertDiagBlocksLowerTriangular" | custom-call | tf_op jit(solution)/shard_map/jit(cholesky)/cholesky | solution.py:57
  55.1 23.5 %custom-call.20 = f32[2,128,128]{2,1,0:T(8,128)S(1)} custom-call(f32[2,128,128]{2,1,0:T(8,128)S(1)} %convolution_subtract_fusion.3), custom_call_target="Cholesky" | custom-call | tf_op jit(solution)/shard_map/jit(cholesky)/cholesky | solution.py:57
  79.0 3.9 while.43
  82.9 39.5 %custom-call.21 = f32[2,2,128,128]{2,3,1,0:T(8,128)S(1)} custom-call(f32[2,2,128,128]{3,2,1,0:T(8,128)S(1)} %bitcast.179), custom_call_target="InvertDiagBlocksLowerTriangular" | custom-call | tf_op jit(solution)/shard_map/triangular_solve | solution.py:29
  124.9 2.2 convolution_subtract_fusion
  129.4 4.0 while.44
  134.9 64.0 %all-gather.3 = f32[256,1,256]{2,1,0:T(1,128)S(1)} all-gather(f32[1,1,256]{2,1,0:T(1,128)S(1)} %bitcast.178), channel_id=3, replica_groups=mesh['grp'=4,'dev'=64] {'grp','dev'}, dimensions={0}, use_global_device_ids=true | all-gather | bytes 263168 | tf_op jit(solution)/shard_map/all_gather | solution.py:11
  198.8 149.2 %all-gather.7.cloned.1.call-done = f32[65536,256]{1,0:T(8,128)} async-done(((f32[256,256]{1,0:T(8,128)}), f32[65536,256]{1,0:T(8,128)}) %all-gather.7.cloned.1.call-update) | async-done | bytes 67108880 | tf_op jit(solution)/shard_map/all_gather | solution.py:11
  348.1 213.3 %all-gather.9.cloned.1.call-done = f32[65536,256]{1,0:T(8,128)} async-done(((f32[256,256]{1,0:T(8,128)}), f32[65536,256]{1,0:T(8,128)}) %all-gather.9.cloned.1.call-update) | async-done | bytes 67108880 | tf_op jit(solution)/shard_map/all_gather | solution.py:11
  561.4 1050.1 %while.42 = (s32[]{:T(128)}, f32[256]{0:T(256)S(1)}, f32[256,256]{1,0:T(8,128)S(1)}, s32[]{:T(128)}, f32[256,256,256]{2,1,0:T(8,128)}, /*index=5*/f32[256,256]{1...) while((s32[]{:T(128)}, f32[256]{0:T(256)S(1)}, ...), condition=%wide.region_7.8_spmd, body=%wide.region_6.7_spmd.sunk | while | flops 403505408 | bytes 2105519 | solution.py:20
  576.4 1.4 convolution_add_fusion.5
  621.7 1.4 convolution_add_fusion.5
  638.2 1.4 convolution_add_fusion.5
  654.6 1.4 convolution_add_fusion.5
  699.9 1.4 convolution_add_fusion.5
  716.4 1.4 convolution_add_fusion.5
  732.9 1.4 convolution_add_fusion.5
  778.2 1.4 convolution_add_fusion.5
  794.6 1.4 convolution_add_fusion.5
  811.1 1.4 convolution_add_fusion.5
  856.4 1.4 convolution_add_fusion.5
  872.9 1.4 convolution_add_fusion.5
  889.4 1.4 convolution_add_fusion.5
  934.6 1.4 convolution_add_fusion.5
  951.1 1.4 convolution_add_fusion.5
  967.6 1.4 convolution_add_fusion.5
  1012.9 1.4 convolution_add_fusion.5
  1029.4 1.4 convolution_add_fusion.5
  1045.8 1.4 convolution_add_fusion.5
  1613.2 1.5 convolution_add_fusion.2
  (1332 shorter events, 1028.6 us)
Async XLA Ops:
  7.2 1.5 copy-start
  7.2 340.9 %all-gather.7.cloned.1.call-start = ((), (), s32[]{:S(2)}) async-start(), calls=%async_computation | async-start | bytes 67371008 | tf_op jit(solution)/shard_map/all_gather | solution.py:11
  133.4 0.7 copy-start.1
  133.4 0.8 copy-start.2
  134.1 427.2 %all-gather.9.cloned.1.call-start = ((), (), s32[]{:S(2)}) async-start(), calls=%async_computation.1 | async-start | bytes 67371008 | tf_op jit(solution)/shard_map/all_gather | solution.py:11
Sparse Core Ops, SparseCore 0:
  134.2 213.7 all-gather.6
  351.8 209.5 all-gather.8
where the time goes:
time: 1640 us; the launch traced here: 1620 us
  matrix products  1040 us (63%)
  waiting for transfers between devices  363 us (22%)
  other arithmetic  109 us (7%)
  blocking collectives  64 us (4%)
  local copies, waits for them, and re-layouts  21.8 us (1%)
    dot_general x781, matrix products, product(): return jnp.matmul(left, right, precision=lax.Precision.HIGHEST)  1030 us
    all_gather x2, waiting for transfers between devices, carried_in(): gathered = jax.tree.map(lambda a: lax.all_gather(a, axis), part)  362 us
    another operation x9, other arithmetic, local(): factor = jnp.linalg.cholesky(predicted)  66.8 us
    all_gather x1, blocking collectives, carried_in(): gathered = jax.tree.map(lambda a: lax.all_gather(a, axis), part)  64 us
    another operation x4, other arithmetic, chol_solve(): lax.linalg.triangular_solve(factor, middle, left_side=True, lower=True, t...  39.7 us
  transfers between devices with their start and end apart: 2, of which 2 were waited for; matrix products, arithmetic and copies ran while one was open for 0% of the time, Pallas kernels for 0%

commit v1 on v0

v1 whole, which is shorter than its diff:
```python
import jax
import jax.numpy as jnp
from jax import lax
from jax.sharding import PartitionSpec as P

AXES = ("grp", "dev")
EXTRA = 8


def product(left, right):
    return jnp.matmul(left, right, precision=lax.Precision.HIGHEST)


def flipped(matrix):
    return jnp.swapaxes(matrix, -1, -2)


def chol_solve(factor, rhs):
    middle = lax.linalg.triangular_solve(factor, rhs, left_side=True, lower=True)
    return lax.linalg.triangular_solve(factor, middle, left_side=True, lower=True, transpose_a=True)


def grown(matrix, row):
    return jnp.concatenate([matrix, jnp.broadcast_to(row, (EXTRA, row.shape[-1]))], axis=0)


def applied(turned, held_next, held):
    width = turned.shape[0]
    first = product(held_next, turned)
    square = product(flipped(turned), first[:width]) + held[:width]
    return jnp.concatenate([square, first[width:] + held[width:]], axis=0)


def local(filt_mean, filt_cov, noise_cov, transition):
    width = filt_mean.shape[1]
    devices = lax.axis_size(AXES)
    chips = devices // 2
    place = lax.axis_index(AXES)
    core = place % 2
    moved = product(transition, filt_cov)
    predicted = product(moved, transition.T) + noise_cov
    factor = jnp.linalg.cholesky(predicted)
    solved = chol_solve(factor, moved)
    final = (place == devices - 1) & (jnp.arange(2) == 1)
    solved = jnp.where(final[:, None, None], 0.0, solved)
    ahead = product(filt_mean, transition.T)
    offset = filt_mean - product(ahead[:, None, :], solved)[:, 0]
    remainder = filt_cov - product(flipped(solved), moved)
    turned = [solved[0], solved[1]]
    held = [grown(remainder[0], offset[0]), grown(remainder[1], offset[1])]
    both_turned = product(turned[1], turned[0])
    both_held = applied(turned[0], held[1], held[0])
    swap = [(p, p ^ 1) for p in range(devices)]
    other_turned = lax.ppermute(both_turned, AXES, swap)
    other_held = lax.ppermute(both_held, AXES, swap)
    is_first = core == 0
    a_turned = jnp.where(is_first, both_turned, other_turned)
    b_turned = jnp.where(is_first, other_turned, both_turned)
    a_held = jnp.where(is_first, both_held, other_held)
    b_held = jnp.where(is_first, other_held, both_held)
    chip_turned = product(b_turned, a_turned)
    chip_held = applied(a_turned, b_held, a_held)
    late = [jnp.where(is_first, product(other_turned, t), t) for t in (both_turned, turned[1])]
    late_held = [
        jnp.where(is_first, applied(t, other_held, h), h)
        for t, h in ((both_turned, both_held), (turned[1], held[1]))
    ]
    blank = jnp.zeros((EXTRA, width), jnp.float32)
    mine = jnp.where(is_first, jnp.concatenate([chip_turned, blank], axis=0), chip_held)
    gain = chip_turned
    stride = 1
    while stride < chips:
        pairs = [(2 * (c + stride) + 1, 2 * c + 1) for c in range(chips - stride)]
        pairs += [(2 * (c + stride), 2 * c) for c in range(chips - 2 * stride)]
        got = lax.ppermute(mine, AXES, pairs)
        first = product(got, gain)
        if stride * 2 < chips:
            passed = lax.ppermute(first[:width], AXES, [(2 * c, 2 * c + 1) for c in range(chips)])
            later = jnp.where(is_first, first[:width], passed)
        square = product(flipped(gain), first[:width]) + mine[:width]
        row = first[width:] + mine[width:]
        mine = jnp.where(is_first, first, jnp.concatenate([square, row], axis=0))
        gain = later
        stride *= 2
    to_second = lax.ppermute(mine, AXES, [(2 * c + 3, 2 * c + 1) for c in range(chips - 1)])
    to_first = lax.ppermute(mine, AXES, [(2 * c + 3, 2 * c) for c in range(chips - 1)])
    after = jnp.where(is_first, to_first, to_second)
    outs = [applied(t, after, h) for t, h in zip(late, late_held)]
    smooth_cov = jnp.stack([o[:width] for o in outs])
    smooth_mean = jnp.stack([o[width] for o in outs])
    return (smooth_mean, smooth_cov)


def solution(mesh):
    in_specs = (P(AXES, None), P(AXES, None, None), P(AXES, None, None), P())
    out_specs = (P(AXES, None), P(AXES, None, None))
    return jax.shard_map(local, mesh=mesh, in_specs=in_specs, out_specs=out_specs, check_vma=False)
```

time: 1640 us -> 242 us (0.15)
  the two profiles are of different devices: /device:TPU:0 before, /device:TPU:3 now
where the time goes in v1:
time: 242 us
  other arithmetic  109 us (45%)
  starting transfers between devices  65.4 us (27%)
  waiting for transfers between devices  39.7 us (16%)
  matrix products  20.5 us (8%)
  local copies, waits for them, and re-layouts  5.95 us (2%)
    another operation x9, other arithmetic, local(): factor = jnp.linalg.cholesky(predicted)  66.8 us
    another operation x4, other arithmetic, chol_solve(): lax.linalg.triangular_solve(factor, middle, left_side=True, lower=True, t...  39.7 us
    ppermute x7, starting transfers between devices, local(): got = lax.ppermute(mine, AXES, pairs)  33.1 us
    ppermute x6, waiting for transfers between devices, local(): lax.ppermute(first[:width], AXES, [(2 * c, 2 * c + 1) for c in range(chip...  19.9 us
    ppermute x1, starting transfers between devices, local(): lax.ppermute(mine, AXES, [(2 * c + 3, 2 * c) for c in range(chips - 1)])  18.1 us
    dot_general x35, matrix products, product(): return jnp.matmul(left, right, precision=lax.Precision.HIGHEST)  17.5 us
    ppermute x7, waiting for transfers between devices, local(): got = lax.ppermute(mine, AXES, pairs)  15.4 us
    ppermute x6, starting transfers between devices, local(): lax.ppermute(first[:width], AXES, [(2 * c, 2 * c + 1) for c in range(chip...  7.97 us
  transfers between devices with their start and end apart: 17, of which 13 were waited for; matrix products, arithmetic and copies ran while one was open for 2% of the time, Pallas kernels for 0%

profile of v1, /device:TPU:3, one launch (start us, length us, event | category | flops | bytes accessed | tf_op | source)
XLA Modules:
  0.0 241.7 jit_solution(7593886686476693184)
XLA Ops:
  0.8 1.3 copy.15
  3.7 23.5 %custom-call.18 = f32[2,128,128]{2,1,0:T(8,128)S(1)} custom-call(f32[2,128,128]{2,1,0:T(8,128)S(1)} %cholesky.119), custom_call_target="Cholesky" | custom-call | tf_op jit(solution)/shard_map/jit(cholesky)/cholesky | solution.py:42
  27.2 19.7 %custom-call.19 = f32[2,1,128,128]{2,3,1,0:T(8,128)S(1)} custom-call(f32[2,1,128,128]{3,2,1,0:T(8,128)S(1)} %select_bitcast_fusion), custom_call_target="InvertDiagBlocksLowerTriangular" | custom-call | tf_op jit(solution)/shard_map/jit(cholesky)/cholesky | solution.py:42
  47.5 23.5 %custom-call.20 = f32[2,128,128]{2,1,0:T(8,128)S(1)} custom-call(f32[2,128,128]{2,1,0:T(8,128)S(1)} %convolution_subtract_fusion.3), custom_call_target="Cholesky" | custom-call | tf_op jit(solution)/shard_map/jit(cholesky)/cholesky | solution.py:42
  71.4 4.1 %while.1 = (s32[]{:T(128)}, f32[2,256,256]{2,1,0:T(8,128)S(1)}, s32[2,2]{1,0:T(2,128)S(1)}, f32[2,2,128,128]{3,2,0,1:T(8,128)S(1)}, s32[]{:T(128)}) while((s32[]{:T(128)}, f32[2,256,256]{2,1,0:T(8,128)S(1)}, s32[2,2]{1,0:T(2,128)S(1)}, f32[2,2,128,128]{3,2,0,1:T(8,128)S(1)}, s32[]{:T(128)}) %tuple.29), condition=%wide.while_cond, body=%wide.while_body.sunk | while | flops 2 | bytes 262261 | solution.py:20
  72.0 1.4 bitcast_dynamic-update-slice_fusion.2
  74.1 1.4 bitcast_dynamic-update-slice_fusion.2
  75.5 39.5 %custom-call.21 = f32[2,2,128,128]{2,3,1,0:T(8,128)S(1)} custom-call(f32[2,2,128,128]{3,2,1,0:T(8,128)S(1)} %bitcast.111), custom_call_target="InvertDiagBlocksLowerTriangular" | custom-call | tf_op jit(solution)/shard_map/triangular_solve | solution.py:20
  125.4 9.9 %collective-permute-start.2 = (f32[264,256]{1,0:T(8,128)S(1)}, f32[264,256]{1,0:T(8,128)S(1)}, u32[]{:S(2)}, u32[]{:S(2)}) collective-permute-start(f32[264,256]{1,0:T(8,128)S(1)} %maximum_select_fusion.1), channel_id=1, source_target_pairs={{3,1},{5,3},{7,5},{9,7},{11,9},{13,11},{15,13},{17,15},{19,17},{21... | collective-permute-start | bytes 811016 | tf_op jit(solution)/shard_map/ppermute | solution.py:75
  135.3 5.7 %collective-permute-done.2 = f32[264,256]{1,0:T(8,128)S(1)} collective-permute-done((f32[264,256]{1,0:T(8,128)S(1)}, f32[264,256]{1,0:T(8,128)S(1)}, u32[]{:S(2)}, u32[]{:S(2)}) %collective-permute-start.2) | collective-permute-done | bytes 270368 | tf_op jit(solution)/shard_map/ppermute | solution.py:75
  142.1 4.3 %collective-permute-start.3 = (f32[264,256]{1,0:T(8,128)S(1)}, f32[264,256]{1,0:T(8,128)S(1)}, u32[]{:S(2)}, u32[]{:S(2)}) collective-permute-start(f32[264,256]{1,0:T(8,128)S(1)} %maximum_select_fusion.2), channel_id=1, source_target_pairs={{5,1},{7,3},{9,5},{11,7},{13,9},{15,11},{17,13},{19,15},{21,17},{2... | collective-permute-start | bytes 811016 | tf_op jit(solution)/shard_map/ppermute | solution.py:75
  146.4 1.5 collective-permute-start.4
  147.9 2.0 collective-permute-done.4
  149.9 2.6 %collective-permute-done.3 = f32[264,256]{1,0:T(8,128)S(1)} collective-permute-done((f32[264,256]{1,0:T(8,128)S(1)}, f32[264,256]{1,0:T(8,128)S(1)}, u32[]{:S(2)}, u32[]{:S(2)}) %collective-permute-start.3) | collective-permute-done | bytes 270368 | tf_op jit(solution)/shard_map/ppermute | solution.py:75
  153.6 2.6 %collective-permute-start.5 = (f32[264,256]{1,0:T(8,128)S(1)}, f32[264,256]{1,0:T(8,128)S(1)}, u32[]{:S(2)}, u32[]{:S(2)}) collective-permute-start(f32[264,256]{1,0:T(8,128)S(1)} %maximum_select_fusion.3), channel_id=1, source_target_pairs={{9,1},{11,3},{13,5},{15,7},{17,9},{19,11},{21,13},{23,15},{25,17},... | collective-permute-start | bytes 811016 | tf_op jit(solution)/shard_map/ppermute | solution.py:75
  156.2 1.3 collective-permute-start.6
  157.5 3.2 %collective-permute-done.6 = f32[256,256]{1,0:T(8,128)S(1)} collective-permute-done((f32[256,256]{1,0:T(8,128)S(1)}, f32[256,256]{1,0:T(8,128)S(1)}, u32[]{:S(2)}, u32[]{:S(2)}) %collective-permute-start.6) | collective-permute-done | bytes 262176 | tf_op jit(solution)/shard_map/ppermute | solution.py:78
  162.7 3.1 %collective-permute-start.7 = (f32[264,256]{1,0:T(8,128)S(1)}, f32[264,256]{1,0:T(8,128)S(1)}, u32[]{:S(2)}, u32[]{:S(2)}) collective-permute-start(f32[264,256]{1,0:T(8,128)S(1)} %maximum_select_fusion.4), channel_id=1, source_target_pairs={{17,1},{19,3},{21,5},{23,7},{25,9},{27,11},{29,13},{31,15},{33,17}... | collective-permute-start | bytes 811016 | tf_op jit(solution)/shard_map/ppermute | solution.py:75
  165.8 1.3 collective-permute-start.8
  167.1 4.1 %collective-permute-done.8 = f32[256,256]{1,0:T(8,128)S(1)} collective-permute-done((f32[256,256]{1,0:T(8,128)S(1)}, f32[256,256]{1,0:T(8,128)S(1)}, u32[]{:S(2)}, u32[]{:S(2)}) %collective-permute-start.8) | collective-permute-done | bytes 262176 | tf_op jit(solution)/shard_map/ppermute | solution.py:78
  172.2 10.0 %collective-permute-start.9 = (f32[264,256]{1,0:T(8,128)S(1)}, f32[264,256]{1,0:T(8,128)S(1)}, u32[]{:S(2)}, u32[]{:S(2)}) collective-permute-start(f32[264,256]{1,0:T(8,128)S(1)} %maximum_select_fusion.5), channel_id=1, source_target_pairs={{33,1},{35,3},{37,5},{39,7},{41,9},{43,11},{45,13},{47,15},{49,17}... | collective-permute-start | bytes 811016 | tf_op jit(solution)/shard_map/ppermute | solution.py:75
  182.3 1.3 collective-permute-start.10
  183.6 3.7 %collective-permute-done.10 = f32[256,256]{1,0:T(8,128)S(1)} collective-permute-done((f32[256,256]{1,0:T(8,128)S(1)}, f32[256,256]{1,0:T(8,128)S(1)}, u32[]{:S(2)}, u32[]{:S(2)}) %collective-permute-start.10) | collective-permute-done | bytes 262176 | tf_op jit(solution)/shard_map/ppermute | solution.py:78
  187.4 4.6 %collective-permute-done.9 = f32[264,256]{1,0:T(8,128)S(1)} collective-permute-done((f32[264,256]{1,0:T(8,128)S(1)}, f32[264,256]{1,0:T(8,128)S(1)}, u32[]{:S(2)}, u32[]{:S(2)}) %collective-permute-start.9) | collective-permute-done | bytes 270368 | tf_op jit(solution)/shard_map/ppermute | solution.py:75
  193.1 1.9 collective-permute-start.11
  195.0 1.3 collective-permute-start.12
  197.1 3.4 %collective-permute-done.12 = f32[256,256]{1,0:T(8,128)S(1)} collective-permute-done((f32[256,256]{1,0:T(8,128)S(1)}, f32[256,256]{1,0:T(8,128)S(1)}, u32[]{:S(2)}, u32[]{:S(2)}) %collective-permute-start.12) | collective-permute-done | bytes 262176 | tf_op jit(solution)/shard_map/ppermute | solution.py:78
  205.2 3.5 %collective-permute-done.14 = f32[256,256]{1,0:T(8,128)S(1)} collective-permute-done((f32[256,256]{1,0:T(8,128)S(1)}, f32[256,256]{1,0:T(8,128)S(1)}, u32[]{:S(2)}, u32[]{:S(2)}) %collective-permute-start.14) | collective-permute-done | bytes 262176 | tf_op jit(solution)/shard_map/ppermute | solution.py:78
  208.7 1.6 collective-permute-done.13
  211.3 18.1 %collective-permute-start.15 = (f32[264,256]{1,0:T(8,128)S(1)}, f32[264,256]{1,0:T(8,128)S(1)}, u32[]{:S(2)}, u32[]{:S(2)}) collective-permute-start(f32[264,256]{1,0:T(8,128)S(1)} %maximum_select_fusion.8), channel_id=1, source_target_pairs={{3,0},{5,2},{7,4},{9,6},{11,8},{13,10},{15,12},{17,14},{19,16},{21... | collective-permute-start | bytes 811016 | tf_op jit(solution)/shard_map/ppermute | solution.py:86
  229.5 5.2 %collective-permute-start.16 = (f32[264,256]{1,0:T(8,128)S(1)}, f32[264,256]{1,0:T(8,128)S(1)}, u32[]{:S(2)}, u32[]{:S(2)}) collective-permute-start(f32[264,256]{1,0:T(8,128)S(1)} %maximum_select_fusion.8), channel_id=1, source_target_pairs={{3,1},{5,3},{7,5},{9,7},{11,9},{13,11},{15,13},{17,15},{19,17},{21... | collective-permute-start | bytes 811016 | tf_op jit(solution)/shard_map/ppermute | solution.py:85
  234.8 3.3 %collective-permute-done.16 = f32[264,256]{1,0:T(8,128)S(1)} collective-permute-done((f32[264,256]{1,0:T(8,128)S(1)}, f32[264,256]{1,0:T(8,128)S(1)}, u32[]{:S(2)}, u32[]{:S(2)}) %collective-permute-start.16) | collective-permute-done | bytes 270368 | tf_op jit(solution)/shard_map/ppermute | solution.py:85
  (123 shorter events, 30.3 us)
Async XLA Ops:
  0.6 1.4 copy-start
  0.7 1.3 copy-start.1
  118.0 1.8 copy-start.3
  118.0 3.7 %collective-permute-start = (f32[256,256]{1,0:T(8,128)S(1)}, f32[256,256]{1,0:T(8,128)S(1)}, u32[]{:S(2)}, u32[]{:S(2)}) collective-permute-start(f32[256,256]{1,0:T(8,128)S(1)} %fusion.19), channel_id=1, source_target_pairs={{0,1},{1,0},{2,3},{3,2},{4,5},{5,4},{6,7},{7,6},{8,9},{9,8},{10,11... | collective-permute-start | bytes 786440 | tf_op jit(solution)/shard_map/ppermute | solution.py:54
  121.6 1.6 collective-permute-start.1
  125.4 15.6 %collective-permute-start.2 = (f32[264,256]{1,0:T(8,128)S(1)}, f32[264,256]{1,0:T(8,128)S(1)}, u32[]{:S(2)}, u32[]{:S(2)}) collective-permute-start(f32[264,256]{1,0:T(8,128)S(1)} %maximum_select_fusion.1), channel_id=1, source_target_pairs={{3,1},{5,3},{7,5},{9,7},{11,9},{13,11},{15,13},{17,15},{19,17},{21... | collective-permute-start | bytes 811016 | tf_op jit(solution)/shard_map/ppermute | solution.py:75
  142.1 10.4 %collective-permute-start.3 = (f32[264,256]{1,0:T(8,128)S(1)}, f32[264,256]{1,0:T(8,128)S(1)}, u32[]{:S(2)}, u32[]{:S(2)}) collective-permute-start(f32[264,256]{1,0:T(8,128)S(1)} %maximum_select_fusion.2), channel_id=1, source_target_pairs={{5,1},{7,3},{9,5},{11,7},{13,9},{15,11},{17,13},{19,15},{21,17},{2... | collective-permute-start | bytes 811016 | tf_op jit(solution)/shard_map/ppermute | solution.py:75
  146.4 3.5 %collective-permute-start.4 = (f32[256,256]{1,0:T(8,128)S(1)}, f32[256,256]{1,0:T(8,128)S(1)}, u32[]{:S(2)}, u32[]{:S(2)}) collective-permute-start(f32[256,256]{1,0:T(8,128)S(1)} %slice.305), channel_id=1, source_target_pairs={{0,1},{2,3},{4,5},{6,7},{8,9},{10,11},{12,13},{14,15},{16,17},{18,... | collective-permute-start | bytes 786440 | tf_op jit(solution)/shard_map/ppermute | solution.py:78
  153.6 8.0 %collective-permute-start.5 = (f32[264,256]{1,0:T(8,128)S(1)}, f32[264,256]{1,0:T(8,128)S(1)}, u32[]{:S(2)}, u32[]{:S(2)}) collective-permute-start(f32[264,256]{1,0:T(8,128)S(1)} %maximum_select_fusion.3), channel_id=1, source_target_pairs={{9,1},{11,3},{13,5},{15,7},{17,9},{19,11},{21,13},{23,15},{25,17},... | collective-permute-start | bytes 811016 | tf_op jit(solution)/shard_map/ppermute | solution.py:75
  156.2 4.5 %collective-permute-start.6 = (f32[256,256]{1,0:T(8,128)S(1)}, f32[256,256]{1,0:T(8,128)S(1)}, u32[]{:S(2)}, u32[]{:S(2)}) collective-permute-start(f32[256,256]{1,0:T(8,128)S(1)} %slice.309), channel_id=1, source_target_pairs={{0,1},{2,3},{4,5},{6,7},{8,9},{10,11},{12,13},{14,15},{16,17},{18,... | collective-permute-start | bytes 786440 | tf_op jit(solution)/shard_map/ppermute | solution.py:78
  162.7 8.5 %collective-permute-start.7 = (f32[264,256]{1,0:T(8,128)S(1)}, f32[264,256]{1,0:T(8,128)S(1)}, u32[]{:S(2)}, u32[]{:S(2)}) collective-permute-start(f32[264,256]{1,0:T(8,128)S(1)} %maximum_select_fusion.4), channel_id=1, source_target_pairs={{17,1},{19,3},{21,5},{23,7},{25,9},{27,11},{29,13},{31,15},{33,17}... | collective-permute-start | bytes 811016 | tf_op jit(solution)/shard_map/ppermute | solution.py:75
  165.8 5.4 %collective-permute-start.8 = (f32[256,256]{1,0:T(8,128)S(1)}, f32[256,256]{1,0:T(8,128)S(1)}, u32[]{:S(2)}, u32[]{:S(2)}) collective-permute-start(f32[256,256]{1,0:T(8,128)S(1)} %slice.313), channel_id=1, source_target_pairs={{0,1},{2,3},{4,5},{6,7},{8,9},{10,11},{12,13},{14,15},{16,17},{18,... | collective-permute-start | bytes 786440 | tf_op jit(solution)/shard_map/ppermute | solution.py:78
  172.2 19.7 %collective-permute-start.9 = (f32[264,256]{1,0:T(8,128)S(1)}, f32[264,256]{1,0:T(8,128)S(1)}, u32[]{:S(2)}, u32[]{:S(2)}) collective-permute-start(f32[264,256]{1,0:T(8,128)S(1)} %maximum_select_fusion.5), channel_id=1, source_target_pairs={{33,1},{35,3},{37,5},{39,7},{41,9},{43,11},{45,13},{47,15},{49,17}... | collective-permute-start | bytes 811016 | tf_op jit(solution)/shard_map/ppermute | solution.py:75
  182.3 5.0 %collective-permute-start.10 = (f32[256,256]{1,0:T(8,128)S(1)}, f32[256,256]{1,0:T(8,128)S(1)}, u32[]{:S(2)}, u32[]{:S(2)}) collective-permute-start(f32[256,256]{1,0:T(8,128)S(1)} %slice.317), channel_id=1, source_target_pairs={{0,1},{2,3},{4,5},{6,7},{8,9},{10,11},{12,13},{14,15},{16,17},{18,... | collective-permute-start | bytes 786440 | tf_op jit(solution)/shard_map/ppermute | solution.py:78
  193.1 7.4 %collective-permute-start.11 = (f32[264,256]{1,0:T(8,128)S(1)}, f32[264,256]{1,0:T(8,128)S(1)}, u32[]{:S(2)}, u32[]{:S(2)}) collective-permute-start(f32[264,256]{1,0:T(8,128)S(1)} %maximum_select_fusion.6), channel_id=1, source_target_pairs={{65,1},{67,3},{69,5},{71,7},{73,9},{75,11},{77,13},{79,15},{81,17}... | collective-permute-start | bytes 811016 | tf_op jit(solution)/shard_map/ppermute | solution.py:75
  195.0 5.4 %collective-permute-start.12 = (f32[256,256]{1,0:T(8,128)S(1)}, f32[256,256]{1,0:T(8,128)S(1)}, u32[]{:S(2)}, u32[]{:S(2)}) collective-permute-start(f32[256,256]{1,0:T(8,128)S(1)} %slice.321), channel_id=1, source_target_pairs={{0,1},{2,3},{4,5},{6,7},{8,9},{10,11},{12,13},{14,15},{16,17},{18,... | collective-permute-start | bytes 786440 | tf_op jit(solution)/shard_map/ppermute | solution.py:78
  201.6 8.7 %collective-permute-start.13 = (f32[264,256]{1,0:T(8,128)S(1)}, f32[264,256]{1,0:T(8,128)S(1)}, u32[]{:S(2)}, u32[]{:S(2)}) collective-permute-start(f32[264,256]{1,0:T(8,128)S(1)} %maximum_select_fusion.7), channel_id=1, source_target_pairs={{129,1},{131,3},{133,5},{135,7},{137,9},{139,11},{141,13},{143,15}... | collective-permute-start | bytes 811016 | tf_op jit(solution)/shard_map/ppermute | solution.py:75
  202.9 5.8 %collective-permute-start.14 = (f32[256,256]{1,0:T(8,128)S(1)}, f32[256,256]{1,0:T(8,128)S(1)}, u32[]{:S(2)}, u32[]{:S(2)}) collective-permute-start(f32[256,256]{1,0:T(8,128)S(1)} %slice.325), channel_id=1, source_target_pairs={{0,1},{2,3},{4,5},{6,7},{8,9},{10,11},{12,13},{14,15},{16,17},{18,... | collective-permute-start | bytes 786440 | tf_op jit(solution)/shard_map/ppermute | solution.py:78
  211.3 23.5 %collective-permute-start.15 = (f32[264,256]{1,0:T(8,128)S(1)}, f32[264,256]{1,0:T(8,128)S(1)}, u32[]{:S(2)}, u32[]{:S(2)}) collective-permute-start(f32[264,256]{1,0:T(8,128)S(1)} %maximum_select_fusion.8), channel_id=1, source_target_pairs={{3,0},{5,2},{7,4},{9,6},{11,8},{13,10},{15,12},{17,14},{19,16},{21... | collective-permute-start | bytes 811016 | tf_op jit(solution)/shard_map/ppermute | solution.py:86
  229.5 8.6 %collective-permute-start.16 = (f32[264,256]{1,0:T(8,128)S(1)}, f32[264,256]{1,0:T(8,128)S(1)}, u32[]{:S(2)}, u32[]{:S(2)}) collective-permute-start(f32[264,256]{1,0:T(8,128)S(1)} %maximum_select_fusion.8), channel_id=1, source_target_pairs={{3,1},{5,3},{7,5},{9,7},{11,9},{13,11},{15,13},{17,15},{19,17},{21... | collective-permute-start | bytes 811016 | tf_op jit(solution)/shard_map/ppermute | solution.py:85
  234.8 3.7 %copy-start.2 = (f32[264,256]{1,0:T(8,128)}, f32[264,256]{1,0:T(8,128)S(1)}, u32[]{:S(2)}) copy-start(f32[264,256]{1,0:T(8,128)S(1)} %maximum_select_fusion.10) | copy-start | bytes 811012
  239.6 0.7 slice-start

commit v2 on v1

--- a/solution.py
+++ b/solution.py
@@ -1,10 +1,95 @@
 import jax
 import jax.numpy as jnp
 from jax import lax
+from jax.experimental import pallas as pl
+from jax.experimental.pallas import tpu as pltpu
 from jax.sharding import PartitionSpec as P
 
 AXES = ("grp", "dev")
 EXTRA = 8
+
+BASE = 32
+HALF = 128
+
+
+def dot(left, right):
+    return jnp.dot(left, right, precision=lax.Precision.HIGHEST, preferred_element_type=jnp.float32)
+
+
+def base_inverse(first, second):
+    unit = (lax.broadcasted_iota(jnp.int32, (BASE, BASE), 0) == lax.broadcasted_iota(jnp.int32, (BASE, BASE), 1)).astype(jnp.float32)
+    whole = jnp.concatenate([first, unit, second, unit], axis=1)
+    tiles = [whole[8 * i : 8 * i + 8] for i in range(BASE // 8)]
+    lane = lax.broadcasted_iota(jnp.int32, (8, 128), 1)
+    sub = lax.broadcasted_iota(jnp.int32, (8, 128), 0)
+    for q in range(BASE // 8):
+        cols = []
+        for j in range(8):
+            at = 8 * q + j
+            cols.append([
+                jnp.where(lane < 64, jnp.broadcast_to(t[:, at : at + 1], (8, 128)), jnp.broadcast_to(t[:, 64 + at : 65 + at], (8, 128)))
+                for t in tiles
+            ])
+        for k in range(8):
+            def row(t):
+                return jnp.broadcast_to(t[k : k + 1], (8, 128))
+            ratio = 1.0 / row(cols[k][q])
+            scaled = row(tiles[q]) * ratio
+            factors = [row(cols[j][q]) * ratio for j in range(k + 1, 8)]
+            down = list(cols[k])
+            down[q] = down[q] - jnp.where(sub == k, 1.0, 0.0)
+            tiles = [t - d * scaled for t, d in zip(tiles, down)]
+            for j, f in zip(range(k + 1, 8), factors):
+                cols[j] = [c - d * f for c, d in zip(cols[j], down)]
+    whole = jnp.concatenate(tiles, axis=0)
+    return whole[:, BASE : 2 * BASE], whole[:, 64 + BASE : 64 + 2 * BASE]
+
+
+def half_inverse(work):
+    for j in range(HALF // BASE):
+        rows = slice(BASE * j, BASE * j + BASE)
+        inv = base_inverse(work[0, rows, rows], work[1, rows, rows])
+        lane = lax.broadcasted_iota(jnp.int32, (HALF, HALF), 1)
+        inside = (lane >= BASE * j) & (lane < BASE * (j + 1))
+        r = lax.broadcasted_iota(jnp.int32, (BASE, HALF), 0)
+        c = lax.broadcasted_iota(jnp.int32, (BASE, HALF), 1)
+        for m in range(2):
+            old = work[m]
+            top = jnp.where(inside[:BASE], (c == r + BASE * j).astype(jnp.float32), old[rows])
+            new = dot(inv[m], top)
+            work[m] = jnp.where(inside, 0.0, old) - dot(old[:, rows], new)
+            work[m, rows] = new
+
+
+def solve_kernel(pred, moved, out, work):
+    lo, hi = slice(0, HALF), slice(HALF, 2 * HALF)
+    for m in range(2):
+        work[m] = pred[m, lo, lo]
+    half_inverse(work)
+    wide, rest = [], []
+    for m in range(2):
+        rhs = jnp.concatenate([pred[m, lo, hi], moved[m, lo]], axis=1)
+        w = dot(work[m], rhs)
+        s = jnp.concatenate([pred[m, hi, hi], moved[m, hi]], axis=1) - dot(pred[m, hi, lo], w)
+        wide.append(w)
+        rest.append(s[:, HALF:])
+        work[m] = s[:, :HALF]
+    half_inverse(work)
+    for m in range(2):
+        h2 = dot(work[m], rest[m])
+        out[m, hi] = h2
+        out[m, lo] = wide[m][:, HALF:] - dot(wide[m][:, :HALF], h2)
+
+
+def solve(pred, moved):
+    return pl.pallas_call(
+        solve_kernel,
+        out_shape=jax.ShapeDtypeStruct(moved.shape, jnp.float32),
+        in_specs=[pl.BlockSpec(memory_space=pltpu.VMEM)] * 2,
+        out_specs=pl.BlockSpec(memory_space=pltpu.VMEM),
+        scratch_shapes=[pltpu.VMEM((2, HALF, HALF), jnp.float32)],
+        compiler_params=pltpu.CompilerParams(vmem_limit_bytes=32 * 1024 * 1024),
+    )(pred, moved)
 
 
 def product(left, right):
@@ -13,11 +98,6 @@
 
 def flipped(matrix):
     return jnp.swapaxes(matrix, -1, -2)
-
-
-def chol_solve(factor, rhs):
-    middle = lax.linalg.triangular_solve(factor, rhs, left_side=True, lower=True)
-    return lax.linalg.triangular_solve(factor, middle, left_side=True, lower=True, transpose_a=True)
 
 
 def grown(matrix, row):
@@ -39,8 +119,7 @@
     core = place % 2
     moved = product(transition, filt_cov)
     predicted = product(moved, transition.T) + noise_cov
-    factor = jnp.linalg.cholesky(predicted)
-    solved = chol_solve(factor, moved)
+    solved = solve(predicted, moved)
     final = (place == devices - 1) & (jnp.arange(2) == 1)
     solved = jnp.where(final[:, None, None], 0.0, solved)
     ahead = product(filt_mean, transition.T)

time: 242 us -> 140 us (0.58)
  other arithmetic: 109 us -> 2.06 us
  Pallas kernels: 0 us -> 13 us
  local copies, waits for them, and re-layouts: 5.95 us -> 1.28 us
    another operation x13 -> x0, other arithmetic: 107 us -> none  [the longest x9 66.8 us: local(): factor = jnp.linalg.cholesky(predicted)]
    pallas_call x0 -> x1, Pallas kernels: none -> 13 us  [solve(): pl.pallas_call(solve_kernel, out_shape=jax.ShapeDtypeStruct(moved.shape,...]
    another operation x9 -> x0, local copies, waits for them, and re-layouts: 4.19 us -> none
    another operation x8 -> x0, matrix products: 3.02 us -> none  [the longest x3 1.21 us: chol_solve(): lax.linalg.triangular_solve(factor, rhs, left_side=True, lower=True)]
  transfers between devices with their start and end apart: 17 -> 17, of which waited for: 13 -> 14; matrix products, arithmetic and copies ran while one was open for 2% -> 4% of each run, Pallas kernels for 0% -> 0%
where the time goes in v2:
time: 140 us; the launch traced here: 139 us
  starting transfers between devices  64 us (46%)
  waiting for transfers between devices  38.8 us (28%)
  matrix products  18.6 us (13%)
  Pallas kernels  13 us (9%)
  other arithmetic  2.06 us (1%)
    ppermute x7, starting transfers between devices, local(): got = lax.ppermute(mine, AXES, pairs)  32.9 us
    ppermute x6, waiting for transfers between devices, local(): lax.ppermute(first[:width], AXES, [(2 * c, 2 * c + 1) for c in range(chip...  18.9 us
    dot_general x35, matrix products, product(): return jnp.matmul(left, right, precision=lax.Precision.HIGHEST)  18.6 us
    ppermute x1, starting transfers between devices, local(): lax.ppermute(mine, AXES, [(2 * c + 3, 2 * c) for c in range(chips - 1)])  17.1 us
    ppermute x7, waiting for transfers between devices, local(): got = lax.ppermute(mine, AXES, pairs)  15.8 us
    pallas_call x1, Pallas kernels, solve(): pl.pallas_call(solve_kernel, out_shape=jax.ShapeDtypeStruct(moved.shape,...  13 us
    ppermute x6, starting transfers between devices, local(): lax.ppermute(first[:width], AXES, [(2 * c, 2 * c + 1) for c in range(chip...  7.97 us
    ppermute x1, starting transfers between devices, local(): lax.ppermute(mine, AXES, [(2 * c + 3, 2 * c + 1) for c in range(chips - 1)])  4.74 us
  transfers between devices with their start and end apart: 17, of which 14 were waited for; matrix products, arithmetic and copies ran while one was open for 4% of the time, Pallas kernels for 0%

profile of v2, /device:TPU:3, one launch (start us, length us, event | category | flops | bytes accessed | tf_op | source)
XLA Modules:
  0.0 139.1 jit_solution(4887772201025391214)
XLA Ops:
  0.6 0.9 copy-done
  1.6 1.7 %convolution_bitcast_fusion.moved = f32[2,256,256]{2,1,0:T(8,128)S(1)} fusion(f32[2,256,256]{2,1,0:T(8,128)} %param.5, f32[256,256]{1,0:T(8,128)S(1)} %copy-done), kind=kOutput, calls=%fused_computation.1 | convolution fusion | flops 402653184 | bytes 1310720 | tf_op jit(solution)/shard_map/dot_general | solution.py:96
  3.9 13.0 %shard_map.59 = f32[2,256,256]{2,1,0:T(8,128)S(1)} custom-call(f32[2,256,256]{2,1,0:T(8,128)S(1)} %convolution_add_fusion.pred, f32[2,256,256]{2,1,0:T(8,128)S(1)} %convolution_bitcast_fusion.moved), custom_call_target="tpu_custom_call" | custom-call | tf_op jit(solution)/shard_map/pallas_call | solution.py:85
  17.5 1.0 collective-permute-start
  18.5 1.0 convolution_subtract_fusion
  25.1 9.9 %collective-permute-start.2 = (f32[264,256]{1,0:T(8,128)S(1)}, f32[264,256]{1,0:T(8,128)S(1)}, u32[]{:S(2)}, u32[]{:S(2)}) collective-permute-start(f32[264,256]{1,0:T(8,128)S(1)} %maximum_select_fusion), channel_id=1, source_target_pairs={{3,1},{5,3},{7,5},{9,7},{11,9},{13,11},{15,13},{17,15},{19,17},{21... | collective-permute-start | bytes 811016 | tf_op jit(solution)/shard_map/ppermute | solution.py:154
  35.0 5.5 %collective-permute-done.2 = f32[264,256]{1,0:T(8,128)S(1)} collective-permute-done((f32[264,256]{1,0:T(8,128)S(1)}, f32[264,256]{1,0:T(8,128)S(1)}, u32[]{:S(2)}, u32[]{:S(2)}) %collective-permute-start.2) | collective-permute-done | bytes 270368 | tf_op jit(solution)/shard_map/ppermute | solution.py:154
  41.6 4.3 %collective-permute-start.3 = (f32[264,256]{1,0:T(8,128)S(1)}, f32[264,256]{1,0:T(8,128)S(1)}, u32[]{:S(2)}, u32[]{:S(2)}) collective-permute-start(f32[264,256]{1,0:T(8,128)S(1)} %maximum_select_fusion.1), channel_id=1, source_target_pairs={{5,1},{7,3},{9,5},{11,7},{13,9},{15,11},{17,13},{19,15},{21,17},{2... | collective-permute-start | bytes 811016 | tf_op jit(solution)/shard_map/ppermute | solution.py:154
  45.9 1.3 collective-permute-start.4
  47.2 2.5 %collective-permute-done.4 = f32[256,256]{1,0:T(8,128)S(1)} collective-permute-done((f32[256,256]{1,0:T(8,128)S(1)}, f32[256,256]{1,0:T(8,128)S(1)}, u32[]{:S(2)}, u32[]{:S(2)}) %collective-permute-start.4) | collective-permute-done | bytes 262176 | tf_op jit(solution)/shard_map/ppermute | solution.py:157
  49.7 2.1 %collective-permute-done.3 = f32[264,256]{1,0:T(8,128)S(1)} collective-permute-done((f32[264,256]{1,0:T(8,128)S(1)}, f32[264,256]{1,0:T(8,128)S(1)}, u32[]{:S(2)}, u32[]{:S(2)}) %collective-permute-start.3) | collective-permute-done | bytes 270368 | tf_op jit(solution)/shard_map/ppermute | solution.py:154
  52.8 2.6 %collective-permute-start.5 = (f32[264,256]{1,0:T(8,128)S(1)}, f32[264,256]{1,0:T(8,128)S(1)}, u32[]{:S(2)}, u32[]{:S(2)}) collective-permute-start(f32[264,256]{1,0:T(8,128)S(1)} %maximum_select_fusion.2), channel_id=1, source_target_pairs={{9,1},{11,3},{13,5},{15,7},{17,9},{19,11},{21,13},{23,15},{25,17},... | collective-permute-start | bytes 811016 | tf_op jit(solution)/shard_map/ppermute | solution.py:154
  55.5 1.3 collective-permute-start.6
  56.8 3.4 %collective-permute-done.6 = f32[256,256]{1,0:T(8,128)S(1)} collective-permute-done((f32[256,256]{1,0:T(8,128)S(1)}, f32[256,256]{1,0:T(8,128)S(1)}, u32[]{:S(2)}, u32[]{:S(2)}) %collective-permute-start.6) | collective-permute-done | bytes 262176 | tf_op jit(solution)/shard_map/ppermute | solution.py:157
  61.7 3.1 %collective-permute-start.7 = (f32[264,256]{1,0:T(8,128)S(1)}, f32[264,256]{1,0:T(8,128)S(1)}, u32[]{:S(2)}, u32[]{:S(2)}) collective-permute-start(f32[264,256]{1,0:T(8,128)S(1)} %maximum_select_fusion.3), channel_id=1, source_target_pairs={{17,1},{19,3},{21,5},{23,7},{25,9},{27,11},{29,13},{31,15},{33,17}... | collective-permute-start | bytes 811016 | tf_op jit(solution)/shard_map/ppermute | solution.py:154
  64.8 1.3 collective-permute-start.8
  66.1 4.3 %collective-permute-done.8 = f32[256,256]{1,0:T(8,128)S(1)} collective-permute-done((f32[256,256]{1,0:T(8,128)S(1)}, f32[256,256]{1,0:T(8,128)S(1)}, u32[]{:S(2)}, u32[]{:S(2)}) %collective-permute-start.8) | collective-permute-done | bytes 262176 | tf_op jit(solution)/shard_map/ppermute | solution.py:157
  71.5 9.8 %collective-permute-start.9 = (f32[264,256]{1,0:T(8,128)S(1)}, f32[264,256]{1,0:T(8,128)S(1)}, u32[]{:S(2)}, u32[]{:S(2)}) collective-permute-start(f32[264,256]{1,0:T(8,128)S(1)} %maximum_select_fusion.4), channel_id=1, source_target_pairs={{33,1},{35,3},{37,5},{39,7},{41,9},{43,11},{45,13},{47,15},{49,17}... | collective-permute-start | bytes 811016 | tf_op jit(solution)/shard_map/ppermute | solution.py:154
  81.3 1.3 collective-permute-start.10
  82.6 3.7 %collective-permute-done.10 = f32[256,256]{1,0:T(8,128)S(1)} collective-permute-done((f32[256,256]{1,0:T(8,128)S(1)}, f32[256,256]{1,0:T(8,128)S(1)}, u32[]{:S(2)}, u32[]{:S(2)}) %collective-permute-start.10) | collective-permute-done | bytes 262176 | tf_op jit(solution)/shard_map/ppermute | solution.py:157
  86.3 4.4 %collective-permute-done.9 = f32[264,256]{1,0:T(8,128)S(1)} collective-permute-done((f32[264,256]{1,0:T(8,128)S(1)}, f32[264,256]{1,0:T(8,128)S(1)}, u32[]{:S(2)}, u32[]{:S(2)}) %collective-permute-start.9) | collective-permute-done | bytes 270368 | tf_op jit(solution)/shard_map/ppermute | solution.py:154
  91.8 1.9 %collective-permute-start.11 = (f32[264,256]{1,0:T(8,128)S(1)}, f32[264,256]{1,0:T(8,128)S(1)}, u32[]{:S(2)}, u32[]{:S(2)}) collective-permute-start(f32[264,256]{1,0:T(8,128)S(1)} %maximum_select_fusion.5), channel_id=1, source_target_pairs={{65,1},{67,3},{69,5},{71,7},{73,9},{75,11},{77,13},{79,15},{81,17}... | collective-permute-start | bytes 811016 | tf_op jit(solution)/shard_map/ppermute | solution.py:154
  93.7 1.5 %collective-permute-start.12 = (f32[256,256]{1,0:T(8,128)S(1)}, f32[256,256]{1,0:T(8,128)S(1)}, u32[]{:S(2)}, u32[]{:S(2)}) collective-permute-start(f32[256,256]{1,0:T(8,128)S(1)} %slice.256), channel_id=1, source_target_pairs={{0,1},{2,3},{4,5},{6,7},{8,9},{10,11},{12,13},{14,15},{16,17},{18,... | collective-permute-start | bytes 786440 | tf_op jit(solution)/shard_map/ppermute | solution.py:157
  96.0 2.3 %collective-permute-done.12 = f32[256,256]{1,0:T(8,128)S(1)} collective-permute-done((f32[256,256]{1,0:T(8,128)S(1)}, f32[256,256]{1,0:T(8,128)S(1)}, u32[]{:S(2)}, u32[]{:S(2)}) %collective-permute-start.12) | collective-permute-done | bytes 262176 | tf_op jit(solution)/shard_map/ppermute | solution.py:157
  98.3 1.0 collective-permute-done.11
  100.4 1.3 collective-permute-start.13
  101.7 1.3 collective-permute-start.14
  104.0 2.6 %collective-permute-done.14 = f32[256,256]{1,0:T(8,128)S(1)} collective-permute-done((f32[256,256]{1,0:T(8,128)S(1)}, f32[256,256]{1,0:T(8,128)S(1)}, u32[]{:S(2)}, u32[]{:S(2)}) %collective-permute-start.14) | collective-permute-done | bytes 262176 | tf_op jit(solution)/shard_map/ppermute | solution.py:157
  106.7 2.5 %collective-permute-done.13 = f32[264,256]{1,0:T(8,128)S(1)} collective-permute-done((f32[264,256]{1,0:T(8,128)S(1)}, f32[264,256]{1,0:T(8,128)S(1)}, u32[]{:S(2)}, u32[]{:S(2)}) %collective-permute-start.13) | collective-permute-done | bytes 270368 | tf_op jit(solution)/shard_map/ppermute | solution.py:154
  110.2 17.1 %collective-permute-start.15 = (f32[264,256]{1,0:T(8,128)S(1)}, f32[264,256]{1,0:T(8,128)S(1)}, u32[]{:S(2)}, u32[]{:S(2)}) collective-permute-start(f32[264,256]{1,0:T(8,128)S(1)} %maximum_select_fusion.7), channel_id=1, source_target_pairs={{3,0},{5,2},{7,4},{9,6},{11,8},{13,10},{15,12},{17,14},{19,16},{21... | collective-permute-start | bytes 811016 | tf_op jit(solution)/shard_map/ppermute | solution.py:165
  127.3 4.7 %collective-permute-start.16 = (f32[264,256]{1,0:T(8,128)S(1)}, f32[264,256]{1,0:T(8,128)S(1)}, u32[]{:S(2)}, u32[]{:S(2)}) collective-permute-start(f32[264,256]{1,0:T(8,128)S(1)} %maximum_select_fusion.7), channel_id=1, source_target_pairs={{3,1},{5,3},{7,5},{9,7},{11,9},{13,11},{15,13},{17,15},{19,17},{21... | collective-permute-start | bytes 811016 | tf_op jit(solution)/shard_map/ppermute | solution.py:164
  132.2 3.3 %collective-permute-done.16 = f32[264,256]{1,0:T(8,128)S(1)} collective-permute-done((f32[264,256]{1,0:T(8,128)S(1)}, f32[264,256]{1,0:T(8,128)S(1)}, u32[]{:S(2)}, u32[]{:S(2)}) %collective-permute-start.16) | collective-permute-done | bytes 270368 | tf_op jit(solution)/shard_map/ppermute | solution.py:164
  (93 shorter events, 19.9 us)
Async XLA Ops:
  0.6 1.0 copy-start
  1.6 1.7 %copy-start.4 = (f32[2,256,256]{2,1,0:T(8,128)S(1)}, f32[2,256,256]{2,1,0:T(8,128)}, u32[]{:S(2)}) copy-start(f32[2,256,256]{2,1,0:T(8,128)} %param.6) | copy-start | bytes 1572868
  17.1 1.4 copy-start.1
  17.5 2.0 %copy-start.5 = (f32[2,256]{1,0:T(2,128)S(1)}, f32[2,256]{1,0:T(2,128)}, u32[]{:S(2)}) copy-start(f32[2,256]{1,0:T(2,128)} %param.4) | copy-start | bytes 6148
  17.5 4.3 %collective-permute-start = (f32[256,256]{1,0:T(8,128)S(1)}, f32[256,256]{1,0:T(8,128)S(1)}, u32[]{:S(2)}, u32[]{:S(2)}) collective-permute-start(f32[256,256]{1,0:T(8,128)S(1)} %fusion.16), channel_id=1, source_target_pairs={{0,1},{1,0},{2,3},{3,2},{4,5},{5,4},{6,7},{7,6},{8,9},{9,8},{10,11... | collective-permute-start | bytes 786440 | tf_op jit(solution)/shard_map/ppermute | solution.py:133
  21.3 1.6 %collective-permute-start.1 = (f32[264,256]{1,0:T(8,128)S(1)}, f32[264,256]{1,0:T(8,128)S(1)}, u32[]{:S(2)}, u32[]{:S(2)}) collective-permute-start(f32[264,256]{1,0:T(8,128)S(1)} %pad_maximum_fusion.2), channel_id=1, source_target_pairs={{0,1},{1,0},{2,3},{3,2},{4,5},{5,4},{6,7},{7,6},{8,9},{9,8},{10,11... | collective-permute-start | bytes 811016 | tf_op jit(solution)/shard_map/ppermute | solution.py:134
  25.1 15.4 %collective-permute-start.2 = (f32[264,256]{1,0:T(8,128)S(1)}, f32[264,256]{1,0:T(8,128)S(1)}, u32[]{:S(2)}, u32[]{:S(2)}) collective-permute-start(f32[264,256]{1,0:T(8,128)S(1)} %maximum_select_fusion), channel_id=1, source_target_pairs={{3,1},{5,3},{7,5},{9,7},{11,9},{13,11},{15,13},{17,15},{19,17},{21... | collective-permute-start | bytes 811016 | tf_op jit(solution)/shard_map/ppermute | solution.py:154
  41.6 10.2 %collective-permute-start.3 = (f32[264,256]{1,0:T(8,128)S(1)}, f32[264,256]{1,0:T(8,128)S(1)}, u32[]{:S(2)}, u32[]{:S(2)}) collective-permute-start(f32[264,256]{1,0:T(8,128)S(1)} %maximum_select_fusion.1), channel_id=1, source_target_pairs={{5,1},{7,3},{9,5},{11,7},{13,9},{15,11},{17,13},{19,15},{21,17},{2... | collective-permute-start | bytes 811016 | tf_op jit(solution)/shard_map/ppermute | solution.py:154
  45.9 3.8 %collective-permute-start.4 = (f32[256,256]{1,0:T(8,128)S(1)}, f32[256,256]{1,0:T(8,128)S(1)}, u32[]{:S(2)}, u32[]{:S(2)}) collective-permute-start(f32[256,256]{1,0:T(8,128)S(1)} %slice.240), channel_id=1, source_target_pairs={{0,1},{2,3},{4,5},{6,7},{8,9},{10,11},{12,13},{14,15},{16,17},{18,... | collective-permute-start | bytes 786440 | tf_op jit(solution)/shard_map/ppermute | solution.py:157
  52.8 7.8 %collective-permute-start.5 = (f32[264,256]{1,0:T(8,128)S(1)}, f32[264,256]{1,0:T(8,128)S(1)}, u32[]{:S(2)}, u32[]{:S(2)}) collective-permute-start(f32[264,256]{1,0:T(8,128)S(1)} %maximum_select_fusion.2), channel_id=1, source_target_pairs={{9,1},{11,3},{13,5},{15,7},{17,9},{19,11},{21,13},{23,15},{25,17},... | collective-permute-start | bytes 811016 | tf_op jit(solution)/shard_map/ppermute | solution.py:154
  55.5 4.7 %collective-permute-start.6 = (f32[256,256]{1,0:T(8,128)S(1)}, f32[256,256]{1,0:T(8,128)S(1)}, u32[]{:S(2)}, u32[]{:S(2)}) collective-permute-start(f32[256,256]{1,0:T(8,128)S(1)} %slice.244), channel_id=1, source_target_pairs={{0,1},{2,3},{4,5},{6,7},{8,9},{10,11},{12,13},{14,15},{16,17},{18,... | collective-permute-start | bytes 786440 | tf_op jit(solution)/shard_map/ppermute | solution.py:157
  61.7 8.7 %collective-permute-start.7 = (f32[264,256]{1,0:T(8,128)S(1)}, f32[264,256]{1,0:T(8,128)S(1)}, u32[]{:S(2)}, u32[]{:S(2)}) collective-permute-start(f32[264,256]{1,0:T(8,128)S(1)} %maximum_select_fusion.3), channel_id=1, source_target_pairs={{17,1},{19,3},{21,5},{23,7},{25,9},{27,11},{29,13},{31,15},{33,17}... | collective-permute-start | bytes 811016 | tf_op jit(solution)/shard_map/ppermute | solution.py:154
  64.8 5.6 %collective-permute-start.8 = (f32[256,256]{1,0:T(8,128)S(1)}, f32[256,256]{1,0:T(8,128)S(1)}, u32[]{:S(2)}, u32[]{:S(2)}) collective-permute-start(f32[256,256]{1,0:T(8,128)S(1)} %slice.248), channel_id=1, source_target_pairs={{0,1},{2,3},{4,5},{6,7},{8,9},{10,11},{12,13},{14,15},{16,17},{18,... | collective-permute-start | bytes 786440 | tf_op jit(solution)/shard_map/ppermute | solution.py:157
  71.5 19.2 %collective-permute-start.9 = (f32[264,256]{1,0:T(8,128)S(1)}, f32[264,256]{1,0:T(8,128)S(1)}, u32[]{:S(2)}, u32[]{:S(2)}) collective-permute-start(f32[264,256]{1,0:T(8,128)S(1)} %maximum_select_fusion.4), channel_id=1, source_target_pairs={{33,1},{35,3},{37,5},{39,7},{41,9},{43,11},{45,13},{47,15},{49,17}... | collective-permute-start | bytes 811016 | tf_op jit(solution)/shard_map/ppermute | solution.py:154
  81.3 5.0 %collective-permute-start.10 = (f32[256,256]{1,0:T(8,128)S(1)}, f32[256,256]{1,0:T(8,128)S(1)}, u32[]{:S(2)}, u32[]{:S(2)}) collective-permute-start(f32[256,256]{1,0:T(8,128)S(1)} %slice.252), channel_id=1, source_target_pairs={{0,1},{2,3},{4,5},{6,7},{8,9},{10,11},{12,13},{14,15},{16,17},{18,... | collective-permute-start | bytes 786440 | tf_op jit(solution)/shard_map/ppermute | solution.py:157
  91.8 7.5 %collective-permute-start.11 = (f32[264,256]{1,0:T(8,128)S(1)}, f32[264,256]{1,0:T(8,128)S(1)}, u32[]{:S(2)}, u32[]{:S(2)}) collective-permute-start(f32[264,256]{1,0:T(8,128)S(1)} %maximum_select_fusion.5), channel_id=1, source_target_pairs={{65,1},{67,3},{69,5},{71,7},{73,9},{75,11},{77,13},{79,15},{81,17}... | collective-permute-start | bytes 811016 | tf_op jit(solution)/shard_map/ppermute | solution.py:154
  93.7 4.6 %collective-permute-start.12 = (f32[256,256]{1,0:T(8,128)S(1)}, f32[256,256]{1,0:T(8,128)S(1)}, u32[]{:S(2)}, u32[]{:S(2)}) collective-permute-start(f32[256,256]{1,0:T(8,128)S(1)} %slice.256), channel_id=1, source_target_pairs={{0,1},{2,3},{4,5},{6,7},{8,9},{10,11},{12,13},{14,15},{16,17},{18,... | collective-permute-start | bytes 786440 | tf_op jit(solution)/shard_map/ppermute | solution.py:157
  100.4 8.7 %collective-permute-start.13 = (f32[264,256]{1,0:T(8,128)S(1)}, f32[264,256]{1,0:T(8,128)S(1)}, u32[]{:S(2)}, u32[]{:S(2)}) collective-permute-start(f32[264,256]{1,0:T(8,128)S(1)} %maximum_select_fusion.6), channel_id=1, source_target_pairs={{129,1},{131,3},{133,5},{135,7},{137,9},{139,11},{141,13},{143,15}... | collective-permute-start | bytes 811016 | tf_op jit(solution)/shard_map/ppermute | solution.py:154
  101.7 4.9 %collective-permute-start.14 = (f32[256,256]{1,0:T(8,128)S(1)}, f32[256,256]{1,0:T(8,128)S(1)}, u32[]{:S(2)}, u32[]{:S(2)}) collective-permute-start(f32[256,256]{1,0:T(8,128)S(1)} %slice.260), channel_id=1, source_target_pairs={{0,1},{2,3},{4,5},{6,7},{8,9},{10,11},{12,13},{14,15},{16,17},{18,... | collective-permute-start | bytes 786440 | tf_op jit(solution)/shard_map/ppermute | solution.py:157
  110.2 21.9 %collective-permute-start.15 = (f32[264,256]{1,0:T(8,128)S(1)}, f32[264,256]{1,0:T(8,128)S(1)}, u32[]{:S(2)}, u32[]{:S(2)}) collective-permute-start(f32[264,256]{1,0:T(8,128)S(1)} %maximum_select_fusion.7), channel_id=1, source_target_pairs={{3,0},{5,2},{7,4},{9,6},{11,8},{13,10},{15,12},{17,14},{19,16},{21... | collective-permute-start | bytes 811016 | tf_op jit(solution)/shard_map/ppermute | solution.py:165
  127.3 8.1 %collective-permute-start.16 = (f32[264,256]{1,0:T(8,128)S(1)}, f32[264,256]{1,0:T(8,128)S(1)}, u32[]{:S(2)}, u32[]{:S(2)}) collective-permute-start(f32[264,256]{1,0:T(8,128)S(1)} %maximum_select_fusion.7), channel_id=1, source_target_pairs={{3,1},{5,3},{7,5},{9,7},{11,9},{13,11},{15,13},{17,15},{19,17},{21... | collective-permute-start | bytes 811016 | tf_op jit(solution)/shard_map/ppermute | solution.py:164
  132.1 3.7 %copy-start.2 = (f32[264,256]{1,0:T(8,128)}, f32[264,256]{1,0:T(8,128)S(1)}, u32[]{:S(2)}) copy-start(f32[264,256]{1,0:T(8,128)S(1)} %maximum_select_fusion.9) | copy-start | bytes 811012
  135.8 0.7 copy-start.3
  137.0 0.7 slice-start
  137.0 0.7 slice-start.1

commit v3 on v2

--- a/solution.py
+++ b/solution.py
@@ -92,12 +92,147 @@
     )(pred, moved)
 
 
+NS = 256
+TOP = 192
+LOW = NS - TOP
+OFFSET = LOW + HALF
+DIAG = OFFSET + 1
+PART = OFFSET + EXTRA
+
+
+def flipped(matrix):
+    return jnp.swapaxes(matrix, -1, -2)
+
+
+def tdot(left, right):
+    return lax.dot_general(
+        left, right, (((0,), (0,)), ((), ())),
+        precision=lax.Precision.HIGHEST, preferred_element_type=jnp.float32,
+    )
+
+
+def row_col():
+    return (
+        lax.broadcasted_iota(jnp.int32, (HALF, HALF), 0),
+        lax.broadcasted_iota(jnp.int32, (HALF, HALF), 1),
+    )
+
+
+def packed(upper, corner):
+    r, c = row_col()
+    both = jnp.where(r >= c, upper[:, :HALF], corner)
+    diag = jnp.sum(jnp.where(r == c, corner, 0.0), axis=0, keepdims=True)
+    return jnp.concatenate([upper[:, HALF:], both], axis=1), diag
+
+
+def unpacked(half, diag):
+    r, c = row_col()
+    right, both = half[:, :HALF], half[:, HALF:]
+    turned = both.T
+    left = jnp.where(r >= c, both, turned)
+    corner = jnp.where(r < c, both, jnp.where(r == c, diag, turned))
+    return jnp.concatenate(
+        [jnp.concatenate([left, right], axis=1), jnp.concatenate([right.T, corner], axis=1)], axis=0
+    )
+
+
+def sandwich(inner, gain):
+    first = dot(inner, gain)
+    upper = tdot(gain[:, :HALF], first)
+    corner = tdot(gain[:, HALF:], first[:, HALF:])
+    return packed(upper, corner)
+
+
+def diag_row(diag):
+    return jnp.concatenate([diag, jnp.zeros((1, NS - HALF), jnp.float32)], axis=1)
+
+
+def store_held(out, base, half, diag, offset):
+    out[base : base + HALF] = half
+    tail = jnp.concatenate(
+        [offset, diag_row(diag), jnp.zeros((EXTRA - 2, NS), jnp.float32)], axis=0
+    )
+    out[base + HALF : base + HALF + EXTRA] = tail
+
+
+def chip_kernel(core, turned, held, other_turned, other_held, out):
+    @pl.when(core[0] == 0)
+    def _():
+        out[:TOP] = dot(other_turned[:TOP], turned[...])
+        out[TOP:] = jnp.zeros((PART - TOP, NS), jnp.float32)
+
+    @pl.when(core[0] == 1)
+    def _():
+        gain = other_turned[...]
+        out[:LOW] = dot(turned[TOP:], gain)
+        half, diag = sandwich(held[:NS], gain)
+        own, own_diag = packed(other_held[:HALF], other_held[HALF:NS, HALF:])
+        tail = dot(held[NS:], gain) + other_held[NS:]
+        store_held(out, LOW, half + own, diag + own_diag, tail[:1])
+
+
+def join_kernel(core, got, mine, passed, out):
+    @pl.when(core[0] == 0)
+    def _():
+        gain = jnp.concatenate([mine[:TOP], passed[:LOW]], axis=0)
+        out[:TOP] = dot(got[:TOP], gain)
+        out[TOP:] = jnp.zeros((PART - TOP, NS), jnp.float32)
+
+    @pl.when(core[0] == 1)
+    def _():
+        gain = jnp.concatenate([passed[:TOP], mine[:LOW]], axis=0)
+        out[:LOW] = dot(got[:LOW], gain)
+        inner = unpacked(got[LOW:OFFSET], got[DIAG : DIAG + 1, :HALF])
+        half, diag = sandwich(inner, gain)
+        tail = dot(got[OFFSET:], gain)
+        store_held(
+            out, LOW, half + mine[LOW:OFFSET], diag + mine[DIAG : DIAG + 1, :HALF],
+            tail[:1] + mine[OFFSET : OFFSET + 1],
+        )
+
+
+def last_kernel(core, got, mine, passed, out):
+    @pl.when(core[0] == 0)
+    def _():
+        out[...] = jnp.zeros(out.shape, jnp.float32)
+
+    @pl.when(core[0] == 1)
+    def _():
+        gain = jnp.concatenate([passed[:TOP], mine[:LOW]], axis=0)
+        inner = unpacked(got[:HALF], got[HALF + 1 : HALF + 2, :HALF])
+        half, diag = sandwich(inner, gain)
+        tail = dot(got[HALF:], gain)
+        store_held(
+            out, 0, half + mine[LOW:OFFSET], diag + mine[DIAG : DIAG + 1, :HALF],
+            tail[:1] + mine[OFFSET : OFFSET + 1],
+        )
+
+
+def end_kernel(after, turned0, held0, turned1, held1, cov, mean):
+    inner = unpacked(after[:HALF], after[HALF + 1 : HALF + 2, :HALF])
+    for i, (turned, held) in enumerate(((turned0, held0), (turned1, held1))):
+        gain = turned[...]
+        cov[i] = tdot(gain, dot(inner, gain)) + held[:NS]
+        mean[i : i + 1] = (dot(after[HALF:], gain) + held[NS:])[:1]
+
+
+def call(kernel, shapes, scalar, *arrays):
+    vmem = pl.BlockSpec(memory_space=pltpu.VMEM)
+    smem = pl.BlockSpec(memory_space=pltpu.SMEM)
+    scalars = [] if scalar is None else [scalar]
+    outs = [jax.ShapeDtypeStruct(s, jnp.float32) for s in shapes]
+    done = pl.pallas_call(
+        kernel,
+        out_shape=outs,
+        in_specs=[smem] * len(scalars) + [vmem] * len(arrays),
+        out_specs=[vmem] * len(outs),
+        compiler_params=pltpu.CompilerParams(vmem_limit_bytes=32 * 1024 * 1024),
+    )(*scalars, *arrays)
+    return done if len(outs) > 1 else done[0]
+
+
 def product(left, right):
     return jnp.matmul(left, right, precision=lax.Precision.HIGHEST)
-
-
-def flipped(matrix):
-    return jnp.swapaxes(matrix, -1, -2)
 
 
 def grown(matrix, row):
@@ -112,11 +247,12 @@
 
 
 def local(filt_mean, filt_cov, noise_cov, transition):
-    width = filt_mean.shape[1]
     devices = lax.axis_size(AXES)
     chips = devices // 2
     place = lax.axis_index(AXES)
     core = place % 2
+    is_first = core == 0
+    which = core.astype(jnp.int32)[None]
     moved = product(transition, filt_cov)
     predicted = product(moved, transition.T) + noise_cov
     solved = solve(predicted, moved)
@@ -129,44 +265,44 @@
     held = [grown(remainder[0], offset[0]), grown(remainder[1], offset[1])]
     both_turned = product(turned[1], turned[0])
     both_held = applied(turned[0], held[1], held[0])
+
     swap = [(p, p ^ 1) for p in range(devices)]
-    other_turned = lax.ppermute(both_turned, AXES, swap)
-    other_held = lax.ppermute(both_held, AXES, swap)
-    is_first = core == 0
-    a_turned = jnp.where(is_first, both_turned, other_turned)
-    b_turned = jnp.where(is_first, other_turned, both_turned)
-    a_held = jnp.where(is_first, both_held, other_held)
-    b_held = jnp.where(is_first, other_held, both_held)
-    chip_turned = product(b_turned, a_turned)
-    chip_held = applied(a_turned, b_held, a_held)
+
+    def swapped(rows):
+        return lax.ppermute(rows, AXES, swap)
+
+    other_turned = swapped(both_turned)
+    other_held = swapped(both_held)
+    chip = call(chip_kernel, [(PART, NS)], which, both_turned, both_held, other_turned, other_held)
     late = [jnp.where(is_first, product(other_turned, t), t) for t in (both_turned, turned[1])]
     late_held = [
         jnp.where(is_first, applied(t, other_held, h), h)
         for t, h in ((both_turned, both_held), (turned[1], held[1]))
     ]
-    blank = jnp.zeros((EXTRA, width), jnp.float32)
-    mine = jnp.where(is_first, jnp.concatenate([chip_turned, blank], axis=0), chip_held)
-    gain = chip_turned
-    stride = 1
-    while stride < chips:
-        pairs = [(2 * (c + stride) + 1, 2 * c + 1) for c in range(chips - stride)]
-        pairs += [(2 * (c + stride), 2 * c) for c in range(chips - 2 * stride)]
-        got = lax.ppermute(mine, AXES, pairs)
-        first = product(got, gain)
-        if stride * 2 < chips:
-            passed = lax.ppermute(first[:width], AXES, [(2 * c, 2 * c + 1) for c in range(chips)])
-            later = jnp.where(is_first, first[:width], passed)
-        square = product(flipped(gain), first[:width]) + mine[:width]
-        row = first[width:] + mine[width:]
-        mine = jnp.where(is_first, first, jnp.concatenate([square, row], axis=0))
-        gain = later
+
+    def fetched(rows, stride, cores):
+        return lax.ppermute(
+            rows, AXES, [(2 * (c + stride) + k, 2 * c + k) for c in range(chips - stride) for k in cores]
+        )
+
+    mine = fetched(chip, 1, (0, 1))
+    got = fetched(chip, 2, (0, 1))
+    stride = 2
+    passed = swapped(mine[:TOP])
+    mine = call(join_kernel, [(PART, NS)], which, got, mine, passed)
+    while 2 * stride < chips:
+        got = fetched(mine, stride, (0, 1))
+        passed = swapped(mine[:TOP])
+        mine = call(join_kernel, [(PART, NS)], which, got, mine, passed)
         stride *= 2
-    to_second = lax.ppermute(mine, AXES, [(2 * c + 3, 2 * c + 1) for c in range(chips - 1)])
-    to_first = lax.ppermute(mine, AXES, [(2 * c + 3, 2 * c) for c in range(chips - 1)])
-    after = jnp.where(is_first, to_first, to_second)
-    outs = [applied(t, after, h) for t, h in zip(late, late_held)]
-    smooth_cov = jnp.stack([o[:width] for o in outs])
-    smooth_mean = jnp.stack([o[width] for o in outs])
+    got = fetched(mine[LOW:], stride, (1,))
+    passed = swapped(mine[:TOP])
+    after = call(last_kernel, [(HALF + EXTRA, NS)], which, got, mine, passed)
+    to_first = lax.ppermute(after, AXES, [(2 * c + 1, 2 * c) for c in range(chips)])
+    after = jnp.where(is_first, to_first, after)
+    smooth_cov, smooth_mean = call(
+        end_kernel, [(2, NS, NS), (2, NS)], None, after, late[0], late_held[0], late[1], late_held[1]
+    )
     return (smooth_mean, smooth_cov)
 
 

time: 140 us -> 130 us (0.929)
  the two profiles are of different devices: /device:TPU:3 before, /device:TPU:240 now
where the time goes in v3:
time: 130 us
  waiting for transfers between devices  72.6 us (56%)
  starting transfers between devices  26.7 us (21%)
  Pallas kernels  18.3 us (14%)
  matrix products  8.19 us (6%)
  local copies, waits for them, and re-layouts  2.65 us (2%)
    ppermute x8, waiting for transfers between devices, fetched(): lax.ppermute(rows, AXES, [(2 * (c + stride) + k, 2 * c + k) for c in rang...  57.4 us
    ppermute x8, starting transfers between devices, fetched(): lax.ppermute(rows, AXES, [(2 * (c + stride) + k, 2 * c + k) for c in rang...  17.2 us
    pallas_call x1, Pallas kernels, solve(): pl.pallas_call(solve_kernel, out_shape=jax.ShapeDtypeStruct(moved.shape,...  13 us
    ppermute x1, waiting for transfers between devices, local(): lax.ppermute(after, AXES, [(2 * c + 1, 2 * c) for c in range(chips)])  10.6 us
    dot_general x14, matrix products, product(): return jnp.matmul(left, right, precision=lax.Precision.HIGHEST)  8.19 us
    ppermute x9, starting transfers between devices, swapped(): return lax.ppermute(rows, AXES, swap)  8.12 us
    pallas_call x9, Pallas kernels, call(): pl.pallas_call(kernel, out_shape=outs, in_specs=[smem] * len(scalars) + [...  5.24 us
    ppermute x9, waiting for transfers between devices, swapped(): return lax.ppermute(rows, AXES, swap)  4.52 us
  transfers between devices with their start and end apart: 18, of which 15 were waited for; matrix products, arithmetic and copies ran while one was open for 2% of the time, Pallas kernels for 0%

profile of v3, /device:TPU:240, one launch (start us, length us, event | category | flops | bytes accessed | tf_op | source)
XLA Modules:
  0.0 129.7 jit_solution(2148255282245196923)
XLA Ops:
  0.7 0.9 copy-done
  1.6 1.7 %convolution_bitcast_fusion.moved = f32[2,256,256]{2,1,0:T(8,128)S(1)} fusion(f32[2,256,256]{2,1,0:T(8,128)} %param.5, f32[256,256]{1,0:T(8,128)S(1)} %copy-done), kind=kOutput, calls=%fused_computation.1 | convolution fusion | flops 402653184 | bytes 1310720 | tf_op jit(solution)/shard_map/dot_general | solution.py:235
  3.9 13.0 %shard_map.59 = f32[2,256,256]{2,1,0:T(8,128)S(1)} custom-call(f32[2,256,256]{2,1,0:T(8,128)S(1)} %convolution_add_fusion.pred, f32[2,256,256]{2,1,0:T(8,128)S(1)} %convolution_bitcast_fusion.moved), custom_call_target="tpu_custom_call" | custom-call | tf_op jit(solution)/shard_map/pallas_call | solution.py:85
  17.1 0.9 copy-done.1
  18.0 1.1 convolution_subtract_fusion
  22.8 1.2 collective-permute-done.other_turned
  24.3 2.4 %collective-permute-start.3 = (f32[200,256]{1,0:T(8,128)S(1)}, f32[200,256]{1,0:T(8,128)S(1)}, u32[]{:S(2)}, u32[]{:S(2)}) collective-permute-start(f32[200,256]{1,0:T(8,128)S(1)} %shard_map.60), channel_id=1, source_target_pairs={{2,0},{3,1},{4,2},{5,3},{6,4},{7,5},{8,6},{9,7},{10,8},{11,9},{12,... | collective-permute-start | bytes 614408 | tf_op jit(solution)/shard_map/ppermute | solution.py:284
  26.7 5.2 %collective-permute-start.2 = (f32[200,256]{1,0:T(8,128)S(1)}, f32[200,256]{1,0:T(8,128)S(1)}, u32[]{:S(2)}, u32[]{:S(2)}) collective-permute-start(f32[200,256]{1,0:T(8,128)S(1)} %shard_map.60), channel_id=1, source_target_pairs={{4,0},{5,1},{6,2},{7,3},{8,4},{9,5},{10,6},{11,7},{12,8},{13,9},{1... | collective-permute-start | bytes 614408 | tf_op jit(solution)/shard_map/ppermute | solution.py:284
  31.9 1.9 %collective-permute-done.3.mine = f32[200,256]{1,0:T(8,128)S(1)} collective-permute-done((f32[200,256]{1,0:T(8,128)S(1)}, f32[200,256]{1,0:T(8,128)S(1)}, u32[]{:S(2)}, u32[]{:S(2)}) %collective-permute-start.3) | collective-permute-done | bytes 204832 | tf_op jit(solution)/shard_map/ppermute | solution.py:284
  34.8 8.0 %collective-permute-done.2.got = f32[200,256]{1,0:T(8,128)S(1)} collective-permute-done((f32[200,256]{1,0:T(8,128)S(1)}, f32[200,256]{1,0:T(8,128)S(1)}, u32[]{:S(2)}, u32[]{:S(2)}) %collective-permute-start.2) | collective-permute-done | bytes 204832 | tf_op jit(solution)/shard_map/ppermute | solution.py:284
  43.1 1.9 %collective-permute-start.5 = (f32[200,256]{1,0:T(8,128)S(1)}, f32[200,256]{1,0:T(8,128)S(1)}, u32[]{:S(2)}, u32[]{:S(2)}) collective-permute-start(f32[200,256]{1,0:T(8,128)S(1)} %shard_map.61.mine), channel_id=1, source_target_pairs={{4,0},{5,1},{6,2},{7,3},{8,4},{9,5},{10,6},{11,7},{12,8},{13,9},{1... | collective-permute-start | bytes 614408 | tf_op jit(solution)/shard_map/ppermute | solution.py:284
  45.0 1.1 collective-permute-start.6
  46.5 0.7 collective-permute-done.6.passed
  47.2 10.2 %collective-permute-done.5.got = f32[200,256]{1,0:T(8,128)S(1)} collective-permute-done((f32[200,256]{1,0:T(8,128)S(1)}, f32[200,256]{1,0:T(8,128)S(1)}, u32[]{:S(2)}, u32[]{:S(2)}) %collective-permute-start.5) | collective-permute-done | bytes 204832 | tf_op jit(solution)/shard_map/ppermute | solution.py:284
  57.8 1.9 %collective-permute-start.7 = (f32[200,256]{1,0:T(8,128)S(1)}, f32[200,256]{1,0:T(8,128)S(1)}, u32[]{:S(2)}, u32[]{:S(2)}) collective-permute-start(f32[200,256]{1,0:T(8,128)S(1)} %shard_map.62.mine), channel_id=1, source_target_pairs={{8,0},{9,1},{10,2},{11,3},{12,4},{13,5},{14,6},{15,7},{16,8},{17,9... | collective-permute-start | bytes 614408 | tf_op jit(solution)/shard_map/ppermute | solution.py:284
  59.7 1.1 collective-permute-start.8
  61.2 0.7 collective-permute-done.8.passed
  61.9 7.8 %collective-permute-done.7.got = f32[200,256]{1,0:T(8,128)S(1)} collective-permute-done((f32[200,256]{1,0:T(8,128)S(1)}, f32[200,256]{1,0:T(8,128)S(1)}, u32[]{:S(2)}, u32[]{:S(2)}) %collective-permute-start.7) | collective-permute-done | bytes 204832 | tf_op jit(solution)/shard_map/ppermute | solution.py:284
  70.1 1.9 %collective-permute-start.9 = (f32[200,256]{1,0:T(8,128)S(1)}, f32[200,256]{1,0:T(8,128)S(1)}, u32[]{:S(2)}, u32[]{:S(2)}) collective-permute-start(f32[200,256]{1,0:T(8,128)S(1)} %shard_map.63.mine), channel_id=1, source_target_pairs={{16,0},{17,1},{18,2},{19,3},{20,4},{21,5},{22,6},{23,7},{24,8},{25... | collective-permute-start | bytes 614408 | tf_op jit(solution)/shard_map/ppermute | solution.py:284
  72.0 1.1 collective-permute-start.10
  74.2 10.3 %collective-permute-done.9.got = f32[200,256]{1,0:T(8,128)S(1)} collective-permute-done((f32[200,256]{1,0:T(8,128)S(1)}, f32[200,256]{1,0:T(8,128)S(1)}, u32[]{:S(2)}, u32[]{:S(2)}) %collective-permute-start.9) | collective-permute-done | bytes 204832 | tf_op jit(solution)/shard_map/ppermute | solution.py:284
  84.8 1.9 %collective-permute-start.11 = (f32[200,256]{1,0:T(8,128)S(1)}, f32[200,256]{1,0:T(8,128)S(1)}, u32[]{:S(2)}, u32[]{:S(2)}) collective-permute-start(f32[200,256]{1,0:T(8,128)S(1)} %shard_map.64.mine), channel_id=1, source_target_pairs={{32,0},{33,1},{34,2},{35,3},{36,4},{37,5},{38,6},{39,7},{40,8},{41... | collective-permute-start | bytes 614408 | tf_op jit(solution)/shard_map/ppermute | solution.py:284
  86.8 1.3 %collective-permute-start.12 = (f32[192,256]{1,0:T(8,128)S(1)}, f32[192,256]{1,0:T(8,128)S(1)}, u32[]{:S(2)}, u32[]{:S(2)}) collective-permute-start(f32[192,256]{1,0:T(8,128)S(1)} %slice.92), channel_id=1, source_target_pairs={{0,1},{1,0},{2,3},{3,2},{4,5},{5,4},{6,7},{7,6},{8,9},{9,8},{10,11... | collective-permute-start | bytes 589832 | tf_op jit(solution)/shard_map/ppermute | solution.py:272
  88.5 0.7 collective-permute-done.12.passed
  89.2 12.8 %collective-permute-done.11.got = f32[200,256]{1,0:T(8,128)S(1)} collective-permute-done((f32[200,256]{1,0:T(8,128)S(1)}, f32[200,256]{1,0:T(8,128)S(1)}, u32[]{:S(2)}, u32[]{:S(2)}) %collective-permute-start.11) | collective-permute-done | bytes 204832 | tf_op jit(solution)/shard_map/ppermute | solution.py:284
  102.4 1.3 collective-permute-start.13
  103.7 1.1 collective-permute-start.14
  105.8 6.3 %collective-permute-done.13.got = f32[200,256]{1,0:T(8,128)S(1)} collective-permute-done((f32[200,256]{1,0:T(8,128)S(1)}, f32[200,256]{1,0:T(8,128)S(1)}, u32[]{:S(2)}, u32[]{:S(2)}) %collective-permute-start.13) | collective-permute-done | bytes 204832 | tf_op jit(solution)/shard_map/ppermute | solution.py:284
  112.6 1.1 collective-permute-start.16
  114.7 1.3 collective-permute-start.17
  116.1 10.6 %collective-permute-done.17 = f32[136,256]{1,0:T(8,128)S(1)} collective-permute-done((f32[136,256]{1,0:T(8,128)S(1)}, f32[136,256]{1,0:T(8,128)S(1)}, u32[]{:S(2)}, u32[]{:S(2)}) %collective-permute-start.17) | collective-permute-done | bytes 139296 | tf_op jit(solution)/shard_map/ppermute | solution.py:301
  126.8 2.9 %shard_map.68 = (f32[2,256,256]{2,1,0:T(8,128)}, f32[2,256]{1,0:T(2,128)}) custom-call(f32[136,256]{1,0:T(8,128)S(1)} %broadcast_select_fusion.1.after, f32[256,256]{1,0:T(8,128)S(1)} %convolution_select_fusion.1.turned0, f32[264,256]{1,0:T(8,128)S(1)} %get-tuple-element.8.held0, f32[256,256]{1,0:T(8,128)S(1)} %convolution_select_fusion.turned1, ...), custom_call_target="tpu_custom_call" | custom-call | tf_op jit(solution)/shard_map/pallas_call | solution.py:224
  (56 shorter events, 12.1 us)
Async XLA Ops:
  0.6 1.0 copy-start
  1.6 1.7 %copy-start.2 = (f32[2,256,256]{2,1,0:T(8,128)S(1)}, f32[2,256,256]{2,1,0:T(8,128)}, u32[]{:S(2)}) copy-start(f32[2,256,256]{2,1,0:T(8,128)} %param.6) | copy-start | bytes 1572868
  17.0 1.0 copy-start.1
  19.1 0.7 copy-start.3
  21.6 2.4 %collective-permute-start.1 = (f32[264,256]{1,0:T(8,128)S(1)}, f32[264,256]{1,0:T(8,128)S(1)}, u32[]{:S(2)}, u32[]{:S(2)}) collective-permute-start(f32[264,256]{1,0:T(8,128)S(1)} %pad_maximum_fusion.1.held), channel_id=1, source_target_pairs={{0,1},{1,0},{2,3},{3,2},{4,5},{5,4},{6,7},{7,6},{8,9},{9,8},{10,11... | collective-permute-start | bytes 811016 | tf_op jit(solution)/shard_map/ppermute | solution.py:272
  22.2 1.7 %collective-permute-start = (f32[256,256]{1,0:T(8,128)S(1)}, f32[256,256]{1,0:T(8,128)S(1)}, u32[]{:S(2)}, u32[]{:S(2)}) collective-permute-start(f32[256,256]{1,0:T(8,128)S(1)} %fusion.6.turned), channel_id=1, source_target_pairs={{0,1},{1,0},{2,3},{3,2},{4,5},{5,4},{6,7},{7,6},{8,9},{9,8},{10,11... | collective-permute-start | bytes 786440 | tf_op jit(solution)/shard_map/ppermute | solution.py:272
  24.3 9.6 %collective-permute-start.3 = (f32[200,256]{1,0:T(8,128)S(1)}, f32[200,256]{1,0:T(8,128)S(1)}, u32[]{:S(2)}, u32[]{:S(2)}) collective-permute-start(f32[200,256]{1,0:T(8,128)S(1)} %shard_map.60), channel_id=1, source_target_pairs={{2,0},{3,1},{4,2},{5,3},{6,4},{7,5},{8,6},{9,7},{10,8},{11,9},{12,... | collective-permute-start | bytes 614408 | tf_op jit(solution)/shard_map/ppermute | solution.py:284
  26.7 16.0 %collective-permute-start.2 = (f32[200,256]{1,0:T(8,128)S(1)}, f32[200,256]{1,0:T(8,128)S(1)}, u32[]{:S(2)}, u32[]{:S(2)}) collective-permute-start(f32[200,256]{1,0:T(8,128)S(1)} %shard_map.60), channel_id=1, source_target_pairs={{4,0},{5,1},{6,2},{7,3},{8,4},{9,5},{10,6},{11,7},{12,8},{13,9},{1... | collective-permute-start | bytes 614408 | tf_op jit(solution)/shard_map/ppermute | solution.py:284
  33.9 8.8 %collective-permute-start.4 = (f32[192,256]{1,0:T(8,128)S(1)}, f32[192,256]{1,0:T(8,128)S(1)}, u32[]{:S(2)}, u32[]{:S(2)}) collective-permute-start(f32[192,256]{1,0:T(8,128)S(1)} %slice.88), channel_id=1, source_target_pairs={{0,1},{1,0},{2,3},{3,2},{4,5},{5,4},{6,7},{7,6},{8,9},{9,8},{10,11... | collective-permute-start | bytes 589832 | tf_op jit(solution)/shard_map/ppermute | solution.py:272
  43.1 14.3 %collective-permute-start.5 = (f32[200,256]{1,0:T(8,128)S(1)}, f32[200,256]{1,0:T(8,128)S(1)}, u32[]{:S(2)}, u32[]{:S(2)}) collective-permute-start(f32[200,256]{1,0:T(8,128)S(1)} %shard_map.61.mine), channel_id=1, source_target_pairs={{4,0},{5,1},{6,2},{7,3},{8,4},{9,5},{10,6},{11,7},{12,8},{13,9},{1... | collective-permute-start | bytes 614408 | tf_op jit(solution)/shard_map/ppermute | solution.py:284
  45.0 2.2 %collective-permute-start.6 = (f32[192,256]{1,0:T(8,128)S(1)}, f32[192,256]{1,0:T(8,128)S(1)}, u32[]{:S(2)}, u32[]{:S(2)}) collective-permute-start(f32[192,256]{1,0:T(8,128)S(1)} %slice.89), channel_id=1, source_target_pairs={{0,1},{1,0},{2,3},{3,2},{4,5},{5,4},{6,7},{7,6},{8,9},{9,8},{10,11... | collective-permute-start | bytes 589832 | tf_op jit(solution)/shard_map/ppermute | solution.py:272
  57.8 11.9 %collective-permute-start.7 = (f32[200,256]{1,0:T(8,128)S(1)}, f32[200,256]{1,0:T(8,128)S(1)}, u32[]{:S(2)}, u32[]{:S(2)}) collective-permute-start(f32[200,256]{1,0:T(8,128)S(1)} %shard_map.62.mine), channel_id=1, source_target_pairs={{8,0},{9,1},{10,2},{11,3},{12,4},{13,5},{14,6},{15,7},{16,8},{17,9... | collective-permute-start | bytes 614408 | tf_op jit(solution)/shard_map/ppermute | solution.py:284
  59.7 2.2 %collective-permute-start.8 = (f32[192,256]{1,0:T(8,128)S(1)}, f32[192,256]{1,0:T(8,128)S(1)}, u32[]{:S(2)}, u32[]{:S(2)}) collective-permute-start(f32[192,256]{1,0:T(8,128)S(1)} %slice.90), channel_id=1, source_target_pairs={{0,1},{1,0},{2,3},{3,2},{4,5},{5,4},{6,7},{7,6},{8,9},{9,8},{10,11... | collective-permute-start | bytes 589832 | tf_op jit(solution)/shard_map/ppermute | solution.py:272
  70.1 14.4 %collective-permute-start.9 = (f32[200,256]{1,0:T(8,128)S(1)}, f32[200,256]{1,0:T(8,128)S(1)}, u32[]{:S(2)}, u32[]{:S(2)}) collective-permute-start(f32[200,256]{1,0:T(8,128)S(1)} %shard_map.63.mine), channel_id=1, source_target_pairs={{16,0},{17,1},{18,2},{19,3},{20,4},{21,5},{22,6},{23,7},{24,8},{25... | collective-permute-start | bytes 614408 | tf_op jit(solution)/shard_map/ppermute | solution.py:284
  72.0 2.2 %collective-permute-start.10 = (f32[192,256]{1,0:T(8,128)S(1)}, f32[192,256]{1,0:T(8,128)S(1)}, u32[]{:S(2)}, u32[]{:S(2)}) collective-permute-start(f32[192,256]{1,0:T(8,128)S(1)} %slice.91), channel_id=1, source_target_pairs={{0,1},{1,0},{2,3},{3,2},{4,5},{5,4},{6,7},{7,6},{8,9},{9,8},{10,11... | collective-permute-start | bytes 589832 | tf_op jit(solution)/shard_map/ppermute | solution.py:272
  84.8 17.2 %collective-permute-start.11 = (f32[200,256]{1,0:T(8,128)S(1)}, f32[200,256]{1,0:T(8,128)S(1)}, u32[]{:S(2)}, u32[]{:S(2)}) collective-permute-start(f32[200,256]{1,0:T(8,128)S(1)} %shard_map.64.mine), channel_id=1, source_target_pairs={{32,0},{33,1},{34,2},{35,3},{36,4},{37,5},{38,6},{39,7},{40,8},{41... | collective-permute-start | bytes 614408 | tf_op jit(solution)/shard_map/ppermute | solution.py:284
  86.8 2.4 %collective-permute-start.12 = (f32[192,256]{1,0:T(8,128)S(1)}, f32[192,256]{1,0:T(8,128)S(1)}, u32[]{:S(2)}, u32[]{:S(2)}) collective-permute-start(f32[192,256]{1,0:T(8,128)S(1)} %slice.92), channel_id=1, source_target_pairs={{0,1},{1,0},{2,3},{3,2},{4,5},{5,4},{6,7},{7,6},{8,9},{9,8},{10,11... | collective-permute-start | bytes 589832 | tf_op jit(solution)/shard_map/ppermute | solution.py:272
  102.4 9.8 %collective-permute-start.13 = (f32[200,256]{1,0:T(8,128)S(1)}, f32[200,256]{1,0:T(8,128)S(1)}, u32[]{:S(2)}, u32[]{:S(2)}) collective-permute-start(f32[200,256]{1,0:T(8,128)S(1)} %shard_map.65.mine), channel_id=1, source_target_pairs={{64,0},{65,1},{66,2},{67,3},{68,4},{69,5},{70,6},{71,7},{72,8},{73... | collective-permute-start | bytes 614408 | tf_op jit(solution)/shard_map/ppermute | solution.py:284
  103.7 2.2 %collective-permute-start.14 = (f32[192,256]{1,0:T(8,128)S(1)}, f32[192,256]{1,0:T(8,128)S(1)}, u32[]{:S(2)}, u32[]{:S(2)}) collective-permute-start(f32[192,256]{1,0:T(8,128)S(1)} %slice.93), channel_id=1, source_target_pairs={{0,1},{1,0},{2,3},{3,2},{4,5},{5,4},{6,7},{7,6},{8,9},{9,8},{10,11... | collective-permute-start | bytes 589832 | tf_op jit(solution)/shard_map/ppermute | solution.py:272
  112.6 2.2 %collective-permute-start.16 = (f32[192,256]{1,0:T(8,128)S(1)}, f32[192,256]{1,0:T(8,128)S(1)}, u32[]{:S(2)}, u32[]{:S(2)}) collective-permute-start(f32[192,256]{1,0:T(8,128)S(1)} %slice.95), channel_id=1, source_target_pairs={{0,1},{1,0},{2,3},{3,2},{4,5},{5,4},{6,7},{7,6},{8,9},{9,8},{10,11... | collective-permute-start | bytes 589832 | tf_op jit(solution)/shard_map/ppermute | solution.py:272
  113.7 0.7 collective-permute-start.15
  114.7 12.0 %collective-permute-start.17 = (f32[136,256]{1,0:T(8,128)S(1)}, f32[136,256]{1,0:T(8,128)S(1)}, u32[]{:S(2)}, u32[]{:S(2)}) collective-permute-start(f32[136,256]{1,0:T(8,128)S(1)} %shard_map.67), channel_id=1, source_target_pairs={{1,0},{3,2},{5,4},{7,6},{9,8},{11,10},{13,12},{15,14},{17,16},{19,... | collective-permute-start | bytes 417800 | tf_op jit(solution)/shard_map/ppermute | solution.py:301

commit v4 on v3

--- a/solution.py
+++ b/solution.py
@@ -104,11 +104,27 @@
     return jnp.swapaxes(matrix, -1, -2)
 
 
+def halves(value):
+    high = value.astype(jnp.bfloat16)
+    return high, (value - high.astype(jnp.float32)).astype(jnp.bfloat16)
+
+
+def three(left, right, dims):
+    lh, ll = halves(left)
+    rh, rl = halves(right)
+
+    def one(a, b):
+        return lax.dot_general(a, b, (dims, ((), ())), preferred_element_type=jnp.float32)
+
+    return one(lh, rh) + (one(lh, rl) + one(ll, rh))
+
+
+def mdot(left, right):
+    return three(left, right, ((1,), (0,)))
+
+
 def tdot(left, right):
-    return lax.dot_general(
-        left, right, (((0,), (0,)), ((), ())),
-        precision=lax.Precision.HIGHEST, preferred_element_type=jnp.float32,
-    )
+    return three(left, right, ((0,), (0,)))
 
 
 def row_col():
@@ -137,7 +153,7 @@
 
 
 def sandwich(inner, gain):
-    first = dot(inner, gain)
+    first = mdot(inner, gain)
     upper = tdot(gain[:, :HALF], first)
     corner = tdot(gain[:, HALF:], first[:, HALF:])
     return packed(upper, corner)
@@ -158,16 +174,16 @@
 def chip_kernel(core, turned, held, other_turned, other_held, out):
     @pl.when(core[0] == 0)
     def _():
-        out[:TOP] = dot(other_turned[:TOP], turned[...])
+        out[:TOP] = mdot(other_turned[:TOP], turned[...])
         out[TOP:] = jnp.zeros((PART - TOP, NS), jnp.float32)
 
     @pl.when(core[0] == 1)
     def _():
         gain = other_turned[...]
-        out[:LOW] = dot(turned[TOP:], gain)
+        out[:LOW] = mdot(turned[TOP:], gain)
         half, diag = sandwich(held[:NS], gain)
         own, own_diag = packed(other_held[:HALF], other_held[HALF:NS, HALF:])
-        tail = dot(held[NS:], gain) + other_held[NS:]
+        tail = mdot(held[NS:], gain) + other_held[NS:]
         store_held(out, LOW, half + own, diag + own_diag, tail[:1])
 
 
@@ -175,45 +191,46 @@
     @pl.when(core[0] == 0)
     def _():
         gain = jnp.concatenate([mine[:TOP], passed[:LOW]], axis=0)
-        out[:TOP] = dot(got[:TOP], gain)
+        out[:TOP] = mdot(got[:TOP], gain)
         out[TOP:] = jnp.zeros((PART - TOP, NS), jnp.float32)
 
     @pl.when(core[0] == 1)
     def _():
         gain = jnp.concatenate([passed[:TOP], mine[:LOW]], axis=0)
-        out[:LOW] = dot(got[:LOW], gain)
+        out[:LOW] = mdot(got[:LOW], gain)
         inner = unpacked(got[LOW:OFFSET], got[DIAG : DIAG + 1, :HALF])
         half, diag = sandwich(inner, gain)
-        tail = dot(got[OFFSET:], gain)
+        tail = mdot(got[OFFSET:], gain)
         store_held(
             out, LOW, half + mine[LOW:OFFSET], diag + mine[DIAG : DIAG + 1, :HALF],
             tail[:1] + mine[OFFSET : OFFSET + 1],
         )
 
 
-def last_kernel(core, got, mine, passed, out):
-    @pl.when(core[0] == 0)
-    def _():
-        out[...] = jnp.zeros(out.shape, jnp.float32)
-
-    @pl.when(core[0] == 1)
-    def _():
-        gain = jnp.concatenate([passed[:TOP], mine[:LOW]], axis=0)
-        inner = unpacked(got[:HALF], got[HALF + 1 : HALF + 2, :HALF])
-        half, diag = sandwich(inner, gain)
-        tail = dot(got[HALF:], gain)
-        store_held(
-            out, 0, half + mine[LOW:OFFSET], diag + mine[DIAG : DIAG + 1, :HALF],
-            tail[:1] + mine[OFFSET : OFFSET + 1],
-        )
-
-
-def end_kernel(after, turned0, held0, turned1, held1, cov, mean):
+def late_kernel(core, mine, passed, turned0, held0, turned1, held1, gain0, rest0, gain1, rest1):
+    first = core[0] == 0
+    gain = jnp.where(
+        first,
+        jnp.concatenate([mine[:TOP], passed[:LOW]], axis=0),
+        jnp.concatenate([passed[:TOP], mine[:LOW]], axis=0),
+    )
+    own = jnp.where(first, passed[LOW:], mine[LOW:])
+    inner = unpacked(own[:HALF], own[HALF + 1 : HALF + 2, :HALF])
+    for turned, held, full, rest in (
+        (turned0[...], held0, gain0, rest0), (turned1[...], held1, gain1, rest1)
+    ):
+        full[...] = mdot(gain, turned)
+        rest[:NS] = tdot(turned, mdot(inner, turned)) + held[:NS]
+        rest[NS:] = mdot(own[HALF:], turned) + held[NS:]
+
+
+def end_kernel(to_second, to_first, turned0, held0, turned1, held1, cov, mean):
+    after = to_second[...] + to_first[...]
     inner = unpacked(after[:HALF], after[HALF + 1 : HALF + 2, :HALF])
     for i, (turned, held) in enumerate(((turned0, held0), (turned1, held1))):
         gain = turned[...]
-        cov[i] = tdot(gain, dot(inner, gain)) + held[:NS]
-        mean[i : i + 1] = (dot(after[HALF:], gain) + held[NS:])[:1]
+        cov[i] = tdot(gain, mdot(inner, gain)) + held[:NS]
+        mean[i : i + 1] = (mdot(after[HALF:], gain) + held[NS:])[:1]
 
 
 def call(kernel, shapes, scalar, *arrays):
@@ -295,13 +312,19 @@
         passed = swapped(mine[:TOP])
         mine = call(join_kernel, [(PART, NS)], which, got, mine, passed)
         stride *= 2
-    got = fetched(mine[LOW:], stride, (1,))
-    passed = swapped(mine[:TOP])
-    after = call(last_kernel, [(HALF + EXTRA, NS)], which, got, mine, passed)
-    to_first = lax.ppermute(after, AXES, [(2 * c + 1, 2 * c) for c in range(chips)])
-    after = jnp.where(is_first, to_first, after)
+    tails = mine[LOW:]
+    to_second, to_first = [
+        lax.ppermute(tails, AXES, [(2 * (c + stride) + 1, 2 * c + k) for c in range(chips - stride)])
+        for k in (1, 0)
+    ]
+    passed = swapped(mine)
+    square, wide = (NS, NS), (NS + EXTRA, NS)
+    gain0, rest0, gain1, rest1 = call(
+        late_kernel, [square, wide, square, wide], which, mine, passed,
+        late[0], late_held[0], late[1], late_held[1],
+    )
     smooth_cov, smooth_mean = call(
-        end_kernel, [(2, NS, NS), (2, NS)], None, after, late[0], late_held[0], late[1], late_held[1]
+        end_kernel, [(2, NS, NS), (2, NS)], None, to_second, to_first, gain0, rest0, gain1, rest1
     )
     return (smooth_mean, smooth_cov)
 

time: 130 us -> 121 us (0.931)
  starting transfers between devices: 26.7 us -> 21.1 us
  waiting for transfers between devices: 72.6 us -> 68.4 us
    ppermute x9, starting transfers between devices: 8.12 us -> 2.55 us  [swapped(): return lax.ppermute(rows, AXES, swap)]
    ppermute x1 -> x2, waiting for transfers between devices: 10.6 us -> 6.1 us  [local(): lax.ppermute(tails, AXES, [(2 * (c + stride) + 1, 2 * c + k) for c in ran...]
    ppermute x8 -> x7, starting transfers between devices: 17.2 us -> 16.6 us  [fetched(): lax.ppermute(rows, AXES, [(2 * (c + stride) + k, 2 * c + k) for c in rang...]
    ppermute x8 -> x7, waiting for transfers between devices: 57.4 us -> 56.9 us  [fetched(): lax.ppermute(rows, AXES, [(2 * (c + stride) + k, 2 * c + k) for c in rang...]
  transfers between devices with their start and end apart: 18 -> 18, of which waited for: 15 -> 14; matrix products, arithmetic and copies ran while one was open for 2% -> 3% of each run, Pallas kernels for 0% -> 1%
where the time goes in v4:
time: 121 us; the launch traced here: 120 us
  waiting for transfers between devices  68.4 us (57%)
  starting transfers between devices  21.1 us (17%)
  Pallas kernels  18.4 us (15%)
  matrix products  8.15 us (7%)
  local copies, waits for them, and re-layouts  2.63 us (2%)
    ppermute x7, waiting for transfers between devices, fetched(): lax.ppermute(rows, AXES, [(2 * (c + stride) + k, 2 * c + k) for c in rang...  56.9 us
    ppermute x7, starting transfers between devices, fetched(): lax.ppermute(rows, AXES, [(2 * (c + stride) + k, 2 * c + k) for c in rang...  16.6 us
    pallas_call x1, Pallas kernels, solve(): pl.pallas_call(solve_kernel, out_shape=jax.ShapeDtypeStruct(moved.shape,...  13 us
    dot_general x14, matrix products, product(): return jnp.matmul(left, right, precision=lax.Precision.HIGHEST)  8.15 us
    ppermute x2, waiting for transfers between devices, local(): lax.ppermute(tails, AXES, [(2 * (c + stride) + 1, 2 * c + k) for c in ran...  6.1 us
    ppermute x9, waiting for transfers between devices, swapped(): return lax.ppermute(rows, AXES, swap)  5.39 us
    pallas_call x9, Pallas kernels, call(): pl.pallas_call(kernel, out_shape=outs, in_specs=[smem] * len(scalars) + [...  5.38 us
    ppermute x9, starting transfers between devices, swapped(): return lax.ppermute(rows, AXES, swap)  2.55 us
  transfers between devices with their start and end apart: 18, of which 14 were waited for; matrix products, arithmetic and copies ran while one was open for 3% of the time, Pallas kernels for 1%

profile of v4, /device:TPU:240, one launch (start us, length us, event | category | flops | bytes accessed | tf_op | source)
XLA Modules:
  0.0 120.0 jit_solution(10987269937151555377)
XLA Ops:
  0.7 0.9 copy-done
  1.6 1.7 %convolution_bitcast_fusion.moved = f32[2,256,256]{2,1,0:T(8,128)S(1)} fusion(f32[2,256,256]{2,1,0:T(8,128)} %param.5, f32[256,256]{1,0:T(8,128)S(1)} %copy-done), kind=kOutput, calls=%fused_computation.1 | convolution fusion | flops 402653184 | bytes 1310720 | tf_op jit(solution)/shard_map/dot_general | solution.py:252
  3.3 0.6 convolution_add_fusion.pred
  3.9 13.0 %shard_map.59 = f32[2,256,256]{2,1,0:T(8,128)S(1)} custom-call(f32[2,256,256]{2,1,0:T(8,128)S(1)} %convolution_add_fusion.pred, f32[2,256,256]{2,1,0:T(8,128)S(1)} %convolution_bitcast_fusion.moved), custom_call_target="tpu_custom_call" | custom-call | tf_op jit(solution)/shard_map/pallas_call | solution.py:85
  17.1 0.9 copy-done.1
  18.0 1.0 convolution_subtract_fusion
  19.1 0.6 copy-done.3
  22.8 1.2 collective-permute-done.other_turned
  24.2 2.4 %collective-permute-start.3 = (f32[200,256]{1,0:T(8,128)S(1)}, f32[200,256]{1,0:T(8,128)S(1)}, u32[]{:S(2)}, u32[]{:S(2)}) collective-permute-start(f32[200,256]{1,0:T(8,128)S(1)} %shard_map.60), channel_id=1, source_target_pairs={{2,0},{3,1},{4,2},{5,3},{6,4},{7,5},{8,6},{9,7},{10,8},{11,9},{12,... | collective-permute-start | bytes 614408 | tf_op jit(solution)/shard_map/ppermute | solution.py:301
  27.0 5.2 %collective-permute-start.2 = (f32[200,256]{1,0:T(8,128)S(1)}, f32[200,256]{1,0:T(8,128)S(1)}, u32[]{:S(2)}, u32[]{:S(2)}) collective-permute-start(f32[200,256]{1,0:T(8,128)S(1)} %shard_map.60), channel_id=1, source_target_pairs={{4,0},{5,1},{6,2},{7,3},{8,4},{9,5},{10,6},{11,7},{12,8},{13,9},{1... | collective-permute-start | bytes 614408 | tf_op jit(solution)/shard_map/ppermute | solution.py:301
  32.2 1.8 %collective-permute-done.3.mine = f32[200,256]{1,0:T(8,128)S(1)} collective-permute-done((f32[200,256]{1,0:T(8,128)S(1)}, f32[200,256]{1,0:T(8,128)S(1)}, u32[]{:S(2)}, u32[]{:S(2)}) %collective-permute-start.3) | collective-permute-done | bytes 204832 | tf_op jit(solution)/shard_map/ppermute | solution.py:301
  34.6 8.2 %collective-permute-done.2.got = f32[200,256]{1,0:T(8,128)S(1)} collective-permute-done((f32[200,256]{1,0:T(8,128)S(1)}, f32[200,256]{1,0:T(8,128)S(1)}, u32[]{:S(2)}, u32[]{:S(2)}) %collective-permute-start.2) | collective-permute-done | bytes 204832 | tf_op jit(solution)/shard_map/ppermute | solution.py:301
  43.0 1.9 %collective-permute-start.5 = (f32[200,256]{1,0:T(8,128)S(1)}, f32[200,256]{1,0:T(8,128)S(1)}, u32[]{:S(2)}, u32[]{:S(2)}) collective-permute-start(f32[200,256]{1,0:T(8,128)S(1)} %shard_map.61.mine), channel_id=1, source_target_pairs={{4,0},{5,1},{6,2},{7,3},{8,4},{9,5},{10,6},{11,7},{12,8},{13,9},{1... | collective-permute-start | bytes 614408 | tf_op jit(solution)/shard_map/ppermute | solution.py:301
  45.7 0.7 collective-permute-done.6.passed
  46.5 10.2 %collective-permute-done.5.got = f32[200,256]{1,0:T(8,128)S(1)} collective-permute-done((f32[200,256]{1,0:T(8,128)S(1)}, f32[200,256]{1,0:T(8,128)S(1)}, u32[]{:S(2)}, u32[]{:S(2)}) %collective-permute-start.5) | collective-permute-done | bytes 204832 | tf_op jit(solution)/shard_map/ppermute | solution.py:301
  57.0 1.9 %collective-permute-start.7 = (f32[200,256]{1,0:T(8,128)S(1)}, f32[200,256]{1,0:T(8,128)S(1)}, u32[]{:S(2)}, u32[]{:S(2)}) collective-permute-start(f32[200,256]{1,0:T(8,128)S(1)} %shard_map.62.mine), channel_id=1, source_target_pairs={{8,0},{9,1},{10,2},{11,3},{12,4},{13,5},{14,6},{15,7},{16,8},{17,9... | collective-permute-start | bytes 614408 | tf_op jit(solution)/shard_map/ppermute | solution.py:301
  59.0 0.6 convolution_add_fusion.1
  59.6 0.8 collective-permute-done.8.passed
  60.5 7.5 %collective-permute-done.7.got = f32[200,256]{1,0:T(8,128)S(1)} collective-permute-done((f32[200,256]{1,0:T(8,128)S(1)}, f32[200,256]{1,0:T(8,128)S(1)}, u32[]{:S(2)}, u32[]{:S(2)}) %collective-permute-start.7) | collective-permute-done | bytes 204832 | tf_op jit(solution)/shard_map/ppermute | solution.py:301
  68.2 1.9 %collective-permute-start.9 = (f32[200,256]{1,0:T(8,128)S(1)}, f32[200,256]{1,0:T(8,128)S(1)}, u32[]{:S(2)}, u32[]{:S(2)}) collective-permute-start(f32[200,256]{1,0:T(8,128)S(1)} %shard_map.63.mine), channel_id=1, source_target_pairs={{16,0},{17,1},{18,2},{19,3},{20,4},{21,5},{22,6},{23,7},{24,8},{25... | collective-permute-start | bytes 614408 | tf_op jit(solution)/shard_map/ppermute | solution.py:301
  70.7 1.0 collective-permute-done.10.passed
  71.7 9.6 %collective-permute-done.9.got = f32[200,256]{1,0:T(8,128)S(1)} collective-permute-done((f32[200,256]{1,0:T(8,128)S(1)}, f32[200,256]{1,0:T(8,128)S(1)}, u32[]{:S(2)}, u32[]{:S(2)}) %collective-permute-start.9) | collective-permute-done | bytes 204832 | tf_op jit(solution)/shard_map/ppermute | solution.py:301
  81.6 1.9 %collective-permute-start.11 = (f32[200,256]{1,0:T(8,128)S(1)}, f32[200,256]{1,0:T(8,128)S(1)}, u32[]{:S(2)}, u32[]{:S(2)}) collective-permute-start(f32[200,256]{1,0:T(8,128)S(1)} %shard_map.64.mine), channel_id=1, source_target_pairs={{32,0},{33,1},{34,2},{35,3},{36,4},{37,5},{38,6},{39,7},{40,8},{41... | collective-permute-start | bytes 614408 | tf_op jit(solution)/shard_map/ppermute | solution.py:301
  85.1 13.1 %collective-permute-done.11.got = f32[200,256]{1,0:T(8,128)S(1)} collective-permute-done((f32[200,256]{1,0:T(8,128)S(1)}, f32[200,256]{1,0:T(8,128)S(1)}, u32[]{:S(2)}, u32[]{:S(2)}) %collective-permute-start.11) | collective-permute-done | bytes 204832 | tf_op jit(solution)/shard_map/ppermute | solution.py:301
  98.4 1.3 %collective-permute-start.13 = (f32[200,256]{1,0:T(8,128)S(1)}, f32[200,256]{1,0:T(8,128)S(1)}, u32[]{:S(2)}, u32[]{:S(2)}) collective-permute-start(f32[200,256]{1,0:T(8,128)S(1)} %shard_map.65.mine), channel_id=1, source_target_pairs={{64,0},{65,1},{66,2},{67,3},{68,4},{69,5},{70,6},{71,7},{72,8},{73... | collective-permute-start | bytes 614408 | tf_op jit(solution)/shard_map/ppermute | solution.py:301
  100.3 1.1 collective-permute-done.14.passed
  101.4 6.4 %collective-permute-done.13.got = f32[200,256]{1,0:T(8,128)S(1)} collective-permute-done((f32[200,256]{1,0:T(8,128)S(1)}, f32[200,256]{1,0:T(8,128)S(1)}, u32[]{:S(2)}, u32[]{:S(2)}) %collective-permute-start.13) | collective-permute-done | bytes 204832 | tf_op jit(solution)/shard_map/ppermute | solution.py:301
  108.4 0.7 collective-permute-start.15
  109.1 1.3 %collective-permute-start.16 = (f32[136,256]{1,0:T(8,128)S(1)}, f32[136,256]{1,0:T(8,128)S(1)}, u32[]{:S(2)}, u32[]{:S(2)}) collective-permute-start(f32[136,256]{1,0:T(8,128)S(1)} %slice.90), channel_id=1, source_target_pairs={{129,0},{131,2},{133,4},{135,6},{137,8},{139,10},{141,12},{143,14}... | collective-permute-start | bytes 417800 | tf_op jit(solution)/shard_map/ppermute | solution.py:317
  110.5 1.3 %shard_map.67 = (f32[256,256]{1,0:T(8,128)S(1)}, f32[264,256]{1,0:T(8,128)S(1)}, f32[256,256]{1,0:T(8,128)S(1)}, f32[264,256]{1,0:T(8,128)S(1)}) custom-call(s32[1]{0:T(128)} %bitcast.core, f32[200,256]{1,0:T(8,128)S(1)} %shard_map.66.mine, f32[200,256]{1,0:T(8,128)S(1)} %collective-permute-done.17.passed, f32[256,256]{1,0:T(8,128)S(1)} %convolution_select_fusion.1.turned0, ...), custom_call_target="tpu_custom_call" | custom-call | tf_op jit(solution)/shard_map/pallas_call | solution.py:241
  111.8 6.1 %collective-permute-done.16.to_first = f32[136,256]{1,0:T(8,128)S(1)} collective-permute-done((f32[136,256]{1,0:T(8,128)S(1)}, f32[136,256]{1,0:T(8,128)S(1)}, u32[]{:S(2)}, u32[]{:S(2)}) %collective-permute-start.16) | collective-permute-done | bytes 139296 | tf_op jit(solution)/shard_map/ppermute | solution.py:317
  117.9 2.1 %shard_map.68 = (f32[2,256,256]{2,1,0:T(8,128)}, f32[2,256]{1,0:T(2,128)}) custom-call(f32[136,256]{1,0:T(8,128)S(1)} %collective-permute-done.15.to_second, f32[136,256]{1,0:T(8,128)S(1)} %collective-permute-done.16.to_first, f32[256,256]{1,0:T(8,128)S(1)} %get-tuple-element.8.turned0, f32[264,256]{1,0:T(8,128)S(1)} %get-tuple-element.9.held0, ...), custom_call_target="tpu_custom_call" | custom-call | tf_op jit(solution)/shard_map/pallas_call | solution.py:241
  (54 shorter events, 9.7 us)
Async XLA Ops:
  0.6 1.0 copy-start
  1.6 1.7 %copy-start.2 = (f32[2,256,256]{2,1,0:T(8,128)S(1)}, f32[2,256,256]{2,1,0:T(8,128)}, u32[]{:S(2)}) copy-start(f32[2,256,256]{2,1,0:T(8,128)} %param.6) | copy-start | bytes 1572868
  17.0 1.0 copy-start.1
  19.1 0.7 copy-start.3
  21.5 2.4 %collective-permute-start.1 = (f32[264,256]{1,0:T(8,128)S(1)}, f32[264,256]{1,0:T(8,128)S(1)}, u32[]{:S(2)}, u32[]{:S(2)}) collective-permute-start(f32[264,256]{1,0:T(8,128)S(1)} %pad_maximum_fusion.1.held), channel_id=1, source_target_pairs={{0,1},{1,0},{2,3},{3,2},{4,5},{5,4},{6,7},{7,6},{8,9},{9,8},{10,11... | collective-permute-start | bytes 811016 | tf_op jit(solution)/shard_map/ppermute | solution.py:289
  22.2 1.7 %collective-permute-start = (f32[256,256]{1,0:T(8,128)S(1)}, f32[256,256]{1,0:T(8,128)S(1)}, u32[]{:S(2)}, u32[]{:S(2)}) collective-permute-start(f32[256,256]{1,0:T(8,128)S(1)} %fusion.6.turned), channel_id=1, source_target_pairs={{0,1},{1,0},{2,3},{3,2},{4,5},{5,4},{6,7},{7,6},{8,9},{9,8},{10,11... | collective-permute-start | bytes 786440 | tf_op jit(solution)/shard_map/ppermute | solution.py:289
  24.2 9.8 %collective-permute-start.3 = (f32[200,256]{1,0:T(8,128)S(1)}, f32[200,256]{1,0:T(8,128)S(1)}, u32[]{:S(2)}, u32[]{:S(2)}) collective-permute-start(f32[200,256]{1,0:T(8,128)S(1)} %shard_map.60), channel_id=1, source_target_pairs={{2,0},{3,1},{4,2},{5,3},{6,4},{7,5},{8,6},{9,7},{10,8},{11,9},{12,... | collective-permute-start | bytes 614408 | tf_op jit(solution)/shard_map/ppermute | solution.py:301
  27.0 15.7 %collective-permute-start.2 = (f32[200,256]{1,0:T(8,128)S(1)}, f32[200,256]{1,0:T(8,128)S(1)}, u32[]{:S(2)}, u32[]{:S(2)}) collective-permute-start(f32[200,256]{1,0:T(8,128)S(1)} %shard_map.60), channel_id=1, source_target_pairs={{4,0},{5,1},{6,2},{7,3},{8,4},{9,5},{10,6},{11,7},{12,8},{13,9},{1... | collective-permute-start | bytes 614408 | tf_op jit(solution)/shard_map/ppermute | solution.py:301
  34.1 8.7 %collective-permute-start.4 = (f32[192,256]{1,0:T(8,128)S(1)}, f32[192,256]{1,0:T(8,128)S(1)}, u32[]{:S(2)}, u32[]{:S(2)}) collective-permute-start(f32[192,256]{1,0:T(8,128)S(1)} %slice.84), channel_id=1, source_target_pairs={{0,1},{1,0},{2,3},{3,2},{4,5},{5,4},{6,7},{7,6},{8,9},{9,8},{10,11... | collective-permute-start | bytes 589832 | tf_op jit(solution)/shard_map/ppermute | solution.py:289
  43.0 13.7 %collective-permute-start.5 = (f32[200,256]{1,0:T(8,128)S(1)}, f32[200,256]{1,0:T(8,128)S(1)}, u32[]{:S(2)}, u32[]{:S(2)}) collective-permute-start(f32[200,256]{1,0:T(8,128)S(1)} %shard_map.61.mine), channel_id=1, source_target_pairs={{4,0},{5,1},{6,2},{7,3},{8,4},{9,5},{10,6},{11,7},{12,8},{13,9},{1... | collective-permute-start | bytes 614408 | tf_op jit(solution)/shard_map/ppermute | solution.py:301
  44.9 1.5 %collective-permute-start.6 = (f32[192,256]{1,0:T(8,128)S(1)}, f32[192,256]{1,0:T(8,128)S(1)}, u32[]{:S(2)}, u32[]{:S(2)}) collective-permute-start(f32[192,256]{1,0:T(8,128)S(1)} %slice.85), channel_id=1, source_target_pairs={{0,1},{1,0},{2,3},{3,2},{4,5},{5,4},{6,7},{7,6},{8,9},{9,8},{10,11... | collective-permute-start | bytes 589832 | tf_op jit(solution)/shard_map/ppermute | solution.py:289
  57.0 10.9 %collective-permute-start.7 = (f32[200,256]{1,0:T(8,128)S(1)}, f32[200,256]{1,0:T(8,128)S(1)}, u32[]{:S(2)}, u32[]{:S(2)}) collective-permute-start(f32[200,256]{1,0:T(8,128)S(1)} %shard_map.62.mine), channel_id=1, source_target_pairs={{8,0},{9,1},{10,2},{11,3},{12,4},{13,5},{14,6},{15,7},{16,8},{17,9... | collective-permute-start | bytes 614408 | tf_op jit(solution)/shard_map/ppermute | solution.py:301
  58.9 1.5 %collective-permute-start.8 = (f32[192,256]{1,0:T(8,128)S(1)}, f32[192,256]{1,0:T(8,128)S(1)}, u32[]{:S(2)}, u32[]{:S(2)}) collective-permute-start(f32[192,256]{1,0:T(8,128)S(1)} %slice.86), channel_id=1, source_target_pairs={{0,1},{1,0},{2,3},{3,2},{4,5},{5,4},{6,7},{7,6},{8,9},{9,8},{10,11... | collective-permute-start | bytes 589832 | tf_op jit(solution)/shard_map/ppermute | solution.py:289
  68.2 13.1 %collective-permute-start.9 = (f32[200,256]{1,0:T(8,128)S(1)}, f32[200,256]{1,0:T(8,128)S(1)}, u32[]{:S(2)}, u32[]{:S(2)}) collective-permute-start(f32[200,256]{1,0:T(8,128)S(1)} %shard_map.63.mine), channel_id=1, source_target_pairs={{16,0},{17,1},{18,2},{19,3},{20,4},{21,5},{22,6},{23,7},{24,8},{25... | collective-permute-start | bytes 614408 | tf_op jit(solution)/shard_map/ppermute | solution.py:301
  70.2 1.5 %collective-permute-start.10 = (f32[192,256]{1,0:T(8,128)S(1)}, f32[192,256]{1,0:T(8,128)S(1)}, u32[]{:S(2)}, u32[]{:S(2)}) collective-permute-start(f32[192,256]{1,0:T(8,128)S(1)} %slice.87), channel_id=1, source_target_pairs={{0,1},{1,0},{2,3},{3,2},{4,5},{5,4},{6,7},{7,6},{8,9},{9,8},{10,11... | collective-permute-start | bytes 589832 | tf_op jit(solution)/shard_map/ppermute | solution.py:289
  81.6 16.5 %collective-permute-start.11 = (f32[200,256]{1,0:T(8,128)S(1)}, f32[200,256]{1,0:T(8,128)S(1)}, u32[]{:S(2)}, u32[]{:S(2)}) collective-permute-start(f32[200,256]{1,0:T(8,128)S(1)} %shard_map.64.mine), channel_id=1, source_target_pairs={{32,0},{33,1},{34,2},{35,3},{36,4},{37,5},{38,6},{39,7},{40,8},{41... | collective-permute-start | bytes 614408 | tf_op jit(solution)/shard_map/ppermute | solution.py:301
  83.5 1.5 %collective-permute-start.12 = (f32[192,256]{1,0:T(8,128)S(1)}, f32[192,256]{1,0:T(8,128)S(1)}, u32[]{:S(2)}, u32[]{:S(2)}) collective-permute-start(f32[192,256]{1,0:T(8,128)S(1)} %slice.88), channel_id=1, source_target_pairs={{0,1},{1,0},{2,3},{3,2},{4,5},{5,4},{6,7},{7,6},{8,9},{9,8},{10,11... | collective-permute-start | bytes 589832 | tf_op jit(solution)/shard_map/ppermute | solution.py:289
  98.4 9.4 %collective-permute-start.13 = (f32[200,256]{1,0:T(8,128)S(1)}, f32[200,256]{1,0:T(8,128)S(1)}, u32[]{:S(2)}, u32[]{:S(2)}) collective-permute-start(f32[200,256]{1,0:T(8,128)S(1)} %shard_map.65.mine), channel_id=1, source_target_pairs={{64,0},{65,1},{66,2},{67,3},{68,4},{69,5},{70,6},{71,7},{72,8},{73... | collective-permute-start | bytes 614408 | tf_op jit(solution)/shard_map/ppermute | solution.py:301
  99.7 1.6 %collective-permute-start.14 = (f32[192,256]{1,0:T(8,128)S(1)}, f32[192,256]{1,0:T(8,128)S(1)}, u32[]{:S(2)}, u32[]{:S(2)}) collective-permute-start(f32[192,256]{1,0:T(8,128)S(1)} %slice.89), channel_id=1, source_target_pairs={{0,1},{1,0},{2,3},{3,2},{4,5},{5,4},{6,7},{7,6},{8,9},{9,8},{10,11... | collective-permute-start | bytes 589832 | tf_op jit(solution)/shard_map/ppermute | solution.py:289
  108.3 2.2 %collective-permute-start.17 = (f32[200,256]{1,0:T(8,128)S(1)}, f32[200,256]{1,0:T(8,128)S(1)}, u32[]{:S(2)}, u32[]{:S(2)}) collective-permute-start(f32[200,256]{1,0:T(8,128)S(1)} %shard_map.66.mine), channel_id=1, source_target_pairs={{0,1},{1,0},{2,3},{3,2},{4,5},{5,4},{6,7},{7,6},{8,9},{9,8},{10,11... | collective-permute-start | bytes 614408 | tf_op jit(solution)/shard_map/ppermute | solution.py:289
  108.4 3.4 %collective-permute-start.15 = (f32[136,256]{1,0:T(8,128)S(1)}, f32[136,256]{1,0:T(8,128)S(1)}, u32[]{:S(2)}, u32[]{:S(2)}) collective-permute-start(f32[136,256]{1,0:T(8,128)S(1)} %slice.90), channel_id=1, source_target_pairs={{129,1},{131,3},{133,5},{135,7},{137,9},{139,11},{141,13},{143,15}... | collective-permute-start | bytes 417800 | tf_op jit(solution)/shard_map/ppermute | solution.py:317
  109.1 8.8 %collective-permute-start.16 = (f32[136,256]{1,0:T(8,128)S(1)}, f32[136,256]{1,0:T(8,128)S(1)}, u32[]{:S(2)}, u32[]{:S(2)}) collective-permute-start(f32[136,256]{1,0:T(8,128)S(1)} %slice.90), channel_id=1, source_target_pairs={{129,0},{131,2},{133,4},{135,6},{137,8},{139,10},{141,12},{143,14}... | collective-permute-start | bytes 417800 | tf_op jit(solution)/shard_map/ppermute | solution.py:317

commit v5 on v4

--- a/solution.py
+++ b/solution.py
@@ -8,7 +8,7 @@
 AXES = ("grp", "dev")
 EXTRA = 8
 
-BASE = 32
+BASE = 16
 HALF = 128
 
 
@@ -16,80 +16,88 @@
     return jnp.dot(left, right, precision=lax.Precision.HIGHEST, preferred_element_type=jnp.float32)
 
 
-def base_inverse(first, second):
-    unit = (lax.broadcasted_iota(jnp.int32, (BASE, BASE), 0) == lax.broadcasted_iota(jnp.int32, (BASE, BASE), 1)).astype(jnp.float32)
-    whole = jnp.concatenate([first, unit, second, unit], axis=1)
-    tiles = [whole[8 * i : 8 * i + 8] for i in range(BASE // 8)]
-    lane = lax.broadcasted_iota(jnp.int32, (8, 128), 1)
-    sub = lax.broadcasted_iota(jnp.int32, (8, 128), 0)
+def eliminated(tops, base):
+    tiles = [[t[8 * i : 8 * i + 8] for i in range(BASE // 8)] for t in tops]
+    lane = lax.broadcasted_iota(jnp.int32, (8, HALF), 1)
+    sub = lax.broadcasted_iota(jnp.int32, (8, HALF), 0)
+
+    def spread(row):
+        return jnp.broadcast_to(row, (8, HALF))
+
     for q in range(BASE // 8):
         cols = []
-        for j in range(8):
-            at = 8 * q + j
-            cols.append([
-                jnp.where(lane < 64, jnp.broadcast_to(t[:, at : at + 1], (8, 128)), jnp.broadcast_to(t[:, 64 + at : 65 + at], (8, 128)))
-                for t in tiles
-            ])
+        for m in range(2):
+            at = base + 8 * q
+            cols.append([[spread(t[:, at + j : at + j + 1]) for t in tiles[m]] for j in range(8)])
         for k in range(8):
-            def row(t):
-                return jnp.broadcast_to(t[k : k + 1], (8, 128))
-            ratio = 1.0 / row(cols[k][q])
-            scaled = row(tiles[q]) * ratio
-            factors = [row(cols[j][q]) * ratio for j in range(k + 1, 8)]
-            down = list(cols[k])
-            down[q] = down[q] - jnp.where(sub == k, 1.0, 0.0)
-            tiles = [t - d * scaled for t, d in zip(tiles, down)]
-            for j, f in zip(range(k + 1, 8), factors):
-                cols[j] = [c - d * f for c, d in zip(cols[j], down)]
-    whole = jnp.concatenate(tiles, axis=0)
-    return whole[:, BASE : 2 * BASE], whole[:, 64 + BASE : 64 + 2 * BASE]
-
-
-def half_inverse(work):
-    for j in range(HALF // BASE):
+            here = lane == base + 8 * q + k
+            unit = jnp.where(sub == k, 1.0, 0.0)
+            for m in range(2):
+                col, tile = cols[m], tiles[m]
+                ratio = 1.0 / (spread(col[k][q][k : k + 1]))
+                scaled = jnp.where(here, ratio, spread(tile[q][k : k + 1]) * ratio)
+                factors = [spread(col[j][q][k : k + 1]) * ratio for j in range(k + 1, 8)]
+                down = list(col[k])
+                down[q] = down[q] - unit
+                for i in range(BASE // 8):
+                    old = jnp.where(here, unit if i == q else 0.0, tile[i])
+                    tile[i] = old - down[i] * scaled
+                for j, f in zip(range(k + 1, 8), factors):
+                    col[j] = [c - d * f for c, d in zip(col[j], down)]
+    return [jnp.concatenate(t, axis=0) for t in tiles]
+
+
+def less_product(rows, base, inside, new):
+    parts = []
+    for i in range(BASE // 8):
+        old = rows[8 * i : 8 * i + 8]
+        terms = [
+            jnp.broadcast_to(old[:, base + k : base + k + 1], (8, HALF)) * jnp.broadcast_to(new[k : k + 1], (8, HALF))
+            for k in range(BASE)
+        ]
+        while len(terms) > 1:
+            terms = [a + b for a, b in zip(terms[::2], terms[1::2])]
+        parts.append(jnp.where(inside[:8], 0.0, old) - terms[0])
+    return jnp.concatenate(parts, axis=0)
+
+
+def half_inverse(pair):
+    lane = lax.broadcasted_iota(jnp.int32, (BASE, HALF), 1)
+    count = HALF // BASE
+    pair = [[p[BASE * i : BASE * i + BASE] for i in range(count)] for p in pair]
+    for j in range(count):
         rows = slice(BASE * j, BASE * j + BASE)
-        inv = base_inverse(work[0, rows, rows], work[1, rows, rows])
-        lane = lax.broadcasted_iota(jnp.int32, (HALF, HALF), 1)
         inside = (lane >= BASE * j) & (lane < BASE * (j + 1))
-        r = lax.broadcasted_iota(jnp.int32, (BASE, HALF), 0)
-        c = lax.broadcasted_iota(jnp.int32, (BASE, HALF), 1)
+        news = eliminated([p[j] for p in pair], BASE * j)
         for m in range(2):
-            old = work[m]
-            top = jnp.where(inside[:BASE], (c == r + BASE * j).astype(jnp.float32), old[rows])
-            new = dot(inv[m], top)
-            work[m] = jnp.where(inside, 0.0, old) - dot(old[:, rows], new)
-            work[m, rows] = new
-
-
-def solve_kernel(pred, moved, out, work):
+            first = (j + 1) % count
+            rest = [i for i in range(count) if i not in (j, first)]
+            old = pair[m]
+            new = [None] * count
+            new[j] = news[m]
+            new[first] = less_product(old[first], BASE * j, inside, news[m])
+            tall = jnp.concatenate([old[i][:, rows] for i in rest], axis=0)
+            tall = dot(tall, news[m])
+            for n, i in enumerate(rest):
+                new[i] = jnp.where(inside, 0.0, old[i]) - tall[BASE * n : BASE * n + BASE]
+            pair[m] = new
+    return [jnp.concatenate(p, axis=0) for p in pair]
+
+
+def solved_pair(pred, moved):
     lo, hi = slice(0, HALF), slice(HALF, 2 * HALF)
+    inv = half_inverse([p[lo, lo] for p in pred])
+    wide, corner, out = [], [], []
     for m in range(2):
-        work[m] = pred[m, lo, lo]
-    half_inverse(work)
-    wide, rest = [], []
+        wide.append(dot(inv[m], jnp.concatenate([pred[m][lo, hi], moved[m][lo]], axis=1)))
+        corner.append(pred[m][hi, hi] - dot(pred[m][hi, lo], wide[m][:, :HALF]))
+    inv = half_inverse(corner)
     for m in range(2):
-        rhs = jnp.concatenate([pred[m, lo, hi], moved[m, lo]], axis=1)
-        w = dot(work[m], rhs)
-        s = jnp.concatenate([pred[m, hi, hi], moved[m, hi]], axis=1) - dot(pred[m, hi, lo], w)
-        wide.append(w)
-        rest.append(s[:, HALF:])
-        work[m] = s[:, :HALF]
-    half_inverse(work)
-    for m in range(2):
-        h2 = dot(work[m], rest[m])
-        out[m, hi] = h2
-        out[m, lo] = wide[m][:, HALF:] - dot(wide[m][:, :HALF], h2)
-
-
-def solve(pred, moved):
-    return pl.pallas_call(
-        solve_kernel,
-        out_shape=jax.ShapeDtypeStruct(moved.shape, jnp.float32),
-        in_specs=[pl.BlockSpec(memory_space=pltpu.VMEM)] * 2,
-        out_specs=pl.BlockSpec(memory_space=pltpu.VMEM),
-        scratch_shapes=[pltpu.VMEM((2, HALF, HALF), jnp.float32)],
-        compiler_params=pltpu.CompilerParams(vmem_limit_bytes=32 * 1024 * 1024),
-    )(pred, moved)
+        rest = moved[m][hi] - dot(pred[m][hi, lo], wide[m][:, HALF:])
+        low = dot(inv[m], rest)
+        top = wide[m][:, HALF:] - dot(wide[m][:, :HALF], low)
+        out.append(jnp.concatenate([top, low], axis=0))
+    return out
 
 
 NS = 256
@@ -171,20 +179,46 @@
     out[base + HALF : base + HALF + EXTRA] = tail
 
 
-def chip_kernel(core, turned, held, other_turned, other_held, out):
+def exact(left, right, dims):
+    return lax.dot_general(
+        left, right, (dims, ((), ())),
+        precision=lax.Precision.HIGHEST, preferred_element_type=jnp.float32,
+    )
+
+
+def local_kernel(final, mean, cov, noise, transition, both, turned1, held1):
+    step = transition[...]
+    moved = [dot(step, cov[m]) for m in range(2)]
+    pred = [exact(moved[m], step, ((1,), (1,))) + noise[m] for m in range(2)]
+    gains = solved_pair(pred, moved)
+    gains[1] = jnp.where(final[0] == 1, 0.0, gains[1])
+    means = jnp.concatenate([mean[...], jnp.zeros((EXTRA - 2, NS), jnp.float32)], axis=0)
+    ahead = exact(means, step, ((1,), (1,)))
+    rests = [cov[m] - exact(gains[m], moved[m], ((0,), (0,))) for m in range(2)]
+    offsets = [means - dot(ahead, gains[m]) for m in range(2)]
+    turned1[...] = gains[1]
+    held1[:NS] = rests[1]
+    held1[NS:] = jnp.broadcast_to(offsets[1][1:2], (EXTRA, NS))
+    both[:NS] = mdot(gains[1], gains[0])
+    both[NS : 2 * NS] = tdot(gains[0], mdot(rests[1], gains[0])) + rests[0]
+    second = mdot(offsets[1], gains[0])[1:2]
+    both[2 * NS :] = jnp.broadcast_to(second + offsets[0][:1], (EXTRA, NS))
+
+
+def chip_kernel(core, own, other, out):
     @pl.when(core[0] == 0)
     def _():
-        out[:TOP] = mdot(other_turned[:TOP], turned[...])
+        out[:TOP] = mdot(other[:TOP], own[:NS])
         out[TOP:] = jnp.zeros((PART - TOP, NS), jnp.float32)
 
     @pl.when(core[0] == 1)
     def _():
-        gain = other_turned[...]
-        out[:LOW] = mdot(turned[TOP:], gain)
-        half, diag = sandwich(held[:NS], gain)
-        own, own_diag = packed(other_held[:HALF], other_held[HALF:NS, HALF:])
-        tail = mdot(held[NS:], gain) + other_held[NS:]
-        store_held(out, LOW, half + own, diag + own_diag, tail[:1])
+        gain = other[:NS]
+        out[:LOW] = mdot(own[TOP:NS], gain)
+        half, diag = sandwich(own[NS : 2 * NS], gain)
+        add, add_diag = packed(other[NS : NS + HALF], other[NS + HALF : 2 * NS, HALF:])
+        tail = mdot(own[2 * NS :], gain) + other[2 * NS :]
+        store_held(out, LOW, half + add, diag + add_diag, tail[:1])
 
 
 def join_kernel(core, got, mine, passed, out):
@@ -252,10 +286,6 @@
     return jnp.matmul(left, right, precision=lax.Precision.HIGHEST)
 
 
-def grown(matrix, row):
-    return jnp.concatenate([matrix, jnp.broadcast_to(row, (EXTRA, row.shape[-1]))], axis=0)
-
-
 def applied(turned, held_next, held):
     width = turned.shape[0]
     first = product(held_next, turned)
@@ -270,31 +300,25 @@
     core = place % 2
     is_first = core == 0
     which = core.astype(jnp.int32)[None]
-    moved = product(transition, filt_cov)
-    predicted = product(moved, transition.T) + noise_cov
-    solved = solve(predicted, moved)
-    final = (place == devices - 1) & (jnp.arange(2) == 1)
-    solved = jnp.where(final[:, None, None], 0.0, solved)
-    ahead = product(filt_mean, transition.T)
-    offset = filt_mean - product(ahead[:, None, :], solved)[:, 0]
-    remainder = filt_cov - product(flipped(solved), moved)
-    turned = [solved[0], solved[1]]
-    held = [grown(remainder[0], offset[0]), grown(remainder[1], offset[1])]
-    both_turned = product(turned[1], turned[0])
-    both_held = applied(turned[0], held[1], held[0])
+    final = (place == devices - 1).astype(jnp.int32)[None]
+    wide = (NS + EXTRA, NS)
+    both, turned1, held1 = call(
+        local_kernel, [(2 * NS + EXTRA, NS), (NS, NS), wide], final,
+        filt_mean, filt_cov, noise_cov, transition,
+    )
 
     swap = [(p, p ^ 1) for p in range(devices)]
 
     def swapped(rows):
         return lax.ppermute(rows, AXES, swap)
 
-    other_turned = swapped(both_turned)
-    other_held = swapped(both_held)
-    chip = call(chip_kernel, [(PART, NS)], which, both_turned, both_held, other_turned, other_held)
-    late = [jnp.where(is_first, product(other_turned, t), t) for t in (both_turned, turned[1])]
+    other = swapped(both)
+    chip = call(chip_kernel, [(PART, NS)], which, both, other)
+    both_turned, both_held = both[:NS], both[NS:]
+    late = [jnp.where(is_first, product(other[:NS], t), t) for t in (both_turned, turned1)]
     late_held = [
-        jnp.where(is_first, applied(t, other_held, h), h)
-        for t, h in ((both_turned, both_held), (turned[1], held[1]))
+        jnp.where(is_first, applied(t, other[NS:], h), h)
+        for t, h in ((both_turned, both_held), (turned1, held1))
     ]
 
     def fetched(rows, stride, cores):
@@ -318,7 +342,7 @@
         for k in (1, 0)
     ]
     passed = swapped(mine)
-    square, wide = (NS, NS), (NS + EXTRA, NS)
+    square = (NS, NS)
     gain0, rest0, gain1, rest1 = call(
         late_kernel, [square, wide, square, wide], which, mine, passed,
         late[0], late_held[0], late[1], late_held[1],

time: 121 us -> 114 us (0.942)
  matrix products: 8.15 us -> 2.73 us
    pallas_call x1 -> x0, Pallas kernels: 13 us -> none  [solve(): pl.pallas_call(solve_kernel, out_shape=jax.ShapeDtypeStruct(moved.shape,...]
    pallas_call x9 -> x10, Pallas kernels: 5.38 us -> 18 us  [call(): pl.pallas_call(kernel, out_shape=outs, in_specs=[smem] * len(scalars) + [...]
    dot_general x14 -> x6, matrix products: 8.15 us -> 2.73 us  [product(): return jnp.matmul(left, right, precision=lax.Precision.HIGHEST)]
    ppermute x7, waiting for transfers between devices: 56.9 us -> 55.1 us  [fetched(): lax.ppermute(rows, AXES, [(2 * (c + stride) + k, 2 * c + k) for c in rang...]
    ppermute x9 -> x8, waiting for transfers between devices: 5.39 us -> 7.11 us  [swapped(): return lax.ppermute(rows, AXES, swap)]
    ppermute x9 -> x8, starting transfers between devices: 2.55 us -> 1.5 us  [swapped(): return lax.ppermute(rows, AXES, swap)]
  transfers between devices with their start and end apart: 18 -> 17, of which waited for: 14 -> 14; matrix products, arithmetic and copies ran while one was open for 3% -> 2% of each run, Pallas kernels for 1% -> 1%
where the time goes in v5:
time: 114 us
  waiting for transfers between devices  68.3 us (60%)
  starting transfers between devices  20.2 us (18%)
  Pallas kernels  18 us (16%)
  local copies, waits for them, and re-layouts  3.8 us (3%)
  matrix products  2.73 us (2%)
    ppermute x7, waiting for transfers between devices, fetched(): lax.ppermute(rows, AXES, [(2 * (c + stride) + k, 2 * c + k) for c in rang...  55.1 us
    pallas_call x10, Pallas kernels, call(): pl.pallas_call(kernel, out_shape=outs, in_specs=[smem] * len(scalars) + [...  18 us
    ppermute x7, starting transfers between devices, fetched(): lax.ppermute(rows, AXES, [(2 * (c + stride) + k, 2 * c + k) for c in rang...  16.8 us
    ppermute x8, waiting for transfers between devices, swapped(): return lax.ppermute(rows, AXES, swap)  7.11 us
    ppermute x2, waiting for transfers between devices, local(): lax.ppermute(tails, AXES, [(2 * (c + stride) + 1, 2 * c + k) for c in ran...  6.03 us
    unnamed x8, local copies, waits for them, and re-layouts  3.71 us
    dot_general x6, matrix products, product(): return jnp.matmul(left, right, precision=lax.Precision.HIGHEST)  2.73 us
  transfers between devices with their start and end apart: 17, of which 14 were waited for; matrix products, arithmetic and copies ran while one was open for 2% of the time, Pallas kernels for 1%

profile of v5, /device:TPU:240, one launch (start us, length us, event | category | flops | bytes accessed | tf_op | source)
XLA Modules:
  0.0 114.0 jit_solution(16187157348130815108)
XLA Ops:
  0.6 0.7 copy-done.3
  1.3 1.0 copy-done
  2.4 1.0 copy-done.1
  3.4 0.9 copy-done.2
  4.4 12.8 %shard_map.59 = (f32[520,256]{1,0:T(8,128)S(1)}, f32[256,256]{1,0:T(8,128)S(1)}, f32[264,256]{1,0:T(8,128)S(1)}) custom-call(s32[1]{0:T(128)} %bitcast.1.final, f32[2,256]{1,0:T(2,128)S(1)} %copy-done.3, f32[2,256,256]{2,1,0:T(8,128)S(1)} %copy-done, f32[2,256,256]{2,1,0:T(8,128)S(1)} %copy-done.1, f32[256,256]{1,0:T(8,128)S(1)} %copy-done.2), custom_call_target="tpu_custom_call" | custom-call | tf_op jit(solution)/shard_map/pallas_call | solution.py:275
  17.3 1.9 %collective-permute-done.other = f32[520,256]{1,0:T(8,128)S(1)} collective-permute-done((f32[520,256]{1,0:T(8,128)S(1)}, f32[520,256]{1,0:T(8,128)S(1)}, u32[]{:S(2)}, u32[]{:S(2)}) %collective-permute-start) | collective-permute-done | bytes 532512 | tf_op jit(solution)/shard_map/ppermute | solution.py:313
  19.4 2.5 %collective-permute-start.2 = (f32[200,256]{1,0:T(8,128)S(1)}, f32[200,256]{1,0:T(8,128)S(1)}, u32[]{:S(2)}, u32[]{:S(2)}) collective-permute-start(f32[200,256]{1,0:T(8,128)S(1)} %shard_map.60), channel_id=1, source_target_pairs={{2,0},{3,1},{4,2},{5,3},{6,4},{7,5},{8,6},{9,7},{10,8},{11,9},{12,... | collective-permute-start | bytes 614408 | tf_op jit(solution)/shard_map/ppermute | solution.py:325
  22.0 5.3 %collective-permute-start.1 = (f32[200,256]{1,0:T(8,128)S(1)}, f32[200,256]{1,0:T(8,128)S(1)}, u32[]{:S(2)}, u32[]{:S(2)}) collective-permute-start(f32[200,256]{1,0:T(8,128)S(1)} %shard_map.60), channel_id=1, source_target_pairs={{4,0},{5,1},{6,2},{7,3},{8,4},{9,5},{10,6},{11,7},{12,8},{13,9},{1... | collective-permute-start | bytes 614408 | tf_op jit(solution)/shard_map/ppermute | solution.py:325
  27.6 0.6 convolution_add_fusion
  28.3 0.9 collective-permute-done.2.mine
  29.7 8.0 %collective-permute-done.1.got = f32[200,256]{1,0:T(8,128)S(1)} collective-permute-done((f32[200,256]{1,0:T(8,128)S(1)}, f32[200,256]{1,0:T(8,128)S(1)}, u32[]{:S(2)}, u32[]{:S(2)}) %collective-permute-start.1) | collective-permute-done | bytes 204832 | tf_op jit(solution)/shard_map/ppermute | solution.py:325
  38.0 1.9 %collective-permute-start.4 = (f32[200,256]{1,0:T(8,128)S(1)}, f32[200,256]{1,0:T(8,128)S(1)}, u32[]{:S(2)}, u32[]{:S(2)}) collective-permute-start(f32[200,256]{1,0:T(8,128)S(1)} %shard_map.61.mine), channel_id=1, source_target_pairs={{4,0},{5,1},{6,2},{7,3},{8,4},{9,5},{10,6},{11,7},{12,8},{13,9},{1... | collective-permute-start | bytes 614408 | tf_op jit(solution)/shard_map/ppermute | solution.py:325
  40.2 0.6 convolution_add_fusion.1
  40.8 0.7 collective-permute-done.5.passed
  41.5 10.1 %collective-permute-done.4.got = f32[200,256]{1,0:T(8,128)S(1)} collective-permute-done((f32[200,256]{1,0:T(8,128)S(1)}, f32[200,256]{1,0:T(8,128)S(1)}, u32[]{:S(2)}, u32[]{:S(2)}) %collective-permute-start.4) | collective-permute-done | bytes 204832 | tf_op jit(solution)/shard_map/ppermute | solution.py:325
  51.9 1.9 %collective-permute-start.6 = (f32[200,256]{1,0:T(8,128)S(1)}, f32[200,256]{1,0:T(8,128)S(1)}, u32[]{:S(2)}, u32[]{:S(2)}) collective-permute-start(f32[200,256]{1,0:T(8,128)S(1)} %shard_map.62.mine), channel_id=1, source_target_pairs={{8,0},{9,1},{10,2},{11,3},{12,4},{13,5},{14,6},{15,7},{16,8},{17,9... | collective-permute-start | bytes 614408 | tf_op jit(solution)/shard_map/ppermute | solution.py:325
  54.3 1.0 collective-permute-done.7.passed
  55.3 7.3 %collective-permute-done.6.got = f32[200,256]{1,0:T(8,128)S(1)} collective-permute-done((f32[200,256]{1,0:T(8,128)S(1)}, f32[200,256]{1,0:T(8,128)S(1)}, u32[]{:S(2)}, u32[]{:S(2)}) %collective-permute-start.6) | collective-permute-done | bytes 204832 | tf_op jit(solution)/shard_map/ppermute | solution.py:325
  62.9 1.9 %collective-permute-start.8 = (f32[200,256]{1,0:T(8,128)S(1)}, f32[200,256]{1,0:T(8,128)S(1)}, u32[]{:S(2)}, u32[]{:S(2)}) collective-permute-start(f32[200,256]{1,0:T(8,128)S(1)} %shard_map.63.mine), channel_id=1, source_target_pairs={{16,0},{17,1},{18,2},{19,3},{20,4},{21,5},{22,6},{23,7},{24,8},{25... | collective-permute-start | bytes 614408 | tf_op jit(solution)/shard_map/ppermute | solution.py:325
  65.3 1.0 collective-permute-done.9.passed
  66.4 9.4 %collective-permute-done.8.got = f32[200,256]{1,0:T(8,128)S(1)} collective-permute-done((f32[200,256]{1,0:T(8,128)S(1)}, f32[200,256]{1,0:T(8,128)S(1)}, u32[]{:S(2)}, u32[]{:S(2)}) %collective-permute-start.8) | collective-permute-done | bytes 204832 | tf_op jit(solution)/shard_map/ppermute | solution.py:325
  76.1 1.9 %collective-permute-start.10 = (f32[200,256]{1,0:T(8,128)S(1)}, f32[200,256]{1,0:T(8,128)S(1)}, u32[]{:S(2)}, u32[]{:S(2)}) collective-permute-start(f32[200,256]{1,0:T(8,128)S(1)} %shard_map.64.mine), channel_id=1, source_target_pairs={{32,0},{33,1},{34,2},{35,3},{36,4},{37,5},{38,6},{39,7},{40,8},{41... | collective-permute-start | bytes 614408 | tf_op jit(solution)/shard_map/ppermute | solution.py:325
  78.1 1.4 %collective-permute-done.11.passed = f32[192,256]{1,0:T(8,128)S(1)} collective-permute-done((f32[192,256]{1,0:T(8,128)S(1)}, f32[192,256]{1,0:T(8,128)S(1)}, u32[]{:S(2)}, u32[]{:S(2)}) %collective-permute-start.11) | collective-permute-done | bytes 196640 | tf_op jit(solution)/shard_map/ppermute | solution.py:313
  79.6 12.9 %collective-permute-done.10.got = f32[200,256]{1,0:T(8,128)S(1)} collective-permute-done((f32[200,256]{1,0:T(8,128)S(1)}, f32[200,256]{1,0:T(8,128)S(1)}, u32[]{:S(2)}, u32[]{:S(2)}) %collective-permute-start.10) | collective-permute-done | bytes 204832 | tf_op jit(solution)/shard_map/ppermute | solution.py:325
  92.8 1.3 %collective-permute-start.12 = (f32[200,256]{1,0:T(8,128)S(1)}, f32[200,256]{1,0:T(8,128)S(1)}, u32[]{:S(2)}, u32[]{:S(2)}) collective-permute-start(f32[200,256]{1,0:T(8,128)S(1)} %shard_map.65.mine), channel_id=1, source_target_pairs={{64,0},{65,1},{66,2},{67,3},{68,4},{69,5},{70,6},{71,7},{72,8},{73... | collective-permute-start | bytes 614408 | tf_op jit(solution)/shard_map/ppermute | solution.py:325
  94.7 1.0 collective-permute-done.13.passed
  95.7 6.4 %collective-permute-done.12.got = f32[200,256]{1,0:T(8,128)S(1)} collective-permute-done((f32[200,256]{1,0:T(8,128)S(1)}, f32[200,256]{1,0:T(8,128)S(1)}, u32[]{:S(2)}, u32[]{:S(2)}) %collective-permute-start.12) | collective-permute-done | bytes 204832 | tf_op jit(solution)/shard_map/ppermute | solution.py:325
  102.6 0.7 collective-permute-start.14
  103.3 1.3 %collective-permute-start.15 = (f32[136,256]{1,0:T(8,128)S(1)}, f32[136,256]{1,0:T(8,128)S(1)}, u32[]{:S(2)}, u32[]{:S(2)}) collective-permute-start(f32[136,256]{1,0:T(8,128)S(1)} %slice.86), channel_id=1, source_target_pairs={{129,0},{131,2},{133,4},{135,6},{137,8},{139,10},{141,12},{143,14}... | collective-permute-start | bytes 417800 | tf_op jit(solution)/shard_map/ppermute | solution.py:341
  104.6 1.3 %shard_map.67 = (f32[256,256]{1,0:T(8,128)S(1)}, f32[264,256]{1,0:T(8,128)S(1)}, f32[256,256]{1,0:T(8,128)S(1)}, f32[264,256]{1,0:T(8,128)S(1)}) custom-call(s32[1]{0:T(128)} %bitcast.core, f32[200,256]{1,0:T(8,128)S(1)} %shard_map.66.mine, f32[200,256]{1,0:T(8,128)S(1)} %collective-permute-done.16.passed, f32[256,256]{1,0:T(8,128)S(1)} %convolution_select_fusion.1.turned0, ...), custom_call_target="tpu_custom_call" | custom-call | tf_op jit(solution)/shard_map/pallas_call | solution.py:275
  105.9 6.0 %collective-permute-done.15.to_first = f32[136,256]{1,0:T(8,128)S(1)} collective-permute-done((f32[136,256]{1,0:T(8,128)S(1)}, f32[136,256]{1,0:T(8,128)S(1)}, u32[]{:S(2)}, u32[]{:S(2)}) %collective-permute-start.15) | collective-permute-done | bytes 139296 | tf_op jit(solution)/shard_map/ppermute | solution.py:341
  112.0 2.1 %shard_map.68 = (f32[2,256,256]{2,1,0:T(8,128)}, f32[2,256]{1,0:T(2,128)}) custom-call(f32[136,256]{1,0:T(8,128)S(1)} %collective-permute-done.14.to_second, f32[136,256]{1,0:T(8,128)S(1)} %collective-permute-done.15.to_first, f32[256,256]{1,0:T(8,128)S(1)} %get-tuple-element.14.turned0, f32[264,256]{1,0:T(8,128)S(1)} %get-tuple-element.15.held0, ...), custom_call_target="tpu_custom_call" | custom-call | tf_op jit(solution)/shard_map/pallas_call | solution.py:275
  (36 shorter events, 5.0 us)
Async XLA Ops:
  0.6 0.7 copy-start.3
  1.3 1.0 copy-start
  2.4 1.0 copy-start.1
  3.4 0.9 copy-start.2
  17.2 2.0 %collective-permute-start = (f32[520,256]{1,0:T(8,128)S(1)}, f32[520,256]{1,0:T(8,128)S(1)}, u32[]{:S(2)}, u32[]{:S(2)}) collective-permute-start(f32[520,256]{1,0:T(8,128)S(1)} %get-tuple-element.11.own), channel_id=1, source_target_pairs={{0,1},{1,0},{2,3},{3,2},{4,5},{5,4},{6,7},{7,6},{8,9},{9,8},{10,11... | collective-permute-start | bytes 1597448 | tf_op jit(solution)/shard_map/ppermute | solution.py:313
  19.4 9.8 %collective-permute-start.2 = (f32[200,256]{1,0:T(8,128)S(1)}, f32[200,256]{1,0:T(8,128)S(1)}, u32[]{:S(2)}, u32[]{:S(2)}) collective-permute-start(f32[200,256]{1,0:T(8,128)S(1)} %shard_map.60), channel_id=1, source_target_pairs={{2,0},{3,1},{4,2},{5,3},{6,4},{7,5},{8,6},{9,7},{10,8},{11,9},{12,... | collective-permute-start | bytes 614408 | tf_op jit(solution)/shard_map/ppermute | solution.py:325
  22.0 15.8 %collective-permute-start.1 = (f32[200,256]{1,0:T(8,128)S(1)}, f32[200,256]{1,0:T(8,128)S(1)}, u32[]{:S(2)}, u32[]{:S(2)}) collective-permute-start(f32[200,256]{1,0:T(8,128)S(1)} %shard_map.60), channel_id=1, source_target_pairs={{4,0},{5,1},{6,2},{7,3},{8,4},{9,5},{10,6},{11,7},{12,8},{13,9},{1... | collective-permute-start | bytes 614408 | tf_op jit(solution)/shard_map/ppermute | solution.py:325
  29.2 8.5 %collective-permute-start.3 = (f32[192,256]{1,0:T(8,128)S(1)}, f32[192,256]{1,0:T(8,128)S(1)}, u32[]{:S(2)}, u32[]{:S(2)}) collective-permute-start(f32[192,256]{1,0:T(8,128)S(1)} %slice.80), channel_id=1, source_target_pairs={{0,1},{1,0},{2,3},{3,2},{4,5},{5,4},{6,7},{7,6},{8,9},{9,8},{10,11... | collective-permute-start | bytes 589832 | tf_op jit(solution)/shard_map/ppermute | solution.py:313
  38.0 13.5 %collective-permute-start.4 = (f32[200,256]{1,0:T(8,128)S(1)}, f32[200,256]{1,0:T(8,128)S(1)}, u32[]{:S(2)}, u32[]{:S(2)}) collective-permute-start(f32[200,256]{1,0:T(8,128)S(1)} %shard_map.61.mine), channel_id=1, source_target_pairs={{4,0},{5,1},{6,2},{7,3},{8,4},{9,5},{10,6},{11,7},{12,8},{13,9},{1... | collective-permute-start | bytes 614408 | tf_op jit(solution)/shard_map/ppermute | solution.py:325
  40.0 1.5 %collective-permute-start.5 = (f32[192,256]{1,0:T(8,128)S(1)}, f32[192,256]{1,0:T(8,128)S(1)}, u32[]{:S(2)}, u32[]{:S(2)}) collective-permute-start(f32[192,256]{1,0:T(8,128)S(1)} %slice.81), channel_id=1, source_target_pairs={{0,1},{1,0},{2,3},{3,2},{4,5},{5,4},{6,7},{7,6},{8,9},{9,8},{10,11... | collective-permute-start | bytes 589832 | tf_op jit(solution)/shard_map/ppermute | solution.py:313
  51.9 10.8 %collective-permute-start.6 = (f32[200,256]{1,0:T(8,128)S(1)}, f32[200,256]{1,0:T(8,128)S(1)}, u32[]{:S(2)}, u32[]{:S(2)}) collective-permute-start(f32[200,256]{1,0:T(8,128)S(1)} %shard_map.62.mine), channel_id=1, source_target_pairs={{8,0},{9,1},{10,2},{11,3},{12,4},{13,5},{14,6},{15,7},{16,8},{17,9... | collective-permute-start | bytes 614408 | tf_op jit(solution)/shard_map/ppermute | solution.py:325
  53.8 1.5 %collective-permute-start.7 = (f32[192,256]{1,0:T(8,128)S(1)}, f32[192,256]{1,0:T(8,128)S(1)}, u32[]{:S(2)}, u32[]{:S(2)}) collective-permute-start(f32[192,256]{1,0:T(8,128)S(1)} %slice.82), channel_id=1, source_target_pairs={{0,1},{1,0},{2,3},{3,2},{4,5},{5,4},{6,7},{7,6},{8,9},{9,8},{10,11... | collective-permute-start | bytes 589832 | tf_op jit(solution)/shard_map/ppermute | solution.py:313
  62.9 12.9 %collective-permute-start.8 = (f32[200,256]{1,0:T(8,128)S(1)}, f32[200,256]{1,0:T(8,128)S(1)}, u32[]{:S(2)}, u32[]{:S(2)}) collective-permute-start(f32[200,256]{1,0:T(8,128)S(1)} %shard_map.63.mine), channel_id=1, source_target_pairs={{16,0},{17,1},{18,2},{19,3},{20,4},{21,5},{22,6},{23,7},{24,8},{25... | collective-permute-start | bytes 614408 | tf_op jit(solution)/shard_map/ppermute | solution.py:325
  64.8 1.5 %collective-permute-start.9 = (f32[192,256]{1,0:T(8,128)S(1)}, f32[192,256]{1,0:T(8,128)S(1)}, u32[]{:S(2)}, u32[]{:S(2)}) collective-permute-start(f32[192,256]{1,0:T(8,128)S(1)} %slice.83), channel_id=1, source_target_pairs={{0,1},{1,0},{2,3},{3,2},{4,5},{5,4},{6,7},{7,6},{8,9},{9,8},{10,11... | collective-permute-start | bytes 589832 | tf_op jit(solution)/shard_map/ppermute | solution.py:313
  76.1 16.4 %collective-permute-start.10 = (f32[200,256]{1,0:T(8,128)S(1)}, f32[200,256]{1,0:T(8,128)S(1)}, u32[]{:S(2)}, u32[]{:S(2)}) collective-permute-start(f32[200,256]{1,0:T(8,128)S(1)} %shard_map.64.mine), channel_id=1, source_target_pairs={{32,0},{33,1},{34,2},{35,3},{36,4},{37,5},{38,6},{39,7},{40,8},{41... | collective-permute-start | bytes 614408 | tf_op jit(solution)/shard_map/ppermute | solution.py:325
  78.0 1.5 %collective-permute-start.11 = (f32[192,256]{1,0:T(8,128)S(1)}, f32[192,256]{1,0:T(8,128)S(1)}, u32[]{:S(2)}, u32[]{:S(2)}) collective-permute-start(f32[192,256]{1,0:T(8,128)S(1)} %slice.84), channel_id=1, source_target_pairs={{0,1},{1,0},{2,3},{3,2},{4,5},{5,4},{6,7},{7,6},{8,9},{9,8},{10,11... | collective-permute-start | bytes 589832 | tf_op jit(solution)/shard_map/ppermute | solution.py:313
  92.8 9.3 %collective-permute-start.12 = (f32[200,256]{1,0:T(8,128)S(1)}, f32[200,256]{1,0:T(8,128)S(1)}, u32[]{:S(2)}, u32[]{:S(2)}) collective-permute-start(f32[200,256]{1,0:T(8,128)S(1)} %shard_map.65.mine), channel_id=1, source_target_pairs={{64,0},{65,1},{66,2},{67,3},{68,4},{69,5},{70,6},{71,7},{72,8},{73... | collective-permute-start | bytes 614408 | tf_op jit(solution)/shard_map/ppermute | solution.py:325
  94.1 1.6 %collective-permute-start.13 = (f32[192,256]{1,0:T(8,128)S(1)}, f32[192,256]{1,0:T(8,128)S(1)}, u32[]{:S(2)}, u32[]{:S(2)}) collective-permute-start(f32[192,256]{1,0:T(8,128)S(1)} %slice.85), channel_id=1, source_target_pairs={{0,1},{1,0},{2,3},{3,2},{4,5},{5,4},{6,7},{7,6},{8,9},{9,8},{10,11... | collective-permute-start | bytes 589832 | tf_op jit(solution)/shard_map/ppermute | solution.py:313
  102.4 2.3 %collective-permute-start.16 = (f32[200,256]{1,0:T(8,128)S(1)}, f32[200,256]{1,0:T(8,128)S(1)}, u32[]{:S(2)}, u32[]{:S(2)}) collective-permute-start(f32[200,256]{1,0:T(8,128)S(1)} %shard_map.66.mine), channel_id=1, source_target_pairs={{0,1},{1,0},{2,3},{3,2},{4,5},{5,4},{6,7},{7,6},{8,9},{9,8},{10,11... | collective-permute-start | bytes 614408 | tf_op jit(solution)/shard_map/ppermute | solution.py:313
  102.6 3.3 %collective-permute-start.14 = (f32[136,256]{1,0:T(8,128)S(1)}, f32[136,256]{1,0:T(8,128)S(1)}, u32[]{:S(2)}, u32[]{:S(2)}) collective-permute-start(f32[136,256]{1,0:T(8,128)S(1)} %slice.86), channel_id=1, source_target_pairs={{129,1},{131,3},{133,5},{135,7},{137,9},{139,11},{141,13},{143,15}... | collective-permute-start | bytes 417800 | tf_op jit(solution)/shard_map/ppermute | solution.py:341
  103.3 8.7 %collective-permute-start.15 = (f32[136,256]{1,0:T(8,128)S(1)}, f32[136,256]{1,0:T(8,128)S(1)}, u32[]{:S(2)}, u32[]{:S(2)}) collective-permute-start(f32[136,256]{1,0:T(8,128)S(1)} %slice.86), channel_id=1, source_target_pairs={{129,0},{131,2},{133,4},{135,6},{137,8},{139,10},{141,12},{143,14}... | collective-permute-start | bytes 417800 | tf_op jit(solution)/shard_map/ppermute | solution.py:341

commit v6 on v5

--- a/solution.py
+++ b/solution.py
@@ -186,9 +186,22 @@
     )
 
 
-def local_kernel(final, mean, cov, noise, transition, both, turned1, held1):
-    step = transition[...]
-    moved = [dot(step, cov[m]) for m in range(2)]
+def local_kernel(
+    final, mean_in, cov_in, noise_in, step_in, both, turned1, held1, mean, cov, noise, step_at, done
+):
+    moves = [(step_in, step_at), (cov_in.at[0], cov.at[0]), (cov_in.at[1], cov.at[1])]
+    moves += [(noise_in.at[0], noise.at[0]), (noise_in.at[1], noise.at[1]), (mean_in, mean)]
+    copies = [pltpu.make_async_copy(a, b, done.at[i]) for i, (a, b) in enumerate(moves)]
+    for copy in copies:
+        copy.start()
+    copies[0].wait()
+    step = step_at[...]
+    moved = []
+    for m in range(2):
+        copies[1 + m].wait()
+        moved.append(dot(step, cov[m]))
+    for copy in copies[3:]:
+        copy.wait()
     pred = [exact(moved[m], step, ((1,), (1,))) + noise[m] for m in range(2)]
     gains = solved_pair(pred, moved)
     gains[1] = jnp.where(final[0] == 1, 0.0, gains[1])
@@ -258,25 +271,31 @@
         rest[NS:] = mdot(own[HALF:], turned) + held[NS:]
 
 
-def end_kernel(to_second, to_first, turned0, held0, turned1, held1, cov, mean):
+def end_kernel(to_second, to_first, turned0, held0, turned1, held1, cov_out, mean, cov, done):
     after = to_second[...] + to_first[...]
     inner = unpacked(after[:HALF], after[HALF + 1 : HALF + 2, :HALF])
+    copies = [pltpu.make_async_copy(cov.at[i], cov_out.at[i], done.at[i]) for i in range(2)]
     for i, (turned, held) in enumerate(((turned0, held0), (turned1, held1))):
         gain = turned[...]
         cov[i] = tdot(gain, mdot(inner, gain)) + held[:NS]
+        copies[i].start()
         mean[i : i + 1] = (mdot(after[HALF:], gain) + held[NS:])[:1]
-
-
-def call(kernel, shapes, scalar, *arrays):
+    for copy in copies:
+        copy.wait()
+
+
+def call(kernel, shapes, scalar, *arrays, far_in=False, far_out=(), scratch=()):
     vmem = pl.BlockSpec(memory_space=pltpu.VMEM)
+    far = pl.BlockSpec(memory_space=pltpu.HBM)
     smem = pl.BlockSpec(memory_space=pltpu.SMEM)
     scalars = [] if scalar is None else [scalar]
     outs = [jax.ShapeDtypeStruct(s, jnp.float32) for s in shapes]
     done = pl.pallas_call(
         kernel,
         out_shape=outs,
-        in_specs=[smem] * len(scalars) + [vmem] * len(arrays),
-        out_specs=[vmem] * len(outs),
+        in_specs=[smem] * len(scalars) + [far if far_in else vmem] * len(arrays),
+        out_specs=[far if i in far_out else vmem for i in range(len(outs))],
+        scratch_shapes=scratch,
         compiler_params=pltpu.CompilerParams(vmem_limit_bytes=32 * 1024 * 1024),
     )(*scalars, *arrays)
     return done if len(outs) > 1 else done[0]
@@ -304,7 +323,12 @@
     wide = (NS + EXTRA, NS)
     both, turned1, held1 = call(
         local_kernel, [(2 * NS + EXTRA, NS), (NS, NS), wide], final,
-        filt_mean, filt_cov, noise_cov, transition,
+        *(pltpu.with_memory_space_constraint(a, pltpu.HBM) for a in (filt_mean, filt_cov, noise_cov, transition)),
+        far_in=True,
+        scratch=[
+            *(pltpu.VMEM(a.shape, jnp.float32) for a in (filt_mean, filt_cov, noise_cov, transition)),
+            pltpu.SemaphoreType.DMA((6,)),
+        ],
     )
 
     swap = [(p, p ^ 1) for p in range(devices)]
@@ -348,7 +372,8 @@
         late[0], late_held[0], late[1], late_held[1],
     )
     smooth_cov, smooth_mean = call(
-        end_kernel, [(2, NS, NS), (2, NS)], None, to_second, to_first, gain0, rest0, gain1, rest1
+        end_kernel, [(2, NS, NS), (2, NS)], None, to_second, to_first, gain0, rest0, gain1, rest1,
+        far_out=(0,), scratch=[pltpu.VMEM((2, NS, NS), jnp.float32), pltpu.SemaphoreType.DMA((2,))],
     )
     return (smooth_mean, smooth_cov)
 

time: 114 us -> 112 us (0.982)
  local copies, waits for them, and re-layouts: 3.8 us -> 0.1 us
  Pallas kernels: 18 us -> 20.4 us
    unnamed x8 -> x0, local copies, waits for them, and re-layouts: 3.71 us -> none
    pallas_call x10, Pallas kernels: 18 us -> 20.4 us  [call(): pl.pallas_call(kernel, out_shape=outs, in_specs=[smem] * len(scalars) + [...]
  transfers between devices with their start and end apart: 17 -> 17, of which waited for: 14 -> 14; matrix products, arithmetic and copies ran while one was open for 2% -> 3% of each run, Pallas kernels for 1% -> 1%
where the time goes in v6:
time: 112 us
  waiting for transfers between devices  67.3 us (60%)
  Pallas kernels  20.4 us (18%)
  starting transfers between devices  19.9 us (18%)
  matrix products  2.73 us (2%)
  between operations  1.14 us (1%)
    ppermute x7, waiting for transfers between devices, fetched(): lax.ppermute(rows, AXES, [(2 * (c + stride) + k, 2 * c + k) for c in rang...  54.1 us
    pallas_call x10, Pallas kernels, call(): pl.pallas_call(kernel, out_shape=outs, in_specs=[smem] * len(scalars) + [...  20.4 us
    ppermute x7, starting transfers between devices, fetched(): lax.ppermute(rows, AXES, [(2 * (c + stride) + k, 2 * c + k) for c in rang...  16.6 us
    ppermute x8, waiting for transfers between devices, swapped(): return lax.ppermute(rows, AXES, swap)  7.25 us
    ppermute x2, waiting for transfers between devices, local(): lax.ppermute(tails, AXES, [(2 * (c + stride) + 1, 2 * c + k) for c in ran...  6.04 us
    dot_general x6, matrix products, product(): return jnp.matmul(left, right, precision=lax.Precision.HIGHEST)  2.73 us
  transfers between devices with their start and end apart: 17, of which 14 were waited for; matrix products, arithmetic and copies ran while one was open for 3% of the time, Pallas kernels for 1%

profile of v6, /device:TPU:240, one launch (start us, length us, event | category | flops | bytes accessed | tf_op | source)
XLA Modules:
  0.0 111.7 jit_solution(15564086123010436939)
XLA Ops:
  0.6 14.6 %shard_map.59 = (f32[520,256]{1,0:T(8,128)S(1)}, f32[256,256]{1,0:T(8,128)S(1)}, f32[264,256]{1,0:T(8,128)S(1)}) custom-call(s32[1]{0:T(128)} %bitcast.1.final, f32[2,256]{1,0:T(2,128)} %mean_in.1, f32[2,256,256]{2,1,0:T(8,128)} %cov_in.1, f32[2,256,256]{2,1,0:T(8,128)} %noise_in.1, f32[256,256]{1,0:T(8,128)} %step_in.1), custom_call_target="tpu_custom_call" | custom-call | tf_op jit(solution)/shard_map/pallas_call | solution.py:293
  15.3 1.9 %collective-permute-done.other = f32[520,256]{1,0:T(8,128)S(1)} collective-permute-done((f32[520,256]{1,0:T(8,128)S(1)}, f32[520,256]{1,0:T(8,128)S(1)}, u32[]{:S(2)}, u32[]{:S(2)}) %collective-permute-start) | collective-permute-done | bytes 532512 | tf_op jit(solution)/shard_map/ppermute | solution.py:337
  17.2 0.4 shard_map.60
  17.7 2.4 %collective-permute-start.2 = (f32[200,256]{1,0:T(8,128)S(1)}, f32[200,256]{1,0:T(8,128)S(1)}, u32[]{:S(2)}, u32[]{:S(2)}) collective-permute-start(f32[200,256]{1,0:T(8,128)S(1)} %shard_map.60), channel_id=1, source_target_pairs={{2,0},{3,1},{4,2},{5,3},{6,4},{7,5},{8,6},{9,7},{10,8},{11,9},{12,... | collective-permute-start | bytes 614408 | tf_op jit(solution)/shard_map/ppermute | solution.py:349
  20.0 5.3 %collective-permute-start.1 = (f32[200,256]{1,0:T(8,128)S(1)}, f32[200,256]{1,0:T(8,128)S(1)}, u32[]{:S(2)}, u32[]{:S(2)}) collective-permute-start(f32[200,256]{1,0:T(8,128)S(1)} %shard_map.60), channel_id=1, source_target_pairs={{4,0},{5,1},{6,2},{7,3},{8,4},{9,5},{10,6},{11,7},{12,8},{13,9},{1... | collective-permute-start | bytes 614408 | tf_op jit(solution)/shard_map/ppermute | solution.py:349
  25.3 0.4 fusion.2
  25.7 0.6 convolution_add_fusion
  26.3 1.1 %collective-permute-done.2.mine = f32[200,256]{1,0:T(8,128)S(1)} collective-permute-done((f32[200,256]{1,0:T(8,128)S(1)}, f32[200,256]{1,0:T(8,128)S(1)}, u32[]{:S(2)}, u32[]{:S(2)}) %collective-permute-start.2) | collective-permute-done | bytes 204832 | tf_op jit(solution)/shard_map/ppermute | solution.py:349
  27.6 0.4 fusion.4
  28.0 7.8 %collective-permute-done.1.got = f32[200,256]{1,0:T(8,128)S(1)} collective-permute-done((f32[200,256]{1,0:T(8,128)S(1)}, f32[200,256]{1,0:T(8,128)S(1)}, u32[]{:S(2)}, u32[]{:S(2)}) %collective-permute-start.1) | collective-permute-done | bytes 204832 | tf_op jit(solution)/shard_map/ppermute | solution.py:349
  36.1 1.9 %collective-permute-start.4 = (f32[200,256]{1,0:T(8,128)S(1)}, f32[200,256]{1,0:T(8,128)S(1)}, u32[]{:S(2)}, u32[]{:S(2)}) collective-permute-start(f32[200,256]{1,0:T(8,128)S(1)} %shard_map.61.mine), channel_id=1, source_target_pairs={{4,0},{5,1},{6,2},{7,3},{8,4},{9,5},{10,6},{11,7},{12,8},{13,9},{1... | collective-permute-start | bytes 614408 | tf_op jit(solution)/shard_map/ppermute | solution.py:349
  38.1 0.6 convolution_add_fusion.1
  38.7 0.8 collective-permute-done.5.passed
  39.5 9.9 %collective-permute-done.4.got = f32[200,256]{1,0:T(8,128)S(1)} collective-permute-done((f32[200,256]{1,0:T(8,128)S(1)}, f32[200,256]{1,0:T(8,128)S(1)}, u32[]{:S(2)}, u32[]{:S(2)}) %collective-permute-start.4) | collective-permute-done | bytes 204832 | tf_op jit(solution)/shard_map/ppermute | solution.py:349
  49.7 1.9 %collective-permute-start.6 = (f32[200,256]{1,0:T(8,128)S(1)}, f32[200,256]{1,0:T(8,128)S(1)}, u32[]{:S(2)}, u32[]{:S(2)}) collective-permute-start(f32[200,256]{1,0:T(8,128)S(1)} %shard_map.62.mine), channel_id=1, source_target_pairs={{8,0},{9,1},{10,2},{11,3},{12,4},{13,5},{14,6},{15,7},{16,8},{17,9... | collective-permute-start | bytes 614408 | tf_op jit(solution)/shard_map/ppermute | solution.py:349
  52.1 1.0 collective-permute-done.7.passed
  53.1 7.1 %collective-permute-done.6.got = f32[200,256]{1,0:T(8,128)S(1)} collective-permute-done((f32[200,256]{1,0:T(8,128)S(1)}, f32[200,256]{1,0:T(8,128)S(1)}, u32[]{:S(2)}, u32[]{:S(2)}) %collective-permute-start.6) | collective-permute-done | bytes 204832 | tf_op jit(solution)/shard_map/ppermute | solution.py:349
  60.5 1.9 %collective-permute-start.8 = (f32[200,256]{1,0:T(8,128)S(1)}, f32[200,256]{1,0:T(8,128)S(1)}, u32[]{:S(2)}, u32[]{:S(2)}) collective-permute-start(f32[200,256]{1,0:T(8,128)S(1)} %shard_map.63.mine), channel_id=1, source_target_pairs={{16,0},{17,1},{18,2},{19,3},{20,4},{21,5},{22,6},{23,7},{24,8},{25... | collective-permute-start | bytes 614408 | tf_op jit(solution)/shard_map/ppermute | solution.py:349
  62.9 1.0 collective-permute-done.9.passed
  63.9 9.1 %collective-permute-done.8.got = f32[200,256]{1,0:T(8,128)S(1)} collective-permute-done((f32[200,256]{1,0:T(8,128)S(1)}, f32[200,256]{1,0:T(8,128)S(1)}, u32[]{:S(2)}, u32[]{:S(2)}) %collective-permute-start.8) | collective-permute-done | bytes 204832 | tf_op jit(solution)/shard_map/ppermute | solution.py:349
  73.3 1.9 %collective-permute-start.10 = (f32[200,256]{1,0:T(8,128)S(1)}, f32[200,256]{1,0:T(8,128)S(1)}, u32[]{:S(2)}, u32[]{:S(2)}) collective-permute-start(f32[200,256]{1,0:T(8,128)S(1)} %shard_map.64.mine), channel_id=1, source_target_pairs={{32,0},{33,1},{34,2},{35,3},{36,4},{37,5},{38,6},{39,7},{40,8},{41... | collective-permute-start | bytes 614408 | tf_op jit(solution)/shard_map/ppermute | solution.py:349
  75.4 1.4 %collective-permute-done.11.passed = f32[192,256]{1,0:T(8,128)S(1)} collective-permute-done((f32[192,256]{1,0:T(8,128)S(1)}, f32[192,256]{1,0:T(8,128)S(1)}, u32[]{:S(2)}, u32[]{:S(2)}) %collective-permute-start.11) | collective-permute-done | bytes 196640 | tf_op jit(solution)/shard_map/ppermute | solution.py:337
  76.8 12.7 %collective-permute-done.10.got = f32[200,256]{1,0:T(8,128)S(1)} collective-permute-done((f32[200,256]{1,0:T(8,128)S(1)}, f32[200,256]{1,0:T(8,128)S(1)}, u32[]{:S(2)}, u32[]{:S(2)}) %collective-permute-start.10) | collective-permute-done | bytes 204832 | tf_op jit(solution)/shard_map/ppermute | solution.py:349
  89.7 1.3 %collective-permute-start.12 = (f32[200,256]{1,0:T(8,128)S(1)}, f32[200,256]{1,0:T(8,128)S(1)}, u32[]{:S(2)}, u32[]{:S(2)}) collective-permute-start(f32[200,256]{1,0:T(8,128)S(1)} %shard_map.65.mine), channel_id=1, source_target_pairs={{64,0},{65,1},{66,2},{67,3},{68,4},{69,5},{70,6},{71,7},{72,8},{73... | collective-permute-start | bytes 614408 | tf_op jit(solution)/shard_map/ppermute | solution.py:349
  91.0 0.5 collective-permute-start.13
  91.6 1.0 collective-permute-done.13.passed
  92.7 6.4 %collective-permute-done.12.got = f32[200,256]{1,0:T(8,128)S(1)} collective-permute-done((f32[200,256]{1,0:T(8,128)S(1)}, f32[200,256]{1,0:T(8,128)S(1)}, u32[]{:S(2)}, u32[]{:S(2)}) %collective-permute-start.12) | collective-permute-done | bytes 204832 | tf_op jit(solution)/shard_map/ppermute | solution.py:349
  99.6 0.7 collective-permute-start.14
  100.2 1.3 %collective-permute-start.15 = (f32[136,256]{1,0:T(8,128)S(1)}, f32[136,256]{1,0:T(8,128)S(1)}, u32[]{:S(2)}, u32[]{:S(2)}) collective-permute-start(f32[136,256]{1,0:T(8,128)S(1)} %slice.86), channel_id=1, source_target_pairs={{129,0},{131,2},{133,4},{135,6},{137,8},{139,10},{141,12},{143,14}... | collective-permute-start | bytes 417800 | tf_op jit(solution)/shard_map/ppermute | solution.py:365
  101.6 1.3 %shard_map.67 = (f32[256,256]{1,0:T(8,128)S(1)}, f32[264,256]{1,0:T(8,128)S(1)}, f32[256,256]{1,0:T(8,128)S(1)}, f32[264,256]{1,0:T(8,128)S(1)}) custom-call(s32[1]{0:T(128)} %bitcast.core, f32[200,256]{1,0:T(8,128)S(1)} %shard_map.66.mine, f32[200,256]{1,0:T(8,128)S(1)} %collective-permute-done.16.passed, f32[256,256]{1,0:T(8,128)S(1)} %convolution_select_fusion.1.turned0, ...), custom_call_target="tpu_custom_call" | custom-call | tf_op jit(solution)/shard_map/pallas_call | solution.py:293
  102.9 6.0 %collective-permute-done.15.to_first = f32[136,256]{1,0:T(8,128)S(1)} collective-permute-done((f32[136,256]{1,0:T(8,128)S(1)}, f32[136,256]{1,0:T(8,128)S(1)}, u32[]{:S(2)}, u32[]{:S(2)}) %collective-permute-start.15) | collective-permute-done | bytes 139296 | tf_op jit(solution)/shard_map/ppermute | solution.py:365
  108.9 2.6 %shard_map.68 = (f32[2,256,256]{2,1,0:T(8,128)}, f32[2,256]{1,0:T(2,128)}) custom-call(f32[136,256]{1,0:T(8,128)S(1)} %collective-permute-done.14.to_second, f32[136,256]{1,0:T(8,128)S(1)} %collective-permute-done.15.to_first, f32[256,256]{1,0:T(8,128)S(1)} %get-tuple-element.14.turned0, f32[264,256]{1,0:T(8,128)S(1)} %get-tuple-element.15.held0, ...), custom_call_target="tpu_custom_call" | custom-call | tf_op jit(solution)/shard_map/pallas_call | solution.py:293
  (28 shorter events, 3.3 us)
Async XLA Ops:
  15.2 2.0 %collective-permute-start = (f32[520,256]{1,0:T(8,128)S(1)}, f32[520,256]{1,0:T(8,128)S(1)}, u32[]{:S(2)}, u32[]{:S(2)}) collective-permute-start(f32[520,256]{1,0:T(8,128)S(1)} %get-tuple-element.11.own), channel_id=1, source_target_pairs={{0,1},{1,0},{2,3},{3,2},{4,5},{5,4},{6,7},{7,6},{8,9},{9,8},{10,11... | collective-permute-start | bytes 1597448 | tf_op jit(solution)/shard_map/ppermute | solution.py:337
  17.7 9.8 %collective-permute-start.2 = (f32[200,256]{1,0:T(8,128)S(1)}, f32[200,256]{1,0:T(8,128)S(1)}, u32[]{:S(2)}, u32[]{:S(2)}) collective-permute-start(f32[200,256]{1,0:T(8,128)S(1)} %shard_map.60), channel_id=1, source_target_pairs={{2,0},{3,1},{4,2},{5,3},{6,4},{7,5},{8,6},{9,7},{10,8},{11,9},{12,... | collective-permute-start | bytes 614408 | tf_op jit(solution)/shard_map/ppermute | solution.py:349
  20.0 15.7 %collective-permute-start.1 = (f32[200,256]{1,0:T(8,128)S(1)}, f32[200,256]{1,0:T(8,128)S(1)}, u32[]{:S(2)}, u32[]{:S(2)}) collective-permute-start(f32[200,256]{1,0:T(8,128)S(1)} %shard_map.60), channel_id=1, source_target_pairs={{4,0},{5,1},{6,2},{7,3},{8,4},{9,5},{10,6},{11,7},{12,8},{13,9},{1... | collective-permute-start | bytes 614408 | tf_op jit(solution)/shard_map/ppermute | solution.py:349
  27.5 8.3 %collective-permute-start.3 = (f32[192,256]{1,0:T(8,128)S(1)}, f32[192,256]{1,0:T(8,128)S(1)}, u32[]{:S(2)}, u32[]{:S(2)}) collective-permute-start(f32[192,256]{1,0:T(8,128)S(1)} %slice.80), channel_id=1, source_target_pairs={{0,1},{1,0},{2,3},{3,2},{4,5},{5,4},{6,7},{7,6},{8,9},{9,8},{10,11... | collective-permute-start | bytes 589832 | tf_op jit(solution)/shard_map/ppermute | solution.py:337
  36.1 13.3 %collective-permute-start.4 = (f32[200,256]{1,0:T(8,128)S(1)}, f32[200,256]{1,0:T(8,128)S(1)}, u32[]{:S(2)}, u32[]{:S(2)}) collective-permute-start(f32[200,256]{1,0:T(8,128)S(1)} %shard_map.61.mine), channel_id=1, source_target_pairs={{4,0},{5,1},{6,2},{7,3},{8,4},{9,5},{10,6},{11,7},{12,8},{13,9},{1... | collective-permute-start | bytes 614408 | tf_op jit(solution)/shard_map/ppermute | solution.py:349
  38.0 1.5 %collective-permute-start.5 = (f32[192,256]{1,0:T(8,128)S(1)}, f32[192,256]{1,0:T(8,128)S(1)}, u32[]{:S(2)}, u32[]{:S(2)}) collective-permute-start(f32[192,256]{1,0:T(8,128)S(1)} %slice.81), channel_id=1, source_target_pairs={{0,1},{1,0},{2,3},{3,2},{4,5},{5,4},{6,7},{7,6},{8,9},{9,8},{10,11... | collective-permute-start | bytes 589832 | tf_op jit(solution)/shard_map/ppermute | solution.py:337
  49.7 10.5 %collective-permute-start.6 = (f32[200,256]{1,0:T(8,128)S(1)}, f32[200,256]{1,0:T(8,128)S(1)}, u32[]{:S(2)}, u32[]{:S(2)}) collective-permute-start(f32[200,256]{1,0:T(8,128)S(1)} %shard_map.62.mine), channel_id=1, source_target_pairs={{8,0},{9,1},{10,2},{11,3},{12,4},{13,5},{14,6},{15,7},{16,8},{17,9... | collective-permute-start | bytes 614408 | tf_op jit(solution)/shard_map/ppermute | solution.py:349
  51.6 1.5 %collective-permute-start.7 = (f32[192,256]{1,0:T(8,128)S(1)}, f32[192,256]{1,0:T(8,128)S(1)}, u32[]{:S(2)}, u32[]{:S(2)}) collective-permute-start(f32[192,256]{1,0:T(8,128)S(1)} %slice.82), channel_id=1, source_target_pairs={{0,1},{1,0},{2,3},{3,2},{4,5},{5,4},{6,7},{7,6},{8,9},{9,8},{10,11... | collective-permute-start | bytes 589832 | tf_op jit(solution)/shard_map/ppermute | solution.py:337
  60.5 12.6 %collective-permute-start.8 = (f32[200,256]{1,0:T(8,128)S(1)}, f32[200,256]{1,0:T(8,128)S(1)}, u32[]{:S(2)}, u32[]{:S(2)}) collective-permute-start(f32[200,256]{1,0:T(8,128)S(1)} %shard_map.63.mine), channel_id=1, source_target_pairs={{16,0},{17,1},{18,2},{19,3},{20,4},{21,5},{22,6},{23,7},{24,8},{25... | collective-permute-start | bytes 614408 | tf_op jit(solution)/shard_map/ppermute | solution.py:349
  62.4 1.5 %collective-permute-start.9 = (f32[192,256]{1,0:T(8,128)S(1)}, f32[192,256]{1,0:T(8,128)S(1)}, u32[]{:S(2)}, u32[]{:S(2)}) collective-permute-start(f32[192,256]{1,0:T(8,128)S(1)} %slice.83), channel_id=1, source_target_pairs={{0,1},{1,0},{2,3},{3,2},{4,5},{5,4},{6,7},{7,6},{8,9},{9,8},{10,11... | collective-permute-start | bytes 589832 | tf_op jit(solution)/shard_map/ppermute | solution.py:337
  73.3 16.1 %collective-permute-start.10 = (f32[200,256]{1,0:T(8,128)S(1)}, f32[200,256]{1,0:T(8,128)S(1)}, u32[]{:S(2)}, u32[]{:S(2)}) collective-permute-start(f32[200,256]{1,0:T(8,128)S(1)} %shard_map.64.mine), channel_id=1, source_target_pairs={{32,0},{33,1},{34,2},{35,3},{36,4},{37,5},{38,6},{39,7},{40,8},{41... | collective-permute-start | bytes 614408 | tf_op jit(solution)/shard_map/ppermute | solution.py:349
  75.3 1.5 %collective-permute-start.11 = (f32[192,256]{1,0:T(8,128)S(1)}, f32[192,256]{1,0:T(8,128)S(1)}, u32[]{:S(2)}, u32[]{:S(2)}) collective-permute-start(f32[192,256]{1,0:T(8,128)S(1)} %slice.84), channel_id=1, source_target_pairs={{0,1},{1,0},{2,3},{3,2},{4,5},{5,4},{6,7},{7,6},{8,9},{9,8},{10,11... | collective-permute-start | bytes 589832 | tf_op jit(solution)/shard_map/ppermute | solution.py:337
  89.7 9.3 %collective-permute-start.12 = (f32[200,256]{1,0:T(8,128)S(1)}, f32[200,256]{1,0:T(8,128)S(1)}, u32[]{:S(2)}, u32[]{:S(2)}) collective-permute-start(f32[200,256]{1,0:T(8,128)S(1)} %shard_map.65.mine), channel_id=1, source_target_pairs={{64,0},{65,1},{66,2},{67,3},{68,4},{69,5},{70,6},{71,7},{72,8},{73... | collective-permute-start | bytes 614408 | tf_op jit(solution)/shard_map/ppermute | solution.py:349
  91.0 1.6 %collective-permute-start.13 = (f32[192,256]{1,0:T(8,128)S(1)}, f32[192,256]{1,0:T(8,128)S(1)}, u32[]{:S(2)}, u32[]{:S(2)}) collective-permute-start(f32[192,256]{1,0:T(8,128)S(1)} %slice.85), channel_id=1, source_target_pairs={{0,1},{1,0},{2,3},{3,2},{4,5},{5,4},{6,7},{7,6},{8,9},{9,8},{10,11... | collective-permute-start | bytes 589832 | tf_op jit(solution)/shard_map/ppermute | solution.py:337
  99.3 2.2 %collective-permute-start.16 = (f32[200,256]{1,0:T(8,128)S(1)}, f32[200,256]{1,0:T(8,128)S(1)}, u32[]{:S(2)}, u32[]{:S(2)}) collective-permute-start(f32[200,256]{1,0:T(8,128)S(1)} %shard_map.66.mine), channel_id=1, source_target_pairs={{0,1},{1,0},{2,3},{3,2},{4,5},{5,4},{6,7},{7,6},{8,9},{9,8},{10,11... | collective-permute-start | bytes 614408 | tf_op jit(solution)/shard_map/ppermute | solution.py:337
  99.6 3.3 %collective-permute-start.14 = (f32[136,256]{1,0:T(8,128)S(1)}, f32[136,256]{1,0:T(8,128)S(1)}, u32[]{:S(2)}, u32[]{:S(2)}) collective-permute-start(f32[136,256]{1,0:T(8,128)S(1)} %slice.86), channel_id=1, source_target_pairs={{129,1},{131,3},{133,5},{135,7},{137,9},{139,11},{141,13},{143,15}... | collective-permute-start | bytes 417800 | tf_op jit(solution)/shard_map/ppermute | solution.py:365
  100.2 8.7 %collective-permute-start.15 = (f32[136,256]{1,0:T(8,128)S(1)}, f32[136,256]{1,0:T(8,128)S(1)}, u32[]{:S(2)}, u32[]{:S(2)}) collective-permute-start(f32[136,256]{1,0:T(8,128)S(1)} %slice.86), channel_id=1, source_target_pairs={{129,0},{131,2},{133,4},{135,6},{137,8},{139,10},{141,12},{143,14}... | collective-permute-start | bytes 417800 | tf_op jit(solution)/shard_map/ppermute | solution.py:365

commit v7 on v6

--- a/solution.py
+++ b/solution.py
@@ -24,26 +24,23 @@
     def spread(row):
         return jnp.broadcast_to(row, (8, HALF))
 
-    for q in range(BASE // 8):
-        cols = []
+    cols = [[[spread(t[:, base + j : base + j + 1]) for t in tiles[m]] for j in range(BASE)] for m in range(2)]
+    for k in range(BASE):
+        q, o = divmod(k, 8)
+        here = lane == base + k
+        unit = jnp.where(sub == o, 1.0, 0.0)
         for m in range(2):
-            at = base + 8 * q
-            cols.append([[spread(t[:, at + j : at + j + 1]) for t in tiles[m]] for j in range(8)])
-        for k in range(8):
-            here = lane == base + 8 * q + k
-            unit = jnp.where(sub == k, 1.0, 0.0)
-            for m in range(2):
-                col, tile = cols[m], tiles[m]
-                ratio = 1.0 / (spread(col[k][q][k : k + 1]))
-                scaled = jnp.where(here, ratio, spread(tile[q][k : k + 1]) * ratio)
-                factors = [spread(col[j][q][k : k + 1]) * ratio for j in range(k + 1, 8)]
-                down = list(col[k])
-                down[q] = down[q] - unit
-                for i in range(BASE // 8):
-                    old = jnp.where(here, unit if i == q else 0.0, tile[i])
-                    tile[i] = old - down[i] * scaled
-                for j, f in zip(range(k + 1, 8), factors):
-                    col[j] = [c - d * f for c, d in zip(col[j], down)]
+            col, tile = cols[m], tiles[m]
+            ratio = 1.0 / spread(col[k][q][o : o + 1])
+            scaled = jnp.where(here, ratio, spread(tile[q][o : o + 1]) * ratio)
+            down = list(col[k])
+            down[q] = down[q] - unit
+            for j in range(k + 1, BASE):
+                f = spread(col[j][q][o : o + 1]) * ratio
+                col[j] = [c - d * f for c, d in zip(col[j], down)]
+            for i in range(BASE // 8):
+                old = jnp.where(here, unit if i == q else 0.0, tile[i])
+                tile[i] = old - down[i] * scaled
     return [jnp.concatenate(t, axis=0) for t in tiles]
 
 
@@ -350,8 +347,9 @@
             rows, AXES, [(2 * (c + stride) + k, 2 * c + k) for c in range(chips - stride) for k in cores]
         )
 
-    mine = fetched(chip, 1, (0, 1))
     got = fetched(chip, 2, (0, 1))
+    nearer, late[1] = lax.optimization_barrier((chip, late[1]))
+    mine = fetched(nearer, 1, (0, 1))
     stride = 2
     passed = swapped(mine[:TOP])
     mine = call(join_kernel, [(PART, NS)], which, got, mine, passed)

time: 112 us -> 116 us (1.036)
  the two profiles are of different devices: /device:TPU:240 before, /device:TPU:250 now
where the time goes in v7:
time: 116 us
  waiting for transfers between devices  73.2 us (63%)
  Pallas kernels  19.4 us (17%)
  starting transfers between devices  19.3 us (17%)
  matrix products  2.73 us (2%)
    ppermute x7, waiting for transfers between devices, fetched(): lax.ppermute(rows, AXES, [(2 * (c + stride) + k, 2 * c + k) for c in rang...  59.5 us
    pallas_call x10, Pallas kernels, call(): pl.pallas_call(kernel, out_shape=outs, in_specs=[smem] * len(scalars) + [...  19.4 us
    ppermute x7, starting transfers between devices, fetched(): lax.ppermute(rows, AXES, [(2 * (c + stride) + k, 2 * c + k) for c in rang...  15.6 us
    ppermute x8, waiting for transfers between devices, swapped(): return lax.ppermute(rows, AXES, swap)  7.57 us
    ppermute x2, waiting for transfers between devices, local(): lax.ppermute(tails, AXES, [(2 * (c + stride) + 1, 2 * c + k) for c in ran...  6.15 us
    dot_general x6, matrix products, product(): return jnp.matmul(left, right, precision=lax.Precision.HIGHEST)  2.73 us
  transfers between devices with their start and end apart: 17, of which 14 were waited for; matrix products, arithmetic and copies ran while one was open for 2% of the time, Pallas kernels for 1%

profile of v7, /device:TPU:250, one launch (start us, length us, event | category | flops | bytes accessed | tf_op | source)
XLA Modules:
  0.0 116.0 jit_solution(3716018636483195333)
XLA Ops:
  0.6 13.7 %shard_map.59 = (f32[520,256]{1,0:T(8,128)S(1)}, f32[256,256]{1,0:T(8,128)S(1)}, f32[264,256]{1,0:T(8,128)S(1)}) custom-call(s32[1]{0:T(128)} %bitcast.1.final, f32[2,256]{1,0:T(2,128)} %mean_in.1, f32[2,256,256]{2,1,0:T(8,128)} %cov_in.1, f32[2,256,256]{2,1,0:T(8,128)} %noise_in.1, f32[256,256]{1,0:T(8,128)} %step_in.1), custom_call_target="tpu_custom_call" | custom-call | tf_op jit(solution)/shard_map/pallas_call | solution.py:290
  14.5 1.9 %collective-permute-done.other = f32[520,256]{1,0:T(8,128)S(1)} collective-permute-done((f32[520,256]{1,0:T(8,128)S(1)}, f32[520,256]{1,0:T(8,128)S(1)}, u32[]{:S(2)}, u32[]{:S(2)}) %collective-permute-start) | collective-permute-done | bytes 532512 | tf_op jit(solution)/shard_map/ppermute | solution.py:334
  16.6 3.1 %collective-permute-start.1 = (f32[200,256]{1,0:T(8,128)S(1)}, f32[200,256]{1,0:T(8,128)S(1)}, u32[]{:S(2)}, u32[]{:S(2)}) collective-permute-start(f32[200,256]{1,0:T(8,128)S(1)} %shard_map.60), channel_id=1, source_target_pairs={{4,0},{5,1},{6,2},{7,3},{8,4},{9,5},{10,6},{11,7},{12,8},{13,9},{1... | collective-permute-start | bytes 614408 | tf_op jit(solution)/shard_map/ppermute | solution.py:346
  19.8 0.4 convolution_select_fusion.1.turned1
  20.2 1.9 %collective-permute-start.2 = (f32[200,256]{1,0:T(8,128)S(1)}, f32[200,256]{1,0:T(8,128)S(1)}, u32[]{:S(2)}, u32[]{:S(2)}) collective-permute-start(f32[200,256]{1,0:T(8,128)S(1)} %shard_map.60), channel_id=1, source_target_pairs={{2,0},{3,1},{4,2},{5,3},{6,4},{7,5},{8,6},{9,7},{10,8},{11,9},{12,... | collective-permute-start | bytes 614408 | tf_op jit(solution)/shard_map/ppermute | solution.py:346
  22.1 0.4 fusion.2
  22.5 12.6 %collective-permute-done.2.mine = f32[200,256]{1,0:T(8,128)S(1)} collective-permute-done((f32[200,256]{1,0:T(8,128)S(1)}, f32[200,256]{1,0:T(8,128)S(1)}, u32[]{:S(2)}, u32[]{:S(2)}) %collective-permute-start.2) | collective-permute-done | bytes 204832 | tf_op jit(solution)/shard_map/ppermute | solution.py:346
  35.2 0.6 convolution_add_fusion
  35.8 0.8 collective-permute-done.3.passed
  36.9 1.9 %collective-permute-start.4 = (f32[200,256]{1,0:T(8,128)S(1)}, f32[200,256]{1,0:T(8,128)S(1)}, u32[]{:S(2)}, u32[]{:S(2)}) collective-permute-start(f32[200,256]{1,0:T(8,128)S(1)} %shard_map.61.mine), channel_id=1, source_target_pairs={{4,0},{5,1},{6,2},{7,3},{8,4},{9,5},{10,6},{11,7},{12,8},{13,9},{1... | collective-permute-start | bytes 614408 | tf_op jit(solution)/shard_map/ppermute | solution.py:346
  38.8 0.7 collective-permute-start.5
  39.5 0.4 fusion.4
  39.9 0.7 collective-permute-done.5.passed
  40.6 10.3 %collective-permute-done.4.got = f32[200,256]{1,0:T(8,128)S(1)} collective-permute-done((f32[200,256]{1,0:T(8,128)S(1)}, f32[200,256]{1,0:T(8,128)S(1)}, u32[]{:S(2)}, u32[]{:S(2)}) %collective-permute-start.4) | collective-permute-done | bytes 204832 | tf_op jit(solution)/shard_map/ppermute | solution.py:346
  51.1 1.9 %collective-permute-start.6 = (f32[200,256]{1,0:T(8,128)S(1)}, f32[200,256]{1,0:T(8,128)S(1)}, u32[]{:S(2)}, u32[]{:S(2)}) collective-permute-start(f32[200,256]{1,0:T(8,128)S(1)} %shard_map.62.mine), channel_id=1, source_target_pairs={{8,0},{9,1},{10,2},{11,3},{12,4},{13,5},{14,6},{15,7},{16,8},{17,9... | collective-permute-start | bytes 614408 | tf_op jit(solution)/shard_map/ppermute | solution.py:346
  53.4 0.6 convolution_add_fusion.1
  54.0 0.6 collective-permute-done.7.passed
  54.6 7.8 %collective-permute-done.6.got = f32[200,256]{1,0:T(8,128)S(1)} collective-permute-done((f32[200,256]{1,0:T(8,128)S(1)}, f32[200,256]{1,0:T(8,128)S(1)}, u32[]{:S(2)}, u32[]{:S(2)}) %collective-permute-start.6) | collective-permute-done | bytes 204832 | tf_op jit(solution)/shard_map/ppermute | solution.py:346
  62.7 1.9 %collective-permute-start.8 = (f32[200,256]{1,0:T(8,128)S(1)}, f32[200,256]{1,0:T(8,128)S(1)}, u32[]{:S(2)}, u32[]{:S(2)}) collective-permute-start(f32[200,256]{1,0:T(8,128)S(1)} %shard_map.63.mine), channel_id=1, source_target_pairs={{16,0},{17,1},{18,2},{19,3},{20,4},{21,5},{22,6},{23,7},{24,8},{25... | collective-permute-start | bytes 614408 | tf_op jit(solution)/shard_map/ppermute | solution.py:346
  65.1 1.0 collective-permute-done.9.passed
  66.1 10.0 %collective-permute-done.8.got = f32[200,256]{1,0:T(8,128)S(1)} collective-permute-done((f32[200,256]{1,0:T(8,128)S(1)}, f32[200,256]{1,0:T(8,128)S(1)}, u32[]{:S(2)}, u32[]{:S(2)}) %collective-permute-start.8) | collective-permute-done | bytes 204832 | tf_op jit(solution)/shard_map/ppermute | solution.py:346
  76.5 2.4 %collective-permute-start.10 = (f32[200,256]{1,0:T(8,128)S(1)}, f32[200,256]{1,0:T(8,128)S(1)}, u32[]{:S(2)}, u32[]{:S(2)}) collective-permute-start(f32[200,256]{1,0:T(8,128)S(1)} %shard_map.64.mine), channel_id=1, source_target_pairs={{32,0},{33,1},{34,2},{35,3},{36,4},{37,5},{38,6},{39,7},{40,8},{41... | collective-permute-start | bytes 614408 | tf_op jit(solution)/shard_map/ppermute | solution.py:346
  79.0 1.4 %collective-permute-done.11.passed = f32[192,256]{1,0:T(8,128)S(1)} collective-permute-done((f32[192,256]{1,0:T(8,128)S(1)}, f32[192,256]{1,0:T(8,128)S(1)}, u32[]{:S(2)}, u32[]{:S(2)}) %collective-permute-start.11) | collective-permute-done | bytes 196640 | tf_op jit(solution)/shard_map/ppermute | solution.py:334
  80.4 12.8 %collective-permute-done.10.got = f32[200,256]{1,0:T(8,128)S(1)} collective-permute-done((f32[200,256]{1,0:T(8,128)S(1)}, f32[200,256]{1,0:T(8,128)S(1)}, u32[]{:S(2)}, u32[]{:S(2)}) %collective-permute-start.10) | collective-permute-done | bytes 204832 | tf_op jit(solution)/shard_map/ppermute | solution.py:346
  93.5 2.3 %collective-permute-start.12 = (f32[200,256]{1,0:T(8,128)S(1)}, f32[200,256]{1,0:T(8,128)S(1)}, u32[]{:S(2)}, u32[]{:S(2)}) collective-permute-start(f32[200,256]{1,0:T(8,128)S(1)} %shard_map.65.mine), channel_id=1, source_target_pairs={{64,0},{65,1},{66,2},{67,3},{68,4},{69,5},{70,6},{71,7},{72,8},{73... | collective-permute-start | bytes 614408 | tf_op jit(solution)/shard_map/ppermute | solution.py:346
  96.2 1.2 %collective-permute-done.13.passed = f32[192,256]{1,0:T(8,128)S(1)} collective-permute-done((f32[192,256]{1,0:T(8,128)S(1)}, f32[192,256]{1,0:T(8,128)S(1)}, u32[]{:S(2)}, u32[]{:S(2)}) %collective-permute-start.13) | collective-permute-done | bytes 196640 | tf_op jit(solution)/shard_map/ppermute | solution.py:334
  97.4 6.0 %collective-permute-done.12.got = f32[200,256]{1,0:T(8,128)S(1)} collective-permute-done((f32[200,256]{1,0:T(8,128)S(1)}, f32[200,256]{1,0:T(8,128)S(1)}, u32[]{:S(2)}, u32[]{:S(2)}) %collective-permute-start.12) | collective-permute-done | bytes 204832 | tf_op jit(solution)/shard_map/ppermute | solution.py:346
  103.8 0.7 collective-permute-start.14
  104.5 1.3 %collective-permute-start.15 = (f32[136,256]{1,0:T(8,128)S(1)}, f32[136,256]{1,0:T(8,128)S(1)}, u32[]{:S(2)}, u32[]{:S(2)}) collective-permute-start(f32[136,256]{1,0:T(8,128)S(1)} %slice.87), channel_id=1, source_target_pairs={{129,0},{131,2},{133,4},{135,6},{137,8},{139,10},{141,12},{143,14}... | collective-permute-start | bytes 417800 | tf_op jit(solution)/shard_map/ppermute | solution.py:363
  105.8 1.3 %shard_map.67 = (f32[256,256]{1,0:T(8,128)S(1)}, f32[264,256]{1,0:T(8,128)S(1)}, f32[256,256]{1,0:T(8,128)S(1)}, f32[264,256]{1,0:T(8,128)S(1)}) custom-call(s32[1]{0:T(128)} %bitcast.core, f32[200,256]{1,0:T(8,128)S(1)} %shard_map.66.mine, f32[200,256]{1,0:T(8,128)S(1)} %collective-permute-done.16.passed, f32[256,256]{1,0:T(8,128)S(1)} %convolution_select_fusion.turned0, ...), custom_call_target="tpu_custom_call" | custom-call | tf_op jit(solution)/shard_map/pallas_call | solution.py:290
  107.1 6.1 %collective-permute-done.15.to_first = f32[136,256]{1,0:T(8,128)S(1)} collective-permute-done((f32[136,256]{1,0:T(8,128)S(1)}, f32[136,256]{1,0:T(8,128)S(1)}, u32[]{:S(2)}, u32[]{:S(2)}) %collective-permute-start.15) | collective-permute-done | bytes 139296 | tf_op jit(solution)/shard_map/ppermute | solution.py:363
  113.3 2.6 %shard_map.68 = (f32[2,256,256]{2,1,0:T(8,128)}, f32[2,256]{1,0:T(2,128)}) custom-call(f32[136,256]{1,0:T(8,128)S(1)} %collective-permute-done.14.to_second, f32[136,256]{1,0:T(8,128)S(1)} %collective-permute-done.15.to_first, f32[256,256]{1,0:T(8,128)S(1)} %get-tuple-element.18.turned0, f32[264,256]{1,0:T(8,128)S(1)} %get-tuple-element.19.held0, ...), custom_call_target="tpu_custom_call" | custom-call | tf_op jit(solution)/shard_map/pallas_call | solution.py:290
  (28 shorter events, 3.5 us)
Async XLA Ops:
  14.3 2.0 %collective-permute-start = (f32[520,256]{1,0:T(8,128)S(1)}, f32[520,256]{1,0:T(8,128)S(1)}, u32[]{:S(2)}, u32[]{:S(2)}) collective-permute-start(f32[520,256]{1,0:T(8,128)S(1)} %get-tuple-element.13.own), channel_id=1, source_target_pairs={{0,1},{1,0},{2,3},{3,2},{4,5},{5,4},{6,7},{7,6},{8,9},{9,8},{10,11... | collective-permute-start | bytes 1597448 | tf_op jit(solution)/shard_map/ppermute | solution.py:334
  16.6 19.1 %collective-permute-start.1 = (f32[200,256]{1,0:T(8,128)S(1)}, f32[200,256]{1,0:T(8,128)S(1)}, u32[]{:S(2)}, u32[]{:S(2)}) collective-permute-start(f32[200,256]{1,0:T(8,128)S(1)} %shard_map.60), channel_id=1, source_target_pairs={{4,0},{5,1},{6,2},{7,3},{8,4},{9,5},{10,6},{11,7},{12,8},{13,9},{1... | collective-permute-start | bytes 614408 | tf_op jit(solution)/shard_map/ppermute | solution.py:346
  20.2 14.9 %collective-permute-start.2 = (f32[200,256]{1,0:T(8,128)S(1)}, f32[200,256]{1,0:T(8,128)S(1)}, u32[]{:S(2)}, u32[]{:S(2)}) collective-permute-start(f32[200,256]{1,0:T(8,128)S(1)} %shard_map.60), channel_id=1, source_target_pairs={{2,0},{3,1},{4,2},{5,3},{6,4},{7,5},{8,6},{9,7},{10,8},{11,9},{12,... | collective-permute-start | bytes 614408 | tf_op jit(solution)/shard_map/ppermute | solution.py:346
  35.1 1.5 %collective-permute-start.3 = (f32[192,256]{1,0:T(8,128)S(1)}, f32[192,256]{1,0:T(8,128)S(1)}, u32[]{:S(2)}, u32[]{:S(2)}) collective-permute-start(f32[192,256]{1,0:T(8,128)S(1)} %slice.81), channel_id=1, source_target_pairs={{0,1},{1,0},{2,3},{3,2},{4,5},{5,4},{6,7},{7,6},{8,9},{9,8},{10,11... | collective-permute-start | bytes 589832 | tf_op jit(solution)/shard_map/ppermute | solution.py:334
  36.9 14.0 %collective-permute-start.4 = (f32[200,256]{1,0:T(8,128)S(1)}, f32[200,256]{1,0:T(8,128)S(1)}, u32[]{:S(2)}, u32[]{:S(2)}) collective-permute-start(f32[200,256]{1,0:T(8,128)S(1)} %shard_map.61.mine), channel_id=1, source_target_pairs={{4,0},{5,1},{6,2},{7,3},{8,4},{9,5},{10,6},{11,7},{12,8},{13,9},{1... | collective-permute-start | bytes 614408 | tf_op jit(solution)/shard_map/ppermute | solution.py:346
  38.8 1.7 %collective-permute-start.5 = (f32[192,256]{1,0:T(8,128)S(1)}, f32[192,256]{1,0:T(8,128)S(1)}, u32[]{:S(2)}, u32[]{:S(2)}) collective-permute-start(f32[192,256]{1,0:T(8,128)S(1)} %slice.82), channel_id=1, source_target_pairs={{0,1},{1,0},{2,3},{3,2},{4,5},{5,4},{6,7},{7,6},{8,9},{9,8},{10,11... | collective-permute-start | bytes 589832 | tf_op jit(solution)/shard_map/ppermute | solution.py:334
  51.1 11.3 %collective-permute-start.6 = (f32[200,256]{1,0:T(8,128)S(1)}, f32[200,256]{1,0:T(8,128)S(1)}, u32[]{:S(2)}, u32[]{:S(2)}) collective-permute-start(f32[200,256]{1,0:T(8,128)S(1)} %shard_map.62.mine), channel_id=1, source_target_pairs={{8,0},{9,1},{10,2},{11,3},{12,4},{13,5},{14,6},{15,7},{16,8},{17,9... | collective-permute-start | bytes 614408 | tf_op jit(solution)/shard_map/ppermute | solution.py:346
  53.1 1.5 %collective-permute-start.7 = (f32[192,256]{1,0:T(8,128)S(1)}, f32[192,256]{1,0:T(8,128)S(1)}, u32[]{:S(2)}, u32[]{:S(2)}) collective-permute-start(f32[192,256]{1,0:T(8,128)S(1)} %slice.83), channel_id=1, source_target_pairs={{0,1},{1,0},{2,3},{3,2},{4,5},{5,4},{6,7},{7,6},{8,9},{9,8},{10,11... | collective-permute-start | bytes 589832 | tf_op jit(solution)/shard_map/ppermute | solution.py:334
  62.7 13.5 %collective-permute-start.8 = (f32[200,256]{1,0:T(8,128)S(1)}, f32[200,256]{1,0:T(8,128)S(1)}, u32[]{:S(2)}, u32[]{:S(2)}) collective-permute-start(f32[200,256]{1,0:T(8,128)S(1)} %shard_map.63.mine), channel_id=1, source_target_pairs={{16,0},{17,1},{18,2},{19,3},{20,4},{21,5},{22,6},{23,7},{24,8},{25... | collective-permute-start | bytes 614408 | tf_op jit(solution)/shard_map/ppermute | solution.py:346
  64.6 1.5 %collective-permute-start.9 = (f32[192,256]{1,0:T(8,128)S(1)}, f32[192,256]{1,0:T(8,128)S(1)}, u32[]{:S(2)}, u32[]{:S(2)}) collective-permute-start(f32[192,256]{1,0:T(8,128)S(1)} %slice.84), channel_id=1, source_target_pairs={{0,1},{1,0},{2,3},{3,2},{4,5},{5,4},{6,7},{7,6},{8,9},{9,8},{10,11... | collective-permute-start | bytes 589832 | tf_op jit(solution)/shard_map/ppermute | solution.py:334
  76.5 16.8 %collective-permute-start.10 = (f32[200,256]{1,0:T(8,128)S(1)}, f32[200,256]{1,0:T(8,128)S(1)}, u32[]{:S(2)}, u32[]{:S(2)}) collective-permute-start(f32[200,256]{1,0:T(8,128)S(1)} %shard_map.64.mine), channel_id=1, source_target_pairs={{32,0},{33,1},{34,2},{35,3},{36,4},{37,5},{38,6},{39,7},{40,8},{41... | collective-permute-start | bytes 614408 | tf_op jit(solution)/shard_map/ppermute | solution.py:346
  78.9 1.5 %collective-permute-start.11 = (f32[192,256]{1,0:T(8,128)S(1)}, f32[192,256]{1,0:T(8,128)S(1)}, u32[]{:S(2)}, u32[]{:S(2)}) collective-permute-start(f32[192,256]{1,0:T(8,128)S(1)} %slice.85), channel_id=1, source_target_pairs={{0,1},{1,0},{2,3},{3,2},{4,5},{5,4},{6,7},{7,6},{8,9},{9,8},{10,11... | collective-permute-start | bytes 589832 | tf_op jit(solution)/shard_map/ppermute | solution.py:334
  93.5 9.9 %collective-permute-start.12 = (f32[200,256]{1,0:T(8,128)S(1)}, f32[200,256]{1,0:T(8,128)S(1)}, u32[]{:S(2)}, u32[]{:S(2)}) collective-permute-start(f32[200,256]{1,0:T(8,128)S(1)} %shard_map.65.mine), channel_id=1, source_target_pairs={{64,0},{65,1},{66,2},{67,3},{68,4},{69,5},{70,6},{71,7},{72,8},{73... | collective-permute-start | bytes 614408 | tf_op jit(solution)/shard_map/ppermute | solution.py:346
  95.8 1.5 %collective-permute-start.13 = (f32[192,256]{1,0:T(8,128)S(1)}, f32[192,256]{1,0:T(8,128)S(1)}, u32[]{:S(2)}, u32[]{:S(2)}) collective-permute-start(f32[192,256]{1,0:T(8,128)S(1)} %slice.86), channel_id=1, source_target_pairs={{0,1},{1,0},{2,3},{3,2},{4,5},{5,4},{6,7},{7,6},{8,9},{9,8},{10,11... | collective-permute-start | bytes 589832 | tf_op jit(solution)/shard_map/ppermute | solution.py:334
  103.7 2.1 %collective-permute-start.16 = (f32[200,256]{1,0:T(8,128)S(1)}, f32[200,256]{1,0:T(8,128)S(1)}, u32[]{:S(2)}, u32[]{:S(2)}) collective-permute-start(f32[200,256]{1,0:T(8,128)S(1)} %shard_map.66.mine), channel_id=1, source_target_pairs={{0,1},{1,0},{2,3},{3,2},{4,5},{5,4},{6,7},{7,6},{8,9},{9,8},{10,11... | collective-permute-start | bytes 614408 | tf_op jit(solution)/shard_map/ppermute | solution.py:334
  103.8 3.3 %collective-permute-start.14 = (f32[136,256]{1,0:T(8,128)S(1)}, f32[136,256]{1,0:T(8,128)S(1)}, u32[]{:S(2)}, u32[]{:S(2)}) collective-permute-start(f32[136,256]{1,0:T(8,128)S(1)} %slice.87), channel_id=1, source_target_pairs={{129,1},{131,3},{133,5},{135,7},{137,9},{139,11},{141,13},{143,15}... | collective-permute-start | bytes 417800 | tf_op jit(solution)/shard_map/ppermute | solution.py:363
  104.5 8.8 %collective-permute-start.15 = (f32[136,256]{1,0:T(8,128)S(1)}, f32[136,256]{1,0:T(8,128)S(1)}, u32[]{:S(2)}, u32[]{:S(2)}) collective-permute-start(f32[136,256]{1,0:T(8,128)S(1)} %slice.87), channel_id=1, source_target_pairs={{129,0},{131,2},{133,4},{135,6},{137,8},{139,10},{141,12},{143,14}... | collective-permute-start | bytes 417800 | tf_op jit(solution)/shard_map/ppermute | solution.py:363

commit v8 on v7

--- a/solution.py
+++ b/solution.py
@@ -268,20 +268,16 @@
         rest[NS:] = mdot(own[HALF:], turned) + held[NS:]
 
 
-def end_kernel(to_second, to_first, turned0, held0, turned1, held1, cov_out, mean, cov, done):
+def end_kernel(to_second, to_first, turned0, held0, turned1, held1, cov, mean):
     after = to_second[...] + to_first[...]
     inner = unpacked(after[:HALF], after[HALF + 1 : HALF + 2, :HALF])
-    copies = [pltpu.make_async_copy(cov.at[i], cov_out.at[i], done.at[i]) for i in range(2)]
     for i, (turned, held) in enumerate(((turned0, held0), (turned1, held1))):
         gain = turned[...]
         cov[i] = tdot(gain, mdot(inner, gain)) + held[:NS]
-        copies[i].start()
         mean[i : i + 1] = (mdot(after[HALF:], gain) + held[NS:])[:1]
-    for copy in copies:
-        copy.wait()
-
-
-def call(kernel, shapes, scalar, *arrays, far_in=False, far_out=(), scratch=()):
+
+
+def call(kernel, shapes, scalar, *arrays, far_in=False, scratch=()):
     vmem = pl.BlockSpec(memory_space=pltpu.VMEM)
     far = pl.BlockSpec(memory_space=pltpu.HBM)
     smem = pl.BlockSpec(memory_space=pltpu.SMEM)
@@ -291,7 +287,7 @@
         kernel,
         out_shape=outs,
         in_specs=[smem] * len(scalars) + [far if far_in else vmem] * len(arrays),
-        out_specs=[far if i in far_out else vmem for i in range(len(outs))],
+        out_specs=[vmem] * len(outs),
         scratch_shapes=scratch,
         compiler_params=pltpu.CompilerParams(vmem_limit_bytes=32 * 1024 * 1024),
     )(*scalars, *arrays)
@@ -347,12 +343,14 @@
             rows, AXES, [(2 * (c + stride) + k, 2 * c + k) for c in range(chips - stride) for k in cores]
         )
 
-    got = fetched(chip, 2, (0, 1))
-    nearer, late[1] = lax.optimization_barrier((chip, late[1]))
-    mine = fetched(nearer, 1, (0, 1))
-    stride = 2
+    got = fetched(chip, 1, (0, 1))
+    passed = swapped(chip[:TOP])
+    mine = call(join_kernel, [(PART, NS)], which, got, chip, passed)
+    got = fetched(mine, 3, (0, 1))
+    mine = fetched(mine, 1, (0, 1))
     passed = swapped(mine[:TOP])
     mine = call(join_kernel, [(PART, NS)], which, got, mine, passed)
+    stride = 4
     while 2 * stride < chips:
         got = fetched(mine, stride, (0, 1))
         passed = swapped(mine[:TOP])
@@ -370,8 +368,7 @@
         late[0], late_held[0], late[1], late_held[1],
     )
     smooth_cov, smooth_mean = call(
-        end_kernel, [(2, NS, NS), (2, NS)], None, to_second, to_first, gain0, rest0, gain1, rest1,
-        far_out=(0,), scratch=[pltpu.VMEM((2, NS, NS), jnp.float32), pltpu.SemaphoreType.DMA((2,))],
+        end_kernel, [(2, NS, NS), (2, NS)], None, to_second, to_first, gain0, rest0, gain1, rest1
     )
     return (smooth_mean, smooth_cov)
 

time: 116 us -> 112 us (0.966)
  waiting for transfers between devices: 73.2 us -> 68.4 us
  starting transfers between devices: 19.3 us -> 20.8 us
    ppermute x7, waiting for transfers between devices: 59.5 us -> 55.4 us  [fetched(): lax.ppermute(rows, AXES, [(2 * (c + stride) + k, 2 * c + k) for c in rang...]
    ppermute x7, starting transfers between devices: 15.6 us -> 16.7 us  [fetched(): lax.ppermute(rows, AXES, [(2 * (c + stride) + k, 2 * c + k) for c in rang...]
  transfers between devices with their start and end apart: 17 -> 17, of which waited for: 14 -> 14; matrix products, arithmetic and copies ran while one was open for 2% -> 3% of each run, Pallas kernels for 1% -> 1%
where the time goes in v8:
time: 112 us
  waiting for transfers between devices  68.4 us (61%)
  starting transfers between devices  20.8 us (19%)
  Pallas kernels  18.9 us (17%)
  matrix products  2.73 us (2%)
    ppermute x7, waiting for transfers between devices, fetched(): lax.ppermute(rows, AXES, [(2 * (c + stride) + k, 2 * c + k) for c in rang...  55.4 us
    pallas_call x10, Pallas kernels, call(): pl.pallas_call(kernel, out_shape=outs, in_specs=[smem] * len(scalars) + [...  18.9 us
    ppermute x7, starting transfers between devices, fetched(): lax.ppermute(rows, AXES, [(2 * (c + stride) + k, 2 * c + k) for c in rang...  16.7 us
    ppermute x8, waiting for transfers between devices, swapped(): return lax.ppermute(rows, AXES, swap)  6.95 us
    ppermute x2, waiting for transfers between devices, local(): lax.ppermute(tails, AXES, [(2 * (c + stride) + 1, 2 * c + k) for c in ran...  6.15 us
    dot_general x6, matrix products, product(): return jnp.matmul(left, right, precision=lax.Precision.HIGHEST)  2.73 us
  transfers between devices with their start and end apart: 17, of which 14 were waited for; matrix products, arithmetic and copies ran while one was open for 3% of the time, Pallas kernels for 1%

profile of v8, /device:TPU:250, one launch (start us, length us, event | category | flops | bytes accessed | tf_op | source)
XLA Modules:
  0.0 112.0 jit_solution(17544141746420871982)
XLA Ops:
  0.6 13.7 %shard_map.59 = (f32[520,256]{1,0:T(8,128)S(1)}, f32[256,256]{1,0:T(8,128)S(1)}, f32[264,256]{1,0:T(8,128)S(1)}) custom-call(s32[1]{0:T(128)} %bitcast.1.final, f32[2,256]{1,0:T(2,128)} %mean_in.1, f32[2,256,256]{2,1,0:T(8,128)} %cov_in.1, f32[2,256,256]{2,1,0:T(8,128)} %noise_in.1, f32[256,256]{1,0:T(8,128)} %step_in.1), custom_call_target="tpu_custom_call" | custom-call | tf_op jit(solution)/shard_map/pallas_call | solution.py:286
  14.5 1.9 %collective-permute-done.other = f32[520,256]{1,0:T(8,128)S(1)} collective-permute-done((f32[520,256]{1,0:T(8,128)S(1)}, f32[520,256]{1,0:T(8,128)S(1)}, u32[]{:S(2)}, u32[]{:S(2)}) %collective-permute-start) | collective-permute-done | bytes 532512 | tf_op jit(solution)/shard_map/ppermute | solution.py:330
  16.6 2.7 %collective-permute-start.1 = (f32[200,256]{1,0:T(8,128)S(1)}, f32[200,256]{1,0:T(8,128)S(1)}, u32[]{:S(2)}, u32[]{:S(2)}) collective-permute-start(f32[200,256]{1,0:T(8,128)S(1)} %shard_map.60.mine), channel_id=1, source_target_pairs={{2,0},{3,1},{4,2},{5,3},{6,4},{7,5},{8,6},{9,7},{10,8},{11,9},{12,... | collective-permute-start | bytes 614408 | tf_op jit(solution)/shard_map/ppermute | solution.py:342
  19.7 0.4 fusion.2
  20.1 0.6 convolution_add_fusion
  20.8 9.4 %collective-permute-done.1.got = f32[200,256]{1,0:T(8,128)S(1)} collective-permute-done((f32[200,256]{1,0:T(8,128)S(1)}, f32[200,256]{1,0:T(8,128)S(1)}, u32[]{:S(2)}, u32[]{:S(2)}) %collective-permute-start.1) | collective-permute-done | bytes 204832 | tf_op jit(solution)/shard_map/ppermute | solution.py:342
  30.6 1.9 %collective-permute-start.4 = (f32[200,256]{1,0:T(8,128)S(1)}, f32[200,256]{1,0:T(8,128)S(1)}, u32[]{:S(2)}, u32[]{:S(2)}) collective-permute-start(f32[200,256]{1,0:T(8,128)S(1)} %shard_map.61), channel_id=1, source_target_pairs={{2,0},{3,1},{4,2},{5,3},{6,4},{7,5},{8,6},{9,7},{10,8},{11,9},{12,... | collective-permute-start | bytes 614408 | tf_op jit(solution)/shard_map/ppermute | solution.py:342
  32.5 0.4 fusion.4
  32.9 3.5 %collective-permute-start.3 = (f32[200,256]{1,0:T(8,128)S(1)}, f32[200,256]{1,0:T(8,128)S(1)}, u32[]{:S(2)}, u32[]{:S(2)}) collective-permute-start(f32[200,256]{1,0:T(8,128)S(1)} %shard_map.61), channel_id=1, source_target_pairs={{6,0},{7,1},{8,2},{9,3},{10,4},{11,5},{12,6},{13,7},{14,8},{15,9},... | collective-permute-start | bytes 614408 | tf_op jit(solution)/shard_map/ppermute | solution.py:342
  36.3 8.2 %collective-permute-done.4.mine = f32[200,256]{1,0:T(8,128)S(1)} collective-permute-done((f32[200,256]{1,0:T(8,128)S(1)}, f32[200,256]{1,0:T(8,128)S(1)}, u32[]{:S(2)}, u32[]{:S(2)}) %collective-permute-start.4) | collective-permute-done | bytes 204832 | tf_op jit(solution)/shard_map/ppermute | solution.py:342
  44.7 0.6 convolution_add_fusion.1
  45.3 0.8 collective-permute-done.5.passed
  46.4 1.9 %collective-permute-start.6 = (f32[200,256]{1,0:T(8,128)S(1)}, f32[200,256]{1,0:T(8,128)S(1)}, u32[]{:S(2)}, u32[]{:S(2)}) collective-permute-start(f32[200,256]{1,0:T(8,128)S(1)} %shard_map.62.mine), channel_id=1, source_target_pairs={{8,0},{9,1},{10,2},{11,3},{12,4},{13,5},{14,6},{15,7},{16,8},{17,9... | collective-permute-start | bytes 614408 | tf_op jit(solution)/shard_map/ppermute | solution.py:342
  48.3 0.7 collective-permute-start.7
  49.0 0.4 convolution_select_fusion.turned1
  49.4 0.7 collective-permute-done.7.passed
  50.1 7.9 %collective-permute-done.6.got = f32[200,256]{1,0:T(8,128)S(1)} collective-permute-done((f32[200,256]{1,0:T(8,128)S(1)}, f32[200,256]{1,0:T(8,128)S(1)}, u32[]{:S(2)}, u32[]{:S(2)}) %collective-permute-start.6) | collective-permute-done | bytes 204832 | tf_op jit(solution)/shard_map/ppermute | solution.py:342
  58.3 1.9 %collective-permute-start.8 = (f32[200,256]{1,0:T(8,128)S(1)}, f32[200,256]{1,0:T(8,128)S(1)}, u32[]{:S(2)}, u32[]{:S(2)}) collective-permute-start(f32[200,256]{1,0:T(8,128)S(1)} %shard_map.63.mine), channel_id=1, source_target_pairs={{16,0},{17,1},{18,2},{19,3},{20,4},{21,5},{22,6},{23,7},{24,8},{25... | collective-permute-start | bytes 614408 | tf_op jit(solution)/shard_map/ppermute | solution.py:342
  60.5 0.4 convolution_select_fusion.1.turned0
  60.9 0.8 collective-permute-done.9.passed
  61.7 10.3 %collective-permute-done.8.got = f32[200,256]{1,0:T(8,128)S(1)} collective-permute-done((f32[200,256]{1,0:T(8,128)S(1)}, f32[200,256]{1,0:T(8,128)S(1)}, u32[]{:S(2)}, u32[]{:S(2)}) %collective-permute-start.8) | collective-permute-done | bytes 204832 | tf_op jit(solution)/shard_map/ppermute | solution.py:342
  72.3 2.6 %collective-permute-start.10 = (f32[200,256]{1,0:T(8,128)S(1)}, f32[200,256]{1,0:T(8,128)S(1)}, u32[]{:S(2)}, u32[]{:S(2)}) collective-permute-start(f32[200,256]{1,0:T(8,128)S(1)} %shard_map.64.mine), channel_id=1, source_target_pairs={{32,0},{33,1},{34,2},{35,3},{36,4},{37,5},{38,6},{39,7},{40,8},{41... | collective-permute-start | bytes 614408 | tf_op jit(solution)/shard_map/ppermute | solution.py:342
  75.0 1.4 %collective-permute-done.11.passed = f32[192,256]{1,0:T(8,128)S(1)} collective-permute-done((f32[192,256]{1,0:T(8,128)S(1)}, f32[192,256]{1,0:T(8,128)S(1)}, u32[]{:S(2)}, u32[]{:S(2)}) %collective-permute-start.11) | collective-permute-done | bytes 196640 | tf_op jit(solution)/shard_map/ppermute | solution.py:330
  76.4 12.8 %collective-permute-done.10.got = f32[200,256]{1,0:T(8,128)S(1)} collective-permute-done((f32[200,256]{1,0:T(8,128)S(1)}, f32[200,256]{1,0:T(8,128)S(1)}, u32[]{:S(2)}, u32[]{:S(2)}) %collective-permute-start.10) | collective-permute-done | bytes 204832 | tf_op jit(solution)/shard_map/ppermute | solution.py:342
  89.5 2.3 %collective-permute-start.12 = (f32[200,256]{1,0:T(8,128)S(1)}, f32[200,256]{1,0:T(8,128)S(1)}, u32[]{:S(2)}, u32[]{:S(2)}) collective-permute-start(f32[200,256]{1,0:T(8,128)S(1)} %shard_map.65.mine), channel_id=1, source_target_pairs={{64,0},{65,1},{66,2},{67,3},{68,4},{69,5},{70,6},{71,7},{72,8},{73... | collective-permute-start | bytes 614408 | tf_op jit(solution)/shard_map/ppermute | solution.py:342
  92.1 1.2 %collective-permute-done.13.passed = f32[192,256]{1,0:T(8,128)S(1)} collective-permute-done((f32[192,256]{1,0:T(8,128)S(1)}, f32[192,256]{1,0:T(8,128)S(1)}, u32[]{:S(2)}, u32[]{:S(2)}) %collective-permute-start.13) | collective-permute-done | bytes 196640 | tf_op jit(solution)/shard_map/ppermute | solution.py:330
  93.3 6.7 %collective-permute-done.12.got = f32[200,256]{1,0:T(8,128)S(1)} collective-permute-done((f32[200,256]{1,0:T(8,128)S(1)}, f32[200,256]{1,0:T(8,128)S(1)}, u32[]{:S(2)}, u32[]{:S(2)}) %collective-permute-start.12) | collective-permute-done | bytes 204832 | tf_op jit(solution)/shard_map/ppermute | solution.py:342
  100.4 0.7 collective-permute-start.14
  101.1 1.3 %collective-permute-start.15 = (f32[136,256]{1,0:T(8,128)S(1)}, f32[136,256]{1,0:T(8,128)S(1)}, u32[]{:S(2)}, u32[]{:S(2)}) collective-permute-start(f32[136,256]{1,0:T(8,128)S(1)} %slice.86), channel_id=1, source_target_pairs={{129,0},{131,2},{133,4},{135,6},{137,8},{139,10},{141,12},{143,14}... | collective-permute-start | bytes 417800 | tf_op jit(solution)/shard_map/ppermute | solution.py:361
  102.4 1.3 %shard_map.67 = (f32[256,256]{1,0:T(8,128)S(1)}, f32[264,256]{1,0:T(8,128)S(1)}, f32[256,256]{1,0:T(8,128)S(1)}, f32[264,256]{1,0:T(8,128)S(1)}) custom-call(s32[1]{0:T(128)} %bitcast.core, f32[200,256]{1,0:T(8,128)S(1)} %shard_map.66.mine, f32[200,256]{1,0:T(8,128)S(1)} %collective-permute-done.16.passed, f32[256,256]{1,0:T(8,128)S(1)} %convolution_select_fusion.1.turned0, ...), custom_call_target="tpu_custom_call" | custom-call | tf_op jit(solution)/shard_map/pallas_call | solution.py:286
  103.7 6.1 %collective-permute-done.15.to_first = f32[136,256]{1,0:T(8,128)S(1)} collective-permute-done((f32[136,256]{1,0:T(8,128)S(1)}, f32[136,256]{1,0:T(8,128)S(1)}, u32[]{:S(2)}, u32[]{:S(2)}) %collective-permute-start.15) | collective-permute-done | bytes 139296 | tf_op jit(solution)/shard_map/ppermute | solution.py:361
  109.9 2.1 %shard_map.68 = (f32[2,256,256]{2,1,0:T(8,128)}, f32[2,256]{1,0:T(2,128)}) custom-call(f32[136,256]{1,0:T(8,128)S(1)} %collective-permute-done.14.to_second, f32[136,256]{1,0:T(8,128)S(1)} %collective-permute-done.15.to_first, f32[256,256]{1,0:T(8,128)S(1)} %get-tuple-element.14.turned0, f32[264,256]{1,0:T(8,128)S(1)} %get-tuple-element.15.held0, ...), custom_call_target="tpu_custom_call" | custom-call | tf_op jit(solution)/shard_map/pallas_call | solution.py:286
  (28 shorter events, 3.6 us)
Async XLA Ops:
  14.3 2.0 %collective-permute-start = (f32[520,256]{1,0:T(8,128)S(1)}, f32[520,256]{1,0:T(8,128)S(1)}, u32[]{:S(2)}, u32[]{:S(2)}) collective-permute-start(f32[520,256]{1,0:T(8,128)S(1)} %get-tuple-element.11.own), channel_id=1, source_target_pairs={{0,1},{1,0},{2,3},{3,2},{4,5},{5,4},{6,7},{7,6},{8,9},{9,8},{10,11... | collective-permute-start | bytes 1597448 | tf_op jit(solution)/shard_map/ppermute | solution.py:330
  16.6 13.6 %collective-permute-start.1 = (f32[200,256]{1,0:T(8,128)S(1)}, f32[200,256]{1,0:T(8,128)S(1)}, u32[]{:S(2)}, u32[]{:S(2)}) collective-permute-start(f32[200,256]{1,0:T(8,128)S(1)} %shard_map.60.mine), channel_id=1, source_target_pairs={{2,0},{3,1},{4,2},{5,3},{6,4},{7,5},{8,6},{9,7},{10,8},{11,9},{12,... | collective-permute-start | bytes 614408 | tf_op jit(solution)/shard_map/ppermute | solution.py:342
  19.3 1.5 %collective-permute-start.2 = (f32[192,256]{1,0:T(8,128)S(1)}, f32[192,256]{1,0:T(8,128)S(1)}, u32[]{:S(2)}, u32[]{:S(2)}) collective-permute-start(f32[192,256]{1,0:T(8,128)S(1)} %slice.80), channel_id=1, source_target_pairs={{0,1},{1,0},{2,3},{3,2},{4,5},{5,4},{6,7},{7,6},{8,9},{9,8},{10,11... | collective-permute-start | bytes 589832 | tf_op jit(solution)/shard_map/ppermute | solution.py:330
  30.6 14.0 %collective-permute-start.4 = (f32[200,256]{1,0:T(8,128)S(1)}, f32[200,256]{1,0:T(8,128)S(1)}, u32[]{:S(2)}, u32[]{:S(2)}) collective-permute-start(f32[200,256]{1,0:T(8,128)S(1)} %shard_map.61), channel_id=1, source_target_pairs={{2,0},{3,1},{4,2},{5,3},{6,4},{7,5},{8,6},{9,7},{10,8},{11,9},{12,... | collective-permute-start | bytes 614408 | tf_op jit(solution)/shard_map/ppermute | solution.py:342
  32.9 12.4 %collective-permute-start.3 = (f32[200,256]{1,0:T(8,128)S(1)}, f32[200,256]{1,0:T(8,128)S(1)}, u32[]{:S(2)}, u32[]{:S(2)}) collective-permute-start(f32[200,256]{1,0:T(8,128)S(1)} %shard_map.61), channel_id=1, source_target_pairs={{6,0},{7,1},{8,2},{9,3},{10,4},{11,5},{12,6},{13,7},{14,8},{15,9},... | collective-permute-start | bytes 614408 | tf_op jit(solution)/shard_map/ppermute | solution.py:342
  44.6 1.5 %collective-permute-start.5 = (f32[192,256]{1,0:T(8,128)S(1)}, f32[192,256]{1,0:T(8,128)S(1)}, u32[]{:S(2)}, u32[]{:S(2)}) collective-permute-start(f32[192,256]{1,0:T(8,128)S(1)} %slice.81), channel_id=1, source_target_pairs={{0,1},{1,0},{2,3},{3,2},{4,5},{5,4},{6,7},{7,6},{8,9},{9,8},{10,11... | collective-permute-start | bytes 589832 | tf_op jit(solution)/shard_map/ppermute | solution.py:330
  46.4 11.6 %collective-permute-start.6 = (f32[200,256]{1,0:T(8,128)S(1)}, f32[200,256]{1,0:T(8,128)S(1)}, u32[]{:S(2)}, u32[]{:S(2)}) collective-permute-start(f32[200,256]{1,0:T(8,128)S(1)} %shard_map.62.mine), channel_id=1, source_target_pairs={{8,0},{9,1},{10,2},{11,3},{12,4},{13,5},{14,6},{15,7},{16,8},{17,9... | collective-permute-start | bytes 614408 | tf_op jit(solution)/shard_map/ppermute | solution.py:342
  48.3 1.7 %collective-permute-start.7 = (f32[192,256]{1,0:T(8,128)S(1)}, f32[192,256]{1,0:T(8,128)S(1)}, u32[]{:S(2)}, u32[]{:S(2)}) collective-permute-start(f32[192,256]{1,0:T(8,128)S(1)} %slice.82), channel_id=1, source_target_pairs={{0,1},{1,0},{2,3},{3,2},{4,5},{5,4},{6,7},{7,6},{8,9},{9,8},{10,11... | collective-permute-start | bytes 589832 | tf_op jit(solution)/shard_map/ppermute | solution.py:330
  58.3 13.7 %collective-permute-start.8 = (f32[200,256]{1,0:T(8,128)S(1)}, f32[200,256]{1,0:T(8,128)S(1)}, u32[]{:S(2)}, u32[]{:S(2)}) collective-permute-start(f32[200,256]{1,0:T(8,128)S(1)} %shard_map.63.mine), channel_id=1, source_target_pairs={{16,0},{17,1},{18,2},{19,3},{20,4},{21,5},{22,6},{23,7},{24,8},{25... | collective-permute-start | bytes 614408 | tf_op jit(solution)/shard_map/ppermute | solution.py:342
  60.2 1.5 %collective-permute-start.9 = (f32[192,256]{1,0:T(8,128)S(1)}, f32[192,256]{1,0:T(8,128)S(1)}, u32[]{:S(2)}, u32[]{:S(2)}) collective-permute-start(f32[192,256]{1,0:T(8,128)S(1)} %slice.83), channel_id=1, source_target_pairs={{0,1},{1,0},{2,3},{3,2},{4,5},{5,4},{6,7},{7,6},{8,9},{9,8},{10,11... | collective-permute-start | bytes 589832 | tf_op jit(solution)/shard_map/ppermute | solution.py:330
  72.3 16.9 %collective-permute-start.10 = (f32[200,256]{1,0:T(8,128)S(1)}, f32[200,256]{1,0:T(8,128)S(1)}, u32[]{:S(2)}, u32[]{:S(2)}) collective-permute-start(f32[200,256]{1,0:T(8,128)S(1)} %shard_map.64.mine), channel_id=1, source_target_pairs={{32,0},{33,1},{34,2},{35,3},{36,4},{37,5},{38,6},{39,7},{40,8},{41... | collective-permute-start | bytes 614408 | tf_op jit(solution)/shard_map/ppermute | solution.py:342
  74.9 1.5 %collective-permute-start.11 = (f32[192,256]{1,0:T(8,128)S(1)}, f32[192,256]{1,0:T(8,128)S(1)}, u32[]{:S(2)}, u32[]{:S(2)}) collective-permute-start(f32[192,256]{1,0:T(8,128)S(1)} %slice.84), channel_id=1, source_target_pairs={{0,1},{1,0},{2,3},{3,2},{4,5},{5,4},{6,7},{7,6},{8,9},{9,8},{10,11... | collective-permute-start | bytes 589832 | tf_op jit(solution)/shard_map/ppermute | solution.py:330
  89.5 10.5 %collective-permute-start.12 = (f32[200,256]{1,0:T(8,128)S(1)}, f32[200,256]{1,0:T(8,128)S(1)}, u32[]{:S(2)}, u32[]{:S(2)}) collective-permute-start(f32[200,256]{1,0:T(8,128)S(1)} %shard_map.65.mine), channel_id=1, source_target_pairs={{64,0},{65,1},{66,2},{67,3},{68,4},{69,5},{70,6},{71,7},{72,8},{73... | collective-permute-start | bytes 614408 | tf_op jit(solution)/shard_map/ppermute | solution.py:342
  91.8 1.5 %collective-permute-start.13 = (f32[192,256]{1,0:T(8,128)S(1)}, f32[192,256]{1,0:T(8,128)S(1)}, u32[]{:S(2)}, u32[]{:S(2)}) collective-permute-start(f32[192,256]{1,0:T(8,128)S(1)} %slice.85), channel_id=1, source_target_pairs={{0,1},{1,0},{2,3},{3,2},{4,5},{5,4},{6,7},{7,6},{8,9},{9,8},{10,11... | collective-permute-start | bytes 589832 | tf_op jit(solution)/shard_map/ppermute | solution.py:330
  100.3 2.1 %collective-permute-start.16 = (f32[200,256]{1,0:T(8,128)S(1)}, f32[200,256]{1,0:T(8,128)S(1)}, u32[]{:S(2)}, u32[]{:S(2)}) collective-permute-start(f32[200,256]{1,0:T(8,128)S(1)} %shard_map.66.mine), channel_id=1, source_target_pairs={{0,1},{1,0},{2,3},{3,2},{4,5},{5,4},{6,7},{7,6},{8,9},{9,8},{10,11... | collective-permute-start | bytes 614408 | tf_op jit(solution)/shard_map/ppermute | solution.py:330
  100.4 3.3 %collective-permute-start.14 = (f32[136,256]{1,0:T(8,128)S(1)}, f32[136,256]{1,0:T(8,128)S(1)}, u32[]{:S(2)}, u32[]{:S(2)}) collective-permute-start(f32[136,256]{1,0:T(8,128)S(1)} %slice.86), channel_id=1, source_target_pairs={{129,1},{131,3},{133,5},{135,7},{137,9},{139,11},{141,13},{143,15}... | collective-permute-start | bytes 417800 | tf_op jit(solution)/shard_map/ppermute | solution.py:361
  101.1 8.8 %collective-permute-start.15 = (f32[136,256]{1,0:T(8,128)S(1)}, f32[136,256]{1,0:T(8,128)S(1)}, u32[]{:S(2)}, u32[]{:S(2)}) collective-permute-start(f32[136,256]{1,0:T(8,128)S(1)} %slice.86), channel_id=1, source_target_pairs={{129,0},{131,2},{133,4},{135,6},{137,8},{139,10},{141,12},{143,14}... | collective-permute-start | bytes 417800 | tf_op jit(solution)/shard_map/ppermute | solution.py:361

commit v9 on v8

--- a/solution.py
+++ b/solution.py
@@ -343,14 +343,11 @@
             rows, AXES, [(2 * (c + stride) + k, 2 * c + k) for c in range(chips - stride) for k in cores]
         )
 
-    got = fetched(chip, 1, (0, 1))
-    passed = swapped(chip[:TOP])
-    mine = call(join_kernel, [(PART, NS)], which, got, chip, passed)
-    got = fetched(mine, 3, (0, 1))
-    mine = fetched(mine, 1, (0, 1))
+    mine = fetched(chip, 1, (0, 1))
+    got = fetched(chip, 2, (0, 1))
+    stride = 2
     passed = swapped(mine[:TOP])
     mine = call(join_kernel, [(PART, NS)], which, got, mine, passed)
-    stride = 4
     while 2 * stride < chips:
         got = fetched(mine, stride, (0, 1))
         passed = swapped(mine[:TOP])

time: 112 us -> 112 us (level)
  the two profiles are of different devices: /device:TPU:250 before, /device:TPU:240 now
where the time goes in v9:
time: 112 us; the launch traced here: 111 us
  waiting for transfers between devices  68.7 us (61%)
  starting transfers between devices  20.1 us (18%)
  Pallas kernels  18.9 us (17%)
  matrix products  2.73 us (2%)
    ppermute x7, waiting for transfers between devices, fetched(): lax.ppermute(rows, AXES, [(2 * (c + stride) + k, 2 * c + k) for c in rang...  55.6 us
    pallas_call x10, Pallas kernels, call(): pl.pallas_call(kernel, out_shape=outs, in_specs=[smem] * len(scalars) + [...  18.9 us
    ppermute x7, starting transfers between devices, fetched(): lax.ppermute(rows, AXES, [(2 * (c + stride) + k, 2 * c + k) for c in rang...  16.6 us
    ppermute x8, waiting for transfers between devices, swapped(): return lax.ppermute(rows, AXES, swap)  7.02 us
    ppermute x2, waiting for transfers between devices, local(): lax.ppermute(tails, AXES, [(2 * (c + stride) + 1, 2 * c + k) for c in ran...  6.06 us
    dot_general x6, matrix products, product(): return jnp.matmul(left, right, precision=lax.Precision.HIGHEST)  2.73 us
  transfers between devices with their start and end apart: 17, of which 14 were waited for; matrix products, arithmetic and copies ran while one was open for 3% of the time, Pallas kernels for 1%

profile of v9, /device:TPU:240, one launch (start us, length us, event | category | flops | bytes accessed | tf_op | source)
XLA Modules:
  0.0 111.5 jit_solution(17327381409826594536)
XLA Ops:
  0.6 13.7 %shard_map.59 = (f32[520,256]{1,0:T(8,128)S(1)}, f32[256,256]{1,0:T(8,128)S(1)}, f32[264,256]{1,0:T(8,128)S(1)}) custom-call(s32[1]{0:T(128)} %bitcast.1.final, f32[2,256]{1,0:T(2,128)} %mean_in.1, f32[2,256,256]{2,1,0:T(8,128)} %cov_in.1, f32[2,256,256]{2,1,0:T(8,128)} %noise_in.1, f32[256,256]{1,0:T(8,128)} %step_in.1), custom_call_target="tpu_custom_call" | custom-call | tf_op jit(solution)/shard_map/pallas_call | solution.py:286
  14.5 1.9 %collective-permute-done.other = f32[520,256]{1,0:T(8,128)S(1)} collective-permute-done((f32[520,256]{1,0:T(8,128)S(1)}, f32[520,256]{1,0:T(8,128)S(1)}, u32[]{:S(2)}, u32[]{:S(2)}) %collective-permute-start) | collective-permute-done | bytes 532512 | tf_op jit(solution)/shard_map/ppermute | solution.py:330
  16.6 2.4 %collective-permute-start.2 = (f32[200,256]{1,0:T(8,128)S(1)}, f32[200,256]{1,0:T(8,128)S(1)}, u32[]{:S(2)}, u32[]{:S(2)}) collective-permute-start(f32[200,256]{1,0:T(8,128)S(1)} %shard_map.60), channel_id=1, source_target_pairs={{2,0},{3,1},{4,2},{5,3},{6,4},{7,5},{8,6},{9,7},{10,8},{11,9},{12,... | collective-permute-start | bytes 614408 | tf_op jit(solution)/shard_map/ppermute | solution.py:342
  19.0 5.3 %collective-permute-start.1 = (f32[200,256]{1,0:T(8,128)S(1)}, f32[200,256]{1,0:T(8,128)S(1)}, u32[]{:S(2)}, u32[]{:S(2)}) collective-permute-start(f32[200,256]{1,0:T(8,128)S(1)} %shard_map.60), channel_id=1, source_target_pairs={{4,0},{5,1},{6,2},{7,3},{8,4},{9,5},{10,6},{11,7},{12,8},{13,9},{1... | collective-permute-start | bytes 614408 | tf_op jit(solution)/shard_map/ppermute | solution.py:342
  24.3 0.4 fusion.2
  24.6 0.6 convolution_add_fusion
  25.3 1.1 %collective-permute-done.2.mine = f32[200,256]{1,0:T(8,128)S(1)} collective-permute-done((f32[200,256]{1,0:T(8,128)S(1)}, f32[200,256]{1,0:T(8,128)S(1)}, u32[]{:S(2)}, u32[]{:S(2)}) %collective-permute-start.2) | collective-permute-done | bytes 204832 | tf_op jit(solution)/shard_map/ppermute | solution.py:342
  26.5 0.4 fusion.4
  26.9 8.2 %collective-permute-done.1.got = f32[200,256]{1,0:T(8,128)S(1)} collective-permute-done((f32[200,256]{1,0:T(8,128)S(1)}, f32[200,256]{1,0:T(8,128)S(1)}, u32[]{:S(2)}, u32[]{:S(2)}) %collective-permute-start.1) | collective-permute-done | bytes 204832 | tf_op jit(solution)/shard_map/ppermute | solution.py:342
  35.4 1.9 %collective-permute-start.4 = (f32[200,256]{1,0:T(8,128)S(1)}, f32[200,256]{1,0:T(8,128)S(1)}, u32[]{:S(2)}, u32[]{:S(2)}) collective-permute-start(f32[200,256]{1,0:T(8,128)S(1)} %shard_map.61.mine), channel_id=1, source_target_pairs={{4,0},{5,1},{6,2},{7,3},{8,4},{9,5},{10,6},{11,7},{12,8},{13,9},{1... | collective-permute-start | bytes 614408 | tf_op jit(solution)/shard_map/ppermute | solution.py:342
  37.6 0.6 convolution_add_fusion.1
  38.2 0.7 collective-permute-done.5.passed
  38.9 10.1 %collective-permute-done.4.got = f32[200,256]{1,0:T(8,128)S(1)} collective-permute-done((f32[200,256]{1,0:T(8,128)S(1)}, f32[200,256]{1,0:T(8,128)S(1)}, u32[]{:S(2)}, u32[]{:S(2)}) %collective-permute-start.4) | collective-permute-done | bytes 204832 | tf_op jit(solution)/shard_map/ppermute | solution.py:342
  49.3 1.9 %collective-permute-start.6 = (f32[200,256]{1,0:T(8,128)S(1)}, f32[200,256]{1,0:T(8,128)S(1)}, u32[]{:S(2)}, u32[]{:S(2)}) collective-permute-start(f32[200,256]{1,0:T(8,128)S(1)} %shard_map.62.mine), channel_id=1, source_target_pairs={{8,0},{9,1},{10,2},{11,3},{12,4},{13,5},{14,6},{15,7},{16,8},{17,9... | collective-permute-start | bytes 614408 | tf_op jit(solution)/shard_map/ppermute | solution.py:342
  51.3 0.4 convolution_select_fusion.turned1
  51.7 1.0 collective-permute-done.7.passed
  52.7 7.3 %collective-permute-done.6.got = f32[200,256]{1,0:T(8,128)S(1)} collective-permute-done((f32[200,256]{1,0:T(8,128)S(1)}, f32[200,256]{1,0:T(8,128)S(1)}, u32[]{:S(2)}, u32[]{:S(2)}) %collective-permute-start.6) | collective-permute-done | bytes 204832 | tf_op jit(solution)/shard_map/ppermute | solution.py:342
  60.3 1.9 %collective-permute-start.8 = (f32[200,256]{1,0:T(8,128)S(1)}, f32[200,256]{1,0:T(8,128)S(1)}, u32[]{:S(2)}, u32[]{:S(2)}) collective-permute-start(f32[200,256]{1,0:T(8,128)S(1)} %shard_map.63.mine), channel_id=1, source_target_pairs={{16,0},{17,1},{18,2},{19,3},{20,4},{21,5},{22,6},{23,7},{24,8},{25... | collective-permute-start | bytes 614408 | tf_op jit(solution)/shard_map/ppermute | solution.py:342
  62.7 1.0 collective-permute-done.9.passed
  63.8 9.7 %collective-permute-done.8.got = f32[200,256]{1,0:T(8,128)S(1)} collective-permute-done((f32[200,256]{1,0:T(8,128)S(1)}, f32[200,256]{1,0:T(8,128)S(1)}, u32[]{:S(2)}, u32[]{:S(2)}) %collective-permute-start.8) | collective-permute-done | bytes 204832 | tf_op jit(solution)/shard_map/ppermute | solution.py:342
  73.8 1.9 %collective-permute-start.10 = (f32[200,256]{1,0:T(8,128)S(1)}, f32[200,256]{1,0:T(8,128)S(1)}, u32[]{:S(2)}, u32[]{:S(2)}) collective-permute-start(f32[200,256]{1,0:T(8,128)S(1)} %shard_map.64.mine), channel_id=1, source_target_pairs={{32,0},{33,1},{34,2},{35,3},{36,4},{37,5},{38,6},{39,7},{40,8},{41... | collective-permute-start | bytes 614408 | tf_op jit(solution)/shard_map/ppermute | solution.py:342
  75.9 1.3 %collective-permute-done.11.passed = f32[192,256]{1,0:T(8,128)S(1)} collective-permute-done((f32[192,256]{1,0:T(8,128)S(1)}, f32[192,256]{1,0:T(8,128)S(1)}, u32[]{:S(2)}, u32[]{:S(2)}) %collective-permute-start.11) | collective-permute-done | bytes 196640 | tf_op jit(solution)/shard_map/ppermute | solution.py:330
  77.2 12.7 %collective-permute-done.10.got = f32[200,256]{1,0:T(8,128)S(1)} collective-permute-done((f32[200,256]{1,0:T(8,128)S(1)}, f32[200,256]{1,0:T(8,128)S(1)}, u32[]{:S(2)}, u32[]{:S(2)}) %collective-permute-start.10) | collective-permute-done | bytes 204832 | tf_op jit(solution)/shard_map/ppermute | solution.py:342
  90.2 1.3 %collective-permute-start.12 = (f32[200,256]{1,0:T(8,128)S(1)}, f32[200,256]{1,0:T(8,128)S(1)}, u32[]{:S(2)}, u32[]{:S(2)}) collective-permute-start(f32[200,256]{1,0:T(8,128)S(1)} %shard_map.65.mine), channel_id=1, source_target_pairs={{64,0},{65,1},{66,2},{67,3},{68,4},{69,5},{70,6},{71,7},{72,8},{73... | collective-permute-start | bytes 614408 | tf_op jit(solution)/shard_map/ppermute | solution.py:342
  91.5 0.5 collective-permute-start.13
  92.1 1.0 collective-permute-done.13.passed
  93.1 6.4 %collective-permute-done.12.got = f32[200,256]{1,0:T(8,128)S(1)} collective-permute-done((f32[200,256]{1,0:T(8,128)S(1)}, f32[200,256]{1,0:T(8,128)S(1)}, u32[]{:S(2)}, u32[]{:S(2)}) %collective-permute-start.12) | collective-permute-done | bytes 204832 | tf_op jit(solution)/shard_map/ppermute | solution.py:342
  100.0 0.7 collective-permute-start.14
  100.7 1.3 %collective-permute-start.15 = (f32[136,256]{1,0:T(8,128)S(1)}, f32[136,256]{1,0:T(8,128)S(1)}, u32[]{:S(2)}, u32[]{:S(2)}) collective-permute-start(f32[136,256]{1,0:T(8,128)S(1)} %slice.86), channel_id=1, source_target_pairs={{129,0},{131,2},{133,4},{135,6},{137,8},{139,10},{141,12},{143,14}... | collective-permute-start | bytes 417800 | tf_op jit(solution)/shard_map/ppermute | solution.py:358
  102.0 1.3 %shard_map.67 = (f32[256,256]{1,0:T(8,128)S(1)}, f32[264,256]{1,0:T(8,128)S(1)}, f32[256,256]{1,0:T(8,128)S(1)}, f32[264,256]{1,0:T(8,128)S(1)}) custom-call(s32[1]{0:T(128)} %bitcast.core, f32[200,256]{1,0:T(8,128)S(1)} %shard_map.66.mine, f32[200,256]{1,0:T(8,128)S(1)} %collective-permute-done.16.passed, f32[256,256]{1,0:T(8,128)S(1)} %convolution_select_fusion.1.turned0, ...), custom_call_target="tpu_custom_call" | custom-call | tf_op jit(solution)/shard_map/pallas_call | solution.py:286
  103.3 6.1 %collective-permute-done.15.to_first = f32[136,256]{1,0:T(8,128)S(1)} collective-permute-done((f32[136,256]{1,0:T(8,128)S(1)}, f32[136,256]{1,0:T(8,128)S(1)}, u32[]{:S(2)}, u32[]{:S(2)}) %collective-permute-start.15) | collective-permute-done | bytes 139296 | tf_op jit(solution)/shard_map/ppermute | solution.py:358
  109.4 2.1 %shard_map.68 = (f32[2,256,256]{2,1,0:T(8,128)}, f32[2,256]{1,0:T(2,128)}) custom-call(f32[136,256]{1,0:T(8,128)S(1)} %collective-permute-done.14.to_second, f32[136,256]{1,0:T(8,128)S(1)} %collective-permute-done.15.to_first, f32[256,256]{1,0:T(8,128)S(1)} %get-tuple-element.14.turned0, f32[264,256]{1,0:T(8,128)S(1)} %get-tuple-element.15.held0, ...), custom_call_target="tpu_custom_call" | custom-call | tf_op jit(solution)/shard_map/pallas_call | solution.py:286
  (28 shorter events, 3.4 us)
Async XLA Ops:
  14.3 2.0 %collective-permute-start = (f32[520,256]{1,0:T(8,128)S(1)}, f32[520,256]{1,0:T(8,128)S(1)}, u32[]{:S(2)}, u32[]{:S(2)}) collective-permute-start(f32[520,256]{1,0:T(8,128)S(1)} %get-tuple-element.11.own), channel_id=1, source_target_pairs={{0,1},{1,0},{2,3},{3,2},{4,5},{5,4},{6,7},{7,6},{8,9},{9,8},{10,11... | collective-permute-start | bytes 1597448 | tf_op jit(solution)/shard_map/ppermute | solution.py:330
  16.6 9.8 %collective-permute-start.2 = (f32[200,256]{1,0:T(8,128)S(1)}, f32[200,256]{1,0:T(8,128)S(1)}, u32[]{:S(2)}, u32[]{:S(2)}) collective-permute-start(f32[200,256]{1,0:T(8,128)S(1)} %shard_map.60), channel_id=1, source_target_pairs={{2,0},{3,1},{4,2},{5,3},{6,4},{7,5},{8,6},{9,7},{10,8},{11,9},{12,... | collective-permute-start | bytes 614408 | tf_op jit(solution)/shard_map/ppermute | solution.py:342
  19.0 16.1 %collective-permute-start.1 = (f32[200,256]{1,0:T(8,128)S(1)}, f32[200,256]{1,0:T(8,128)S(1)}, u32[]{:S(2)}, u32[]{:S(2)}) collective-permute-start(f32[200,256]{1,0:T(8,128)S(1)} %shard_map.60), channel_id=1, source_target_pairs={{4,0},{5,1},{6,2},{7,3},{8,4},{9,5},{10,6},{11,7},{12,8},{13,9},{1... | collective-permute-start | bytes 614408 | tf_op jit(solution)/shard_map/ppermute | solution.py:342
  26.4 8.7 %collective-permute-start.3 = (f32[192,256]{1,0:T(8,128)S(1)}, f32[192,256]{1,0:T(8,128)S(1)}, u32[]{:S(2)}, u32[]{:S(2)}) collective-permute-start(f32[192,256]{1,0:T(8,128)S(1)} %slice.80), channel_id=1, source_target_pairs={{0,1},{1,0},{2,3},{3,2},{4,5},{5,4},{6,7},{7,6},{8,9},{9,8},{10,11... | collective-permute-start | bytes 589832 | tf_op jit(solution)/shard_map/ppermute | solution.py:330
  35.4 13.6 %collective-permute-start.4 = (f32[200,256]{1,0:T(8,128)S(1)}, f32[200,256]{1,0:T(8,128)S(1)}, u32[]{:S(2)}, u32[]{:S(2)}) collective-permute-start(f32[200,256]{1,0:T(8,128)S(1)} %shard_map.61.mine), channel_id=1, source_target_pairs={{4,0},{5,1},{6,2},{7,3},{8,4},{9,5},{10,6},{11,7},{12,8},{13,9},{1... | collective-permute-start | bytes 614408 | tf_op jit(solution)/shard_map/ppermute | solution.py:342
  37.3 1.5 %collective-permute-start.5 = (f32[192,256]{1,0:T(8,128)S(1)}, f32[192,256]{1,0:T(8,128)S(1)}, u32[]{:S(2)}, u32[]{:S(2)}) collective-permute-start(f32[192,256]{1,0:T(8,128)S(1)} %slice.81), channel_id=1, source_target_pairs={{0,1},{1,0},{2,3},{3,2},{4,5},{5,4},{6,7},{7,6},{8,9},{9,8},{10,11... | collective-permute-start | bytes 589832 | tf_op jit(solution)/shard_map/ppermute | solution.py:330
  49.3 10.8 %collective-permute-start.6 = (f32[200,256]{1,0:T(8,128)S(1)}, f32[200,256]{1,0:T(8,128)S(1)}, u32[]{:S(2)}, u32[]{:S(2)}) collective-permute-start(f32[200,256]{1,0:T(8,128)S(1)} %shard_map.62.mine), channel_id=1, source_target_pairs={{8,0},{9,1},{10,2},{11,3},{12,4},{13,5},{14,6},{15,7},{16,8},{17,9... | collective-permute-start | bytes 614408 | tf_op jit(solution)/shard_map/ppermute | solution.py:342
  51.2 1.5 %collective-permute-start.7 = (f32[192,256]{1,0:T(8,128)S(1)}, f32[192,256]{1,0:T(8,128)S(1)}, u32[]{:S(2)}, u32[]{:S(2)}) collective-permute-start(f32[192,256]{1,0:T(8,128)S(1)} %slice.82), channel_id=1, source_target_pairs={{0,1},{1,0},{2,3},{3,2},{4,5},{5,4},{6,7},{7,6},{8,9},{9,8},{10,11... | collective-permute-start | bytes 589832 | tf_op jit(solution)/shard_map/ppermute | solution.py:330
  60.3 13.2 %collective-permute-start.8 = (f32[200,256]{1,0:T(8,128)S(1)}, f32[200,256]{1,0:T(8,128)S(1)}, u32[]{:S(2)}, u32[]{:S(2)}) collective-permute-start(f32[200,256]{1,0:T(8,128)S(1)} %shard_map.63.mine), channel_id=1, source_target_pairs={{16,0},{17,1},{18,2},{19,3},{20,4},{21,5},{22,6},{23,7},{24,8},{25... | collective-permute-start | bytes 614408 | tf_op jit(solution)/shard_map/ppermute | solution.py:342
  62.2 1.5 %collective-permute-start.9 = (f32[192,256]{1,0:T(8,128)S(1)}, f32[192,256]{1,0:T(8,128)S(1)}, u32[]{:S(2)}, u32[]{:S(2)}) collective-permute-start(f32[192,256]{1,0:T(8,128)S(1)} %slice.83), channel_id=1, source_target_pairs={{0,1},{1,0},{2,3},{3,2},{4,5},{5,4},{6,7},{7,6},{8,9},{9,8},{10,11... | collective-permute-start | bytes 589832 | tf_op jit(solution)/shard_map/ppermute | solution.py:330
  73.8 16.1 %collective-permute-start.10 = (f32[200,256]{1,0:T(8,128)S(1)}, f32[200,256]{1,0:T(8,128)S(1)}, u32[]{:S(2)}, u32[]{:S(2)}) collective-permute-start(f32[200,256]{1,0:T(8,128)S(1)} %shard_map.64.mine), channel_id=1, source_target_pairs={{32,0},{33,1},{34,2},{35,3},{36,4},{37,5},{38,6},{39,7},{40,8},{41... | collective-permute-start | bytes 614408 | tf_op jit(solution)/shard_map/ppermute | solution.py:342
  75.7 1.5 %collective-permute-start.11 = (f32[192,256]{1,0:T(8,128)S(1)}, f32[192,256]{1,0:T(8,128)S(1)}, u32[]{:S(2)}, u32[]{:S(2)}) collective-permute-start(f32[192,256]{1,0:T(8,128)S(1)} %slice.84), channel_id=1, source_target_pairs={{0,1},{1,0},{2,3},{3,2},{4,5},{5,4},{6,7},{7,6},{8,9},{9,8},{10,11... | collective-permute-start | bytes 589832 | tf_op jit(solution)/shard_map/ppermute | solution.py:330
  90.2 9.3 %collective-permute-start.12 = (f32[200,256]{1,0:T(8,128)S(1)}, f32[200,256]{1,0:T(8,128)S(1)}, u32[]{:S(2)}, u32[]{:S(2)}) collective-permute-start(f32[200,256]{1,0:T(8,128)S(1)} %shard_map.65.mine), channel_id=1, source_target_pairs={{64,0},{65,1},{66,2},{67,3},{68,4},{69,5},{70,6},{71,7},{72,8},{73... | collective-permute-start | bytes 614408 | tf_op jit(solution)/shard_map/ppermute | solution.py:342
  91.5 1.6 %collective-permute-start.13 = (f32[192,256]{1,0:T(8,128)S(1)}, f32[192,256]{1,0:T(8,128)S(1)}, u32[]{:S(2)}, u32[]{:S(2)}) collective-permute-start(f32[192,256]{1,0:T(8,128)S(1)} %slice.85), channel_id=1, source_target_pairs={{0,1},{1,0},{2,3},{3,2},{4,5},{5,4},{6,7},{7,6},{8,9},{9,8},{10,11... | collective-permute-start | bytes 589832 | tf_op jit(solution)/shard_map/ppermute | solution.py:330
  99.8 2.2 %collective-permute-start.16 = (f32[200,256]{1,0:T(8,128)S(1)}, f32[200,256]{1,0:T(8,128)S(1)}, u32[]{:S(2)}, u32[]{:S(2)}) collective-permute-start(f32[200,256]{1,0:T(8,128)S(1)} %shard_map.66.mine), channel_id=1, source_target_pairs={{0,1},{1,0},{2,3},{3,2},{4,5},{5,4},{6,7},{7,6},{8,9},{9,8},{10,11... | collective-permute-start | bytes 614408 | tf_op jit(solution)/shard_map/ppermute | solution.py:330
  100.0 3.3 %collective-permute-start.14 = (f32[136,256]{1,0:T(8,128)S(1)}, f32[136,256]{1,0:T(8,128)S(1)}, u32[]{:S(2)}, u32[]{:S(2)}) collective-permute-start(f32[136,256]{1,0:T(8,128)S(1)} %slice.86), channel_id=1, source_target_pairs={{129,1},{131,3},{133,5},{135,7},{137,9},{139,11},{141,13},{143,15}... | collective-permute-start | bytes 417800 | tf_op jit(solution)/shard_map/ppermute | solution.py:358
  100.7 8.7 %collective-permute-start.15 = (f32[136,256]{1,0:T(8,128)S(1)}, f32[136,256]{1,0:T(8,128)S(1)}, u32[]{:S(2)}, u32[]{:S(2)}) collective-permute-start(f32[136,256]{1,0:T(8,128)S(1)} %slice.86), channel_id=1, source_target_pairs={{129,0},{131,2},{133,4},{135,6},{137,8},{139,10},{141,12},{143,14}... | collective-permute-start | bytes 417800 | tf_op jit(solution)/shard_map/ppermute | solution.py:358

commit v10 on v9

--- a/solution.py
+++ b/solution.py
@@ -98,9 +98,7 @@
 
 
 NS = 256
-TOP = 192
-LOW = NS - TOP
-OFFSET = LOW + HALF
+OFFSET = HALF
 DIAG = OFFSET + 1
 PART = OFFSET + EXTRA
 
@@ -168,12 +166,12 @@
     return jnp.concatenate([diag, jnp.zeros((1, NS - HALF), jnp.float32)], axis=1)
 
 
-def store_held(out, base, half, diag, offset):
-    out[base : base + HALF] = half
-    tail = jnp.concatenate(
+def store_held(out, half, diag, offset):
+    out[:HALF] = half
+    out[HALF:PART] = jnp.concatenate(
         [offset, diag_row(diag), jnp.zeros((EXTRA - 2, NS), jnp.float32)], axis=0
     )
-    out[base + HALF : base + HALF + EXTRA] = tail
+    out[PART:] = jnp.zeros((NS - PART, NS), jnp.float32)
 
 
 def exact(left, right, dims):
@@ -218,47 +216,40 @@
 def chip_kernel(core, own, other, out):
     @pl.when(core[0] == 0)
     def _():
-        out[:TOP] = mdot(other[:TOP], own[:NS])
-        out[TOP:] = jnp.zeros((PART - TOP, NS), jnp.float32)
+        out[...] = mdot(other[:NS], own[:NS])
 
     @pl.when(core[0] == 1)
     def _():
         gain = other[:NS]
-        out[:LOW] = mdot(own[TOP:NS], gain)
         half, diag = sandwich(own[NS : 2 * NS], gain)
         add, add_diag = packed(other[NS : NS + HALF], other[NS + HALF : 2 * NS, HALF:])
         tail = mdot(own[2 * NS :], gain) + other[2 * NS :]
-        store_held(out, LOW, half + add, diag + add_diag, tail[:1])
-
-
-def join_kernel(core, got, mine, passed, out):
+        store_held(out, half + add, diag + add_diag, tail[:1])
+
+
+def join_kernel(core, got, more, mine, passed, out):
     @pl.when(core[0] == 0)
     def _():
-        gain = jnp.concatenate([mine[:TOP], passed[:LOW]], axis=0)
-        out[:TOP] = mdot(got[:TOP], gain)
-        out[TOP:] = jnp.zeros((PART - TOP, NS), jnp.float32)
+        gain = mine[...]
+        out[:PART] = mdot(got[...], gain)
+        out[PART:] = mdot(more[...], gain)
 
     @pl.when(core[0] == 1)
     def _():
-        gain = jnp.concatenate([passed[:TOP], mine[:LOW]], axis=0)
-        out[:LOW] = mdot(got[:LOW], gain)
-        inner = unpacked(got[LOW:OFFSET], got[DIAG : DIAG + 1, :HALF])
+        gain = passed[...]
+        inner = unpacked(got[:HALF], got[DIAG : DIAG + 1, :HALF])
         half, diag = sandwich(inner, gain)
         tail = mdot(got[OFFSET:], gain)
         store_held(
-            out, LOW, half + mine[LOW:OFFSET], diag + mine[DIAG : DIAG + 1, :HALF],
+            out, half + mine[:HALF], diag + mine[DIAG : DIAG + 1, :HALF],
             tail[:1] + mine[OFFSET : OFFSET + 1],
         )
 
 
 def late_kernel(core, mine, passed, turned0, held0, turned1, held1, gain0, rest0, gain1, rest1):
     first = core[0] == 0
-    gain = jnp.where(
-        first,
-        jnp.concatenate([mine[:TOP], passed[:LOW]], axis=0),
-        jnp.concatenate([passed[:TOP], mine[:LOW]], axis=0),
-    )
-    own = jnp.where(first, passed[LOW:], mine[LOW:])
+    gain = jnp.where(first, mine[...], passed[...])
+    own = jnp.where(first, passed[:PART], mine[:PART])
     inner = unpacked(own[:HALF], own[HALF + 1 : HALF + 2, :HALF])
     for turned, held, full, rest in (
         (turned0[...], held0, gain0, rest0), (turned1[...], held1, gain1, rest1)
@@ -330,7 +321,7 @@
         return lax.ppermute(rows, AXES, swap)
 
     other = swapped(both)
-    chip = call(chip_kernel, [(PART, NS)], which, both, other)
+    chip = call(chip_kernel, [(NS, NS)], which, both, other)
     both_turned, both_held = both[:NS], both[NS:]
     late = [jnp.where(is_first, product(other[:NS], t), t) for t in (both_turned, turned1)]
     late_held = [
@@ -343,17 +334,21 @@
             rows, AXES, [(2 * (c + stride) + k, 2 * c + k) for c in range(chips - stride) for k in cores]
         )
 
+    def window(rows, stride):
+        return fetched(rows[:PART], stride, (0, 1)), fetched(rows[PART:], stride, (0,))
+
+    def joined(far, near):
+        passed = lax.ppermute(near, AXES, [(2 * c, 2 * c + 1) for c in range(chips)])
+        return call(join_kernel, [(NS, NS)], which, *far, near, passed)
+
     mine = fetched(chip, 1, (0, 1))
-    got = fetched(chip, 2, (0, 1))
+    far = fetched(chip, 2, (0, 1))
+    mine = joined((far[:PART], far[PART:]), mine)
     stride = 2
-    passed = swapped(mine[:TOP])
-    mine = call(join_kernel, [(PART, NS)], which, got, mine, passed)
     while 2 * stride < chips:
-        got = fetched(mine, stride, (0, 1))
-        passed = swapped(mine[:TOP])
-        mine = call(join_kernel, [(PART, NS)], which, got, mine, passed)
+        mine = joined(window(mine, stride), mine)
         stride *= 2
-    tails = mine[LOW:]
+    tails = mine[:PART]
     to_second, to_first = [
         lax.ppermute(tails, AXES, [(2 * (c + stride) + 1, 2 * c + k) for c in range(chips - stride)])
         for k in (1, 0)

time: 112 us -> 130 us (1.16)
  the two profiles are of different devices: /device:TPU:240 before, /device:TPU:2 now
where the time goes in v10:
time: 130 us; the launch traced here: 129 us
  waiting for transfers between devices  53.7 us (41%)
  starting transfers between devices  52.6 us (40%)
  Pallas kernels  19.1 us (15%)
  matrix products  2.74 us (2%)
    ppermute x12, waiting for transfers between devices, fetched(): lax.ppermute(rows, AXES, [(2 * (c + stride) + k, 2 * c + k) for c in rang...  45.6 us
    ppermute x12, starting transfers between devices, fetched(): lax.ppermute(rows, AXES, [(2 * (c + stride) + k, 2 * c + k) for c in rang...  41.7 us
    pallas_call x10, Pallas kernels, call(): pl.pallas_call(kernel, out_shape=outs, in_specs=[smem] * len(scalars) + [...  19.1 us
    ppermute x6, starting transfers between devices, joined(): lax.ppermute(near, AXES, [(2 * c, 2 * c + 1) for c in range(chips)])  8.69 us
    ppermute x2, waiting for transfers between devices, local(): lax.ppermute(tails, AXES, [(2 * (c + stride) + 1, 2 * c + k) for c in ran...  6.15 us
    dot_general x6, matrix products, product(): return jnp.matmul(left, right, precision=lax.Precision.HIGHEST)  2.74 us
  transfers between devices with their start and end apart: 22, of which 9 were waited for; matrix products, arithmetic and copies ran while one was open for 2% of the time, Pallas kernels for 1%

profile of v10, /device:TPU:2, one launch (start us, length us, event | category | flops | bytes accessed | tf_op | source)
XLA Modules:
  0.0 129.4 jit_solution(6402322210211072416)
XLA Ops:
  0.6 13.7 %shard_map.59 = (f32[520,256]{1,0:T(8,128)S(1)}, f32[256,256]{1,0:T(8,128)S(1)}, f32[264,256]{1,0:T(8,128)S(1)}) custom-call(s32[1]{0:T(128)} %bitcast.1.final, f32[2,256]{1,0:T(2,128)} %mean_in.1, f32[2,256,256]{2,1,0:T(8,128)} %cov_in.1, f32[2,256,256]{2,1,0:T(8,128)} %noise_in.1, f32[256,256]{1,0:T(8,128)} %step_in.1), custom_call_target="tpu_custom_call" | custom-call | tf_op jit(solution)/shard_map/pallas_call | solution.py:277
  14.5 1.9 %collective-permute-done.other = f32[520,256]{1,0:T(8,128)S(1)} collective-permute-done((f32[520,256]{1,0:T(8,128)S(1)}, f32[520,256]{1,0:T(8,128)S(1)}, u32[]{:S(2)}, u32[]{:S(2)}) %collective-permute-start) | collective-permute-done | bytes 532512 | tf_op jit(solution)/shard_map/ppermute | solution.py:321
  16.6 10.2 %collective-permute-start.2 = (f32[256,256]{1,0:T(8,128)S(1)}, f32[256,256]{1,0:T(8,128)S(1)}, u32[]{:S(2)}, u32[]{:S(2)}) collective-permute-start(f32[256,256]{1,0:T(8,128)S(1)} %shard_map.60), channel_id=1, source_target_pairs={{2,0},{3,1},{4,2},{5,3},{6,4},{7,5},{8,6},{9,7},{10,8},{11,9},{12,... | collective-permute-start | bytes 786440 | tf_op jit(solution)/shard_map/ppermute | solution.py:333
  26.8 2.5 %collective-permute-start.1 = (f32[256,256]{1,0:T(8,128)S(1)}, f32[256,256]{1,0:T(8,128)S(1)}, u32[]{:S(2)}, u32[]{:S(2)}) collective-permute-start(f32[256,256]{1,0:T(8,128)S(1)} %shard_map.60), channel_id=1, source_target_pairs={{4,0},{5,1},{6,2},{7,3},{8,4},{9,5},{10,6},{11,7},{12,8},{13,9},{1... | collective-permute-start | bytes 786440 | tf_op jit(solution)/shard_map/ppermute | solution.py:333
  29.4 4.0 %collective-permute-done.2.mine = f32[256,256]{1,0:T(8,128)S(1)} collective-permute-done((f32[256,256]{1,0:T(8,128)S(1)}, f32[256,256]{1,0:T(8,128)S(1)}, u32[]{:S(2)}, u32[]{:S(2)}) %collective-permute-start.2) | collective-permute-done | bytes 262176 | tf_op jit(solution)/shard_map/ppermute | solution.py:333
  33.4 1.3 %collective-permute-start.3 = (f32[256,256]{1,0:T(8,128)S(1)}, f32[256,256]{1,0:T(8,128)S(1)}, u32[]{:S(2)}, u32[]{:S(2)}) collective-permute-start(f32[256,256]{1,0:T(8,128)S(1)} %collective-permute-done.2.mine), channel_id=1, source_target_pairs={{0,1},{2,3},{4,5},{6,7},{8,9},{10,11},{12,13},{14,15},{16,17},{18,... | collective-permute-start | bytes 786440 | tf_op jit(solution)/shard_map/ppermute | solution.py:341
  34.8 5.5 %collective-permute-done.1 = f32[256,256]{1,0:T(8,128)S(1)} collective-permute-done((f32[256,256]{1,0:T(8,128)S(1)}, f32[256,256]{1,0:T(8,128)S(1)}, u32[]{:S(2)}, u32[]{:S(2)}) %collective-permute-start.1) | collective-permute-done | bytes 262176 | tf_op jit(solution)/shard_map/ppermute | solution.py:333
  40.6 2.1 %collective-permute-start.6 = (f32[256,256]{1,0:T(8,128)S(1)}, f32[256,256]{1,0:T(8,128)S(1)}, u32[]{:S(2)}, u32[]{:S(2)}) collective-permute-start(f32[256,256]{1,0:T(8,128)S(1)} %shard_map.61.mine), channel_id=1, source_target_pairs={{0,1},{2,3},{4,5},{6,7},{8,9},{10,11},{12,13},{14,15},{16,17},{18,... | collective-permute-start | bytes 786440 | tf_op jit(solution)/shard_map/ppermute | solution.py:341
  42.7 8.9 %collective-permute-start.4 = (f32[136,256]{1,0:T(8,128)S(1)}, f32[136,256]{1,0:T(8,128)S(1)}, u32[]{:S(2)}, u32[]{:S(2)}) collective-permute-start(f32[136,256]{1,0:T(8,128)S(1)} %slice.106), channel_id=1, source_target_pairs={{4,0},{5,1},{6,2},{7,3},{8,4},{9,5},{10,6},{11,7},{12,8},{13,9},{1... | collective-permute-start | bytes 417800 | tf_op jit(solution)/shard_map/ppermute | solution.py:333
  51.7 1.9 %collective-permute-start.5 = (f32[120,256]{1,0:T(8,128)S(1)}, f32[120,256]{1,0:T(8,128)S(1)}, u32[]{:S(2)}, u32[]{:S(2)}) collective-permute-start(f32[120,256]{1,0:T(8,128)S(1)} %slice.107), channel_id=1, source_target_pairs={{4,0},{6,2},{8,4},{10,6},{12,8},{14,10},{16,12},{18,14},{20,16},{2... | collective-permute-start | bytes 368648 | tf_op jit(solution)/shard_map/ppermute | solution.py:333
  53.6 6.3 %collective-permute-done.5.more = f32[120,256]{1,0:T(8,128)S(1)} collective-permute-done((f32[120,256]{1,0:T(8,128)S(1)}, f32[120,256]{1,0:T(8,128)S(1)}, u32[]{:S(2)}, u32[]{:S(2)}) %collective-permute-start.5) | collective-permute-done | bytes 122912 | tf_op jit(solution)/shard_map/ppermute | solution.py:333
  60.3 1.3 %collective-permute-start.9 = (f32[256,256]{1,0:T(8,128)S(1)}, f32[256,256]{1,0:T(8,128)S(1)}, u32[]{:S(2)}, u32[]{:S(2)}) collective-permute-start(f32[256,256]{1,0:T(8,128)S(1)} %shard_map.62.mine), channel_id=1, source_target_pairs={{0,1},{2,3},{4,5},{6,7},{8,9},{10,11},{12,13},{14,15},{16,17},{18,... | collective-permute-start | bytes 786440 | tf_op jit(solution)/shard_map/ppermute | solution.py:341
  61.6 1.9 %collective-permute-start.7 = (f32[136,256]{1,0:T(8,128)S(1)}, f32[136,256]{1,0:T(8,128)S(1)}, u32[]{:S(2)}, u32[]{:S(2)}) collective-permute-start(f32[136,256]{1,0:T(8,128)S(1)} %slice.108), channel_id=1, source_target_pairs={{8,0},{9,1},{10,2},{11,3},{12,4},{13,5},{14,6},{15,7},{16,8},{17,9... | collective-permute-start | bytes 417800 | tf_op jit(solution)/shard_map/ppermute | solution.py:333
  63.5 2.1 %collective-permute-start.8 = (f32[120,256]{1,0:T(8,128)S(1)}, f32[120,256]{1,0:T(8,128)S(1)}, u32[]{:S(2)}, u32[]{:S(2)}) collective-permute-start(f32[120,256]{1,0:T(8,128)S(1)} %slice.109), channel_id=1, source_target_pairs={{8,0},{10,2},{12,4},{14,6},{16,8},{18,10},{20,12},{22,14},{24,16},... | collective-permute-start | bytes 368648 | tf_op jit(solution)/shard_map/ppermute | solution.py:333
  66.0 4.3 %collective-permute-done.8.more = f32[120,256]{1,0:T(8,128)S(1)} collective-permute-done((f32[120,256]{1,0:T(8,128)S(1)}, f32[120,256]{1,0:T(8,128)S(1)}, u32[]{:S(2)}, u32[]{:S(2)}) %collective-permute-start.8) | collective-permute-done | bytes 122912 | tf_op jit(solution)/shard_map/ppermute | solution.py:333
  70.6 1.3 %collective-permute-start.12 = (f32[256,256]{1,0:T(8,128)S(1)}, f32[256,256]{1,0:T(8,128)S(1)}, u32[]{:S(2)}, u32[]{:S(2)}) collective-permute-start(f32[256,256]{1,0:T(8,128)S(1)} %shard_map.63.mine), channel_id=1, source_target_pairs={{0,1},{2,3},{4,5},{6,7},{8,9},{10,11},{12,13},{14,15},{16,17},{18,... | collective-permute-start | bytes 786440 | tf_op jit(solution)/shard_map/ppermute | solution.py:341
  72.6 2.5 %collective-permute-start.10 = (f32[136,256]{1,0:T(8,128)S(1)}, f32[136,256]{1,0:T(8,128)S(1)}, u32[]{:S(2)}, u32[]{:S(2)}) collective-permute-start(f32[136,256]{1,0:T(8,128)S(1)} %slice.110), channel_id=1, source_target_pairs={{16,0},{17,1},{18,2},{19,3},{20,4},{21,5},{22,6},{23,7},{24,8},{25... | collective-permute-start | bytes 417800 | tf_op jit(solution)/shard_map/ppermute | solution.py:333
  75.1 1.9 %collective-permute-start.11 = (f32[120,256]{1,0:T(8,128)S(1)}, f32[120,256]{1,0:T(8,128)S(1)}, u32[]{:S(2)}, u32[]{:S(2)}) collective-permute-start(f32[120,256]{1,0:T(8,128)S(1)} %slice.111), channel_id=1, source_target_pairs={{16,0},{18,2},{20,4},{22,6},{24,8},{26,10},{28,12},{30,14},{32,16}... | collective-permute-start | bytes 368648 | tf_op jit(solution)/shard_map/ppermute | solution.py:333
  77.4 5.6 %collective-permute-done.11.more = f32[120,256]{1,0:T(8,128)S(1)} collective-permute-done((f32[120,256]{1,0:T(8,128)S(1)}, f32[120,256]{1,0:T(8,128)S(1)}, u32[]{:S(2)}, u32[]{:S(2)}) %collective-permute-start.11) | collective-permute-done | bytes 122912 | tf_op jit(solution)/shard_map/ppermute | solution.py:333
  83.4 1.3 %collective-permute-start.15 = (f32[256,256]{1,0:T(8,128)S(1)}, f32[256,256]{1,0:T(8,128)S(1)}, u32[]{:S(2)}, u32[]{:S(2)}) collective-permute-start(f32[256,256]{1,0:T(8,128)S(1)} %shard_map.64.mine), channel_id=1, source_target_pairs={{0,1},{2,3},{4,5},{6,7},{8,9},{10,11},{12,13},{14,15},{16,17},{18,... | collective-permute-start | bytes 786440 | tf_op jit(solution)/shard_map/ppermute | solution.py:341
  85.3 4.0 %collective-permute-start.13 = (f32[136,256]{1,0:T(8,128)S(1)}, f32[136,256]{1,0:T(8,128)S(1)}, u32[]{:S(2)}, u32[]{:S(2)}) collective-permute-start(f32[136,256]{1,0:T(8,128)S(1)} %slice.112), channel_id=1, source_target_pairs={{32,0},{33,1},{34,2},{35,3},{36,4},{37,5},{38,6},{39,7},{40,8},{41... | collective-permute-start | bytes 417800 | tf_op jit(solution)/shard_map/ppermute | solution.py:333
  89.3 1.9 %collective-permute-start.14 = (f32[120,256]{1,0:T(8,128)S(1)}, f32[120,256]{1,0:T(8,128)S(1)}, u32[]{:S(2)}, u32[]{:S(2)}) collective-permute-start(f32[120,256]{1,0:T(8,128)S(1)} %slice.113), channel_id=1, source_target_pairs={{32,0},{34,2},{36,4},{38,6},{40,8},{42,10},{44,12},{46,14},{48,16}... | collective-permute-start | bytes 368648 | tf_op jit(solution)/shard_map/ppermute | solution.py:333
  91.6 10.9 %collective-permute-done.14.more = f32[120,256]{1,0:T(8,128)S(1)} collective-permute-done((f32[120,256]{1,0:T(8,128)S(1)}, f32[120,256]{1,0:T(8,128)S(1)}, u32[]{:S(2)}, u32[]{:S(2)}) %collective-permute-start.14) | collective-permute-done | bytes 122912 | tf_op jit(solution)/shard_map/ppermute | solution.py:333
  102.9 1.3 %collective-permute-start.18 = (f32[256,256]{1,0:T(8,128)S(1)}, f32[256,256]{1,0:T(8,128)S(1)}, u32[]{:S(2)}, u32[]{:S(2)}) collective-permute-start(f32[256,256]{1,0:T(8,128)S(1)} %shard_map.65.mine), channel_id=1, source_target_pairs={{0,1},{2,3},{4,5},{6,7},{8,9},{10,11},{12,13},{14,15},{16,17},{18,... | collective-permute-start | bytes 786440 | tf_op jit(solution)/shard_map/ppermute | solution.py:341
  104.6 1.9 %collective-permute-start.16 = (f32[136,256]{1,0:T(8,128)S(1)}, f32[136,256]{1,0:T(8,128)S(1)}, u32[]{:S(2)}, u32[]{:S(2)}) collective-permute-start(f32[136,256]{1,0:T(8,128)S(1)} %slice.114), channel_id=1, source_target_pairs={{64,0},{65,1},{66,2},{67,3},{68,4},{69,5},{70,6},{71,7},{72,8},{73... | collective-permute-start | bytes 417800 | tf_op jit(solution)/shard_map/ppermute | solution.py:333
  106.5 1.9 %collective-permute-start.17 = (f32[120,256]{1,0:T(8,128)S(1)}, f32[120,256]{1,0:T(8,128)S(1)}, u32[]{:S(2)}, u32[]{:S(2)}) collective-permute-start(f32[120,256]{1,0:T(8,128)S(1)} %slice.115), channel_id=1, source_target_pairs={{64,0},{66,2},{68,4},{70,6},{72,8},{74,10},{76,12},{78,14},{80,16}... | collective-permute-start | bytes 368648 | tf_op jit(solution)/shard_map/ppermute | solution.py:333
  108.5 8.9 %collective-permute-done.17.more = f32[120,256]{1,0:T(8,128)S(1)} collective-permute-done((f32[120,256]{1,0:T(8,128)S(1)}, f32[120,256]{1,0:T(8,128)S(1)}, u32[]{:S(2)}, u32[]{:S(2)}) %collective-permute-start.17) | collective-permute-done | bytes 122912 | tf_op jit(solution)/shard_map/ppermute | solution.py:333
  117.8 0.7 collective-permute-start.19
  118.5 1.3 collective-permute-start.20
  119.8 1.3 shard_map.67
  121.1 6.1 %collective-permute-done.20.to_first = f32[136,256]{1,0:T(8,128)S(1)} collective-permute-done((f32[136,256]{1,0:T(8,128)S(1)}, f32[136,256]{1,0:T(8,128)S(1)}, u32[]{:S(2)}, u32[]{:S(2)}) %collective-permute-start.20) | collective-permute-done | bytes 139296 | tf_op jit(solution)/shard_map/ppermute | solution.py:353
  127.3 2.1 %shard_map.68 = (f32[2,256,256]{2,1,0:T(8,128)}, f32[2,256]{1,0:T(2,128)}) custom-call(f32[136,256]{1,0:T(8,128)S(1)} %collective-permute-done.19.to_second, f32[136,256]{1,0:T(8,128)S(1)} %collective-permute-done.20.to_first, f32[256,256]{1,0:T(8,128)S(1)} %get-tuple-element.14.turned0, f32[264,256]{1,0:T(8,128)S(1)} %get-tuple-element.15.held0, ...), custom_call_target="tpu_custom_call" | custom-call | tf_op jit(solution)/shard_map/pallas_call | solution.py:277
  (44 shorter events, 5.2 us)
Async XLA Ops:
  14.3 2.0 %collective-permute-start = (f32[520,256]{1,0:T(8,128)S(1)}, f32[520,256]{1,0:T(8,128)S(1)}, u32[]{:S(2)}, u32[]{:S(2)}) collective-permute-start(f32[520,256]{1,0:T(8,128)S(1)} %get-tuple-element.11.own), channel_id=1, source_target_pairs={{0,1},{1,0},{2,3},{3,2},{4,5},{5,4},{6,7},{7,6},{8,9},{9,8},{10,11... | collective-permute-start | bytes 1597448 | tf_op jit(solution)/shard_map/ppermute | solution.py:321
  16.6 16.8 %collective-permute-start.2 = (f32[256,256]{1,0:T(8,128)S(1)}, f32[256,256]{1,0:T(8,128)S(1)}, u32[]{:S(2)}, u32[]{:S(2)}) collective-permute-start(f32[256,256]{1,0:T(8,128)S(1)} %shard_map.60), channel_id=1, source_target_pairs={{2,0},{3,1},{4,2},{5,3},{6,4},{7,5},{8,6},{9,7},{10,8},{11,9},{12,... | collective-permute-start | bytes 786440 | tf_op jit(solution)/shard_map/ppermute | solution.py:333
  26.8 13.4 %collective-permute-start.1 = (f32[256,256]{1,0:T(8,128)S(1)}, f32[256,256]{1,0:T(8,128)S(1)}, u32[]{:S(2)}, u32[]{:S(2)}) collective-permute-start(f32[256,256]{1,0:T(8,128)S(1)} %shard_map.60), channel_id=1, source_target_pairs={{4,0},{5,1},{6,2},{7,3},{8,4},{9,5},{10,6},{11,7},{12,8},{13,9},{1... | collective-permute-start | bytes 786440 | tf_op jit(solution)/shard_map/ppermute | solution.py:333
  33.4 6.8 %collective-permute-start.3 = (f32[256,256]{1,0:T(8,128)S(1)}, f32[256,256]{1,0:T(8,128)S(1)}, u32[]{:S(2)}, u32[]{:S(2)}) collective-permute-start(f32[256,256]{1,0:T(8,128)S(1)} %collective-permute-done.2.mine), channel_id=1, source_target_pairs={{0,1},{2,3},{4,5},{6,7},{8,9},{10,11},{12,13},{14,15},{16,17},{18,... | collective-permute-start | bytes 786440 | tf_op jit(solution)/shard_map/ppermute | solution.py:341
  40.6 19.4 %collective-permute-start.6 = (f32[256,256]{1,0:T(8,128)S(1)}, f32[256,256]{1,0:T(8,128)S(1)}, u32[]{:S(2)}, u32[]{:S(2)}) collective-permute-start(f32[256,256]{1,0:T(8,128)S(1)} %shard_map.61.mine), channel_id=1, source_target_pairs={{0,1},{2,3},{4,5},{6,7},{8,9},{10,11},{12,13},{14,15},{16,17},{18,... | collective-permute-start | bytes 786440 | tf_op jit(solution)/shard_map/ppermute | solution.py:341
  42.7 17.2 %collective-permute-start.4 = (f32[136,256]{1,0:T(8,128)S(1)}, f32[136,256]{1,0:T(8,128)S(1)}, u32[]{:S(2)}, u32[]{:S(2)}) collective-permute-start(f32[136,256]{1,0:T(8,128)S(1)} %slice.106), channel_id=1, source_target_pairs={{4,0},{5,1},{6,2},{7,3},{8,4},{9,5},{10,6},{11,7},{12,8},{13,9},{1... | collective-permute-start | bytes 417800 | tf_op jit(solution)/shard_map/ppermute | solution.py:333
  51.7 8.3 %collective-permute-start.5 = (f32[120,256]{1,0:T(8,128)S(1)}, f32[120,256]{1,0:T(8,128)S(1)}, u32[]{:S(2)}, u32[]{:S(2)}) collective-permute-start(f32[120,256]{1,0:T(8,128)S(1)} %slice.107), channel_id=1, source_target_pairs={{4,0},{6,2},{8,4},{10,6},{12,8},{14,10},{16,12},{18,14},{20,16},{2... | collective-permute-start | bytes 368648 | tf_op jit(solution)/shard_map/ppermute | solution.py:333
  60.3 10.1 %collective-permute-start.9 = (f32[256,256]{1,0:T(8,128)S(1)}, f32[256,256]{1,0:T(8,128)S(1)}, u32[]{:S(2)}, u32[]{:S(2)}) collective-permute-start(f32[256,256]{1,0:T(8,128)S(1)} %shard_map.62.mine), channel_id=1, source_target_pairs={{0,1},{2,3},{4,5},{6,7},{8,9},{10,11},{12,13},{14,15},{16,17},{18,... | collective-permute-start | bytes 786440 | tf_op jit(solution)/shard_map/ppermute | solution.py:341
  61.6 8.7 %collective-permute-start.7 = (f32[136,256]{1,0:T(8,128)S(1)}, f32[136,256]{1,0:T(8,128)S(1)}, u32[]{:S(2)}, u32[]{:S(2)}) collective-permute-start(f32[136,256]{1,0:T(8,128)S(1)} %slice.108), channel_id=1, source_target_pairs={{8,0},{9,1},{10,2},{11,3},{12,4},{13,5},{14,6},{15,7},{16,8},{17,9... | collective-permute-start | bytes 417800 | tf_op jit(solution)/shard_map/ppermute | solution.py:333
  63.5 6.8 %collective-permute-start.8 = (f32[120,256]{1,0:T(8,128)S(1)}, f32[120,256]{1,0:T(8,128)S(1)}, u32[]{:S(2)}, u32[]{:S(2)}) collective-permute-start(f32[120,256]{1,0:T(8,128)S(1)} %slice.109), channel_id=1, source_target_pairs={{8,0},{10,2},{12,4},{14,6},{16,8},{18,10},{20,12},{22,14},{24,16},... | collective-permute-start | bytes 368648 | tf_op jit(solution)/shard_map/ppermute | solution.py:333
  70.6 12.5 %collective-permute-start.12 = (f32[256,256]{1,0:T(8,128)S(1)}, f32[256,256]{1,0:T(8,128)S(1)}, u32[]{:S(2)}, u32[]{:S(2)}) collective-permute-start(f32[256,256]{1,0:T(8,128)S(1)} %shard_map.63.mine), channel_id=1, source_target_pairs={{0,1},{2,3},{4,5},{6,7},{8,9},{10,11},{12,13},{14,15},{16,17},{18,... | collective-permute-start | bytes 786440 | tf_op jit(solution)/shard_map/ppermute | solution.py:341
  72.6 10.5 %collective-permute-start.10 = (f32[136,256]{1,0:T(8,128)S(1)}, f32[136,256]{1,0:T(8,128)S(1)}, u32[]{:S(2)}, u32[]{:S(2)}) collective-permute-start(f32[136,256]{1,0:T(8,128)S(1)} %slice.110), channel_id=1, source_target_pairs={{16,0},{17,1},{18,2},{19,3},{20,4},{21,5},{22,6},{23,7},{24,8},{25... | collective-permute-start | bytes 417800 | tf_op jit(solution)/shard_map/ppermute | solution.py:333
  75.1 8.0 %collective-permute-start.11 = (f32[120,256]{1,0:T(8,128)S(1)}, f32[120,256]{1,0:T(8,128)S(1)}, u32[]{:S(2)}, u32[]{:S(2)}) collective-permute-start(f32[120,256]{1,0:T(8,128)S(1)} %slice.111), channel_id=1, source_target_pairs={{16,0},{18,2},{20,4},{22,6},{24,8},{26,10},{28,12},{30,14},{32,16}... | collective-permute-start | bytes 368648 | tf_op jit(solution)/shard_map/ppermute | solution.py:333
  83.4 19.2 %collective-permute-start.15 = (f32[256,256]{1,0:T(8,128)S(1)}, f32[256,256]{1,0:T(8,128)S(1)}, u32[]{:S(2)}, u32[]{:S(2)}) collective-permute-start(f32[256,256]{1,0:T(8,128)S(1)} %shard_map.64.mine), channel_id=1, source_target_pairs={{0,1},{2,3},{4,5},{6,7},{8,9},{10,11},{12,13},{14,15},{16,17},{18,... | collective-permute-start | bytes 786440 | tf_op jit(solution)/shard_map/ppermute | solution.py:341
  85.3 17.2 %collective-permute-start.13 = (f32[136,256]{1,0:T(8,128)S(1)}, f32[136,256]{1,0:T(8,128)S(1)}, u32[]{:S(2)}, u32[]{:S(2)}) collective-permute-start(f32[136,256]{1,0:T(8,128)S(1)} %slice.112), channel_id=1, source_target_pairs={{32,0},{33,1},{34,2},{35,3},{36,4},{37,5},{38,6},{39,7},{40,8},{41... | collective-permute-start | bytes 417800 | tf_op jit(solution)/shard_map/ppermute | solution.py:333
  89.3 13.2 %collective-permute-start.14 = (f32[120,256]{1,0:T(8,128)S(1)}, f32[120,256]{1,0:T(8,128)S(1)}, u32[]{:S(2)}, u32[]{:S(2)}) collective-permute-start(f32[120,256]{1,0:T(8,128)S(1)} %slice.113), channel_id=1, source_target_pairs={{32,0},{34,2},{36,4},{38,6},{40,8},{42,10},{44,12},{46,14},{48,16}... | collective-permute-start | bytes 368648 | tf_op jit(solution)/shard_map/ppermute | solution.py:333
  102.9 14.5 %collective-permute-start.18 = (f32[256,256]{1,0:T(8,128)S(1)}, f32[256,256]{1,0:T(8,128)S(1)}, u32[]{:S(2)}, u32[]{:S(2)}) collective-permute-start(f32[256,256]{1,0:T(8,128)S(1)} %shard_map.65.mine), channel_id=1, source_target_pairs={{0,1},{2,3},{4,5},{6,7},{8,9},{10,11},{12,13},{14,15},{16,17},{18,... | collective-permute-start | bytes 786440 | tf_op jit(solution)/shard_map/ppermute | solution.py:341
  104.6 12.7 %collective-permute-start.16 = (f32[136,256]{1,0:T(8,128)S(1)}, f32[136,256]{1,0:T(8,128)S(1)}, u32[]{:S(2)}, u32[]{:S(2)}) collective-permute-start(f32[136,256]{1,0:T(8,128)S(1)} %slice.114), channel_id=1, source_target_pairs={{64,0},{65,1},{66,2},{67,3},{68,4},{69,5},{70,6},{71,7},{72,8},{73... | collective-permute-start | bytes 417800 | tf_op jit(solution)/shard_map/ppermute | solution.py:333
  106.5 10.8 %collective-permute-start.17 = (f32[120,256]{1,0:T(8,128)S(1)}, f32[120,256]{1,0:T(8,128)S(1)}, u32[]{:S(2)}, u32[]{:S(2)}) collective-permute-start(f32[120,256]{1,0:T(8,128)S(1)} %slice.115), channel_id=1, source_target_pairs={{64,0},{66,2},{68,4},{70,6},{72,8},{74,10},{76,12},{78,14},{80,16}... | collective-permute-start | bytes 368648 | tf_op jit(solution)/shard_map/ppermute | solution.py:333
  117.7 2.2 %collective-permute-start.21 = (f32[256,256]{1,0:T(8,128)S(1)}, f32[256,256]{1,0:T(8,128)S(1)}, u32[]{:S(2)}, u32[]{:S(2)}) collective-permute-start(f32[256,256]{1,0:T(8,128)S(1)} %shard_map.66.mine), channel_id=1, source_target_pairs={{0,1},{1,0},{2,3},{3,2},{4,5},{5,4},{6,7},{7,6},{8,9},{9,8},{10,11... | collective-permute-start | bytes 786440 | tf_op jit(solution)/shard_map/ppermute | solution.py:321
  117.8 3.3 %collective-permute-start.19 = (f32[136,256]{1,0:T(8,128)S(1)}, f32[136,256]{1,0:T(8,128)S(1)}, u32[]{:S(2)}, u32[]{:S(2)}) collective-permute-start(f32[136,256]{1,0:T(8,128)S(1)} %slice.116), channel_id=1, source_target_pairs={{129,1},{131,3},{133,5},{135,7},{137,9},{139,11},{141,13},{143,15}... | collective-permute-start | bytes 417800 | tf_op jit(solution)/shard_map/ppermute | solution.py:353
  118.5 8.8 %collective-permute-start.20 = (f32[136,256]{1,0:T(8,128)S(1)}, f32[136,256]{1,0:T(8,128)S(1)}, u32[]{:S(2)}, u32[]{:S(2)}) collective-permute-start(f32[136,256]{1,0:T(8,128)S(1)} %slice.116), channel_id=1, source_target_pairs={{129,0},{131,2},{133,4},{135,6},{137,8},{139,10},{141,12},{143,14}... | collective-permute-start | bytes 417800 | tf_op jit(solution)/shard_map/ppermute | solution.py:353

commit v11 on v9

--- a/solution.py
+++ b/solution.py
@@ -349,7 +349,9 @@
     passed = swapped(mine[:TOP])
     mine = call(join_kernel, [(PART, NS)], which, got, mine, passed)
     while 2 * stride < chips:
-        got = fetched(mine, stride, (0, 1))
+        pairs = [(2 * (c + stride) + 1, 2 * c + 1) for c in range(chips - stride)]
+        pairs += [(2 * (c + stride), 2 * c) for c in range(chips - 2 * stride)]
+        got = lax.ppermute(mine, AXES, pairs)
         passed = swapped(mine[:TOP])
         mine = call(join_kernel, [(PART, NS)], which, got, mine, passed)
         stride *= 2

time: 112 us -> 112 us (level)
    ppermute x0 -> x5, waiting for transfers between devices: none -> 46.2 us  [local(): got = lax.ppermute(mine, AXES, pairs)]
    ppermute x7 -> x2, waiting for transfers between devices: 55.6 us -> 9.36 us  [fetched(): lax.ppermute(rows, AXES, [(2 * (c + stride) + k, 2 * c + k) for c in rang...]
    ppermute x7 -> x2, starting transfers between devices: 16.6 us -> 7.61 us  [fetched(): lax.ppermute(rows, AXES, [(2 * (c + stride) + k, 2 * c + k) for c in rang...]
    ppermute x0 -> x5, starting transfers between devices: none -> 8.97 us  [local(): got = lax.ppermute(mine, AXES, pairs)]
where the time goes in v11:
time: 112 us; the launch traced here: 111 us
  waiting for transfers between devices  68.7 us (61%)
  starting transfers between devices  20 us (18%)
  Pallas kernels  18.9 us (17%)
  matrix products  2.73 us (2%)
    ppermute x5, waiting for transfers between devices, local(): got = lax.ppermute(mine, AXES, pairs)  46.2 us
    pallas_call x10, Pallas kernels, call(): pl.pallas_call(kernel, out_shape=outs, in_specs=[smem] * len(scalars) + [...  18.9 us
    ppermute x2, waiting for transfers between devices, fetched(): lax.ppermute(rows, AXES, [(2 * (c + stride) + k, 2 * c + k) for c in rang...  9.36 us
    ppermute x5, starting transfers between devices, local(): got = lax.ppermute(mine, AXES, pairs)  8.97 us
    ppermute x2, starting transfers between devices, fetched(): lax.ppermute(rows, AXES, [(2 * (c + stride) + k, 2 * c + k) for c in rang...  7.61 us
    ppermute x8, waiting for transfers between devices, swapped(): return lax.ppermute(rows, AXES, swap)  7.02 us
    ppermute x2, waiting for transfers between devices, local(): lax.ppermute(tails, AXES, [(2 * (c + stride) + 1, 2 * c + k) for c in ran...  6.15 us
    dot_general x6, matrix products, product(): return jnp.matmul(left, right, precision=lax.Precision.HIGHEST)  2.73 us
  transfers between devices with their start and end apart: 17, of which 14 were waited for; matrix products, arithmetic and copies ran while one was open for 3% of the time, Pallas kernels for 1%

profile of v11, /device:TPU:240, one launch (start us, length us, event | category | flops | bytes accessed | tf_op | source)
XLA Modules:
  0.0 111.5 jit_solution(6380678336841432535)
XLA Ops:
  0.6 13.7 %shard_map.59 = (f32[520,256]{1,0:T(8,128)S(1)}, f32[256,256]{1,0:T(8,128)S(1)}, f32[264,256]{1,0:T(8,128)S(1)}) custom-call(s32[1]{0:T(128)} %bitcast.1.final, f32[2,256]{1,0:T(2,128)} %mean_in.1, f32[2,256,256]{2,1,0:T(8,128)} %cov_in.1, f32[2,256,256]{2,1,0:T(8,128)} %noise_in.1, f32[256,256]{1,0:T(8,128)} %step_in.1), custom_call_target="tpu_custom_call" | custom-call | tf_op jit(solution)/shard_map/pallas_call | solution.py:286
  14.5 1.9 %collective-permute-done.other = f32[520,256]{1,0:T(8,128)S(1)} collective-permute-done((f32[520,256]{1,0:T(8,128)S(1)}, f32[520,256]{1,0:T(8,128)S(1)}, u32[]{:S(2)}, u32[]{:S(2)}) %collective-permute-start) | collective-permute-done | bytes 532512 | tf_op jit(solution)/shard_map/ppermute | solution.py:330
  16.6 2.4 %collective-permute-start.2 = (f32[200,256]{1,0:T(8,128)S(1)}, f32[200,256]{1,0:T(8,128)S(1)}, u32[]{:S(2)}, u32[]{:S(2)}) collective-permute-start(f32[200,256]{1,0:T(8,128)S(1)} %shard_map.60), channel_id=1, source_target_pairs={{2,0},{3,1},{4,2},{5,3},{6,4},{7,5},{8,6},{9,7},{10,8},{11,9},{12,... | collective-permute-start | bytes 614408 | tf_op jit(solution)/shard_map/ppermute | solution.py:342
  19.0 5.3 %collective-permute-start.1 = (f32[200,256]{1,0:T(8,128)S(1)}, f32[200,256]{1,0:T(8,128)S(1)}, u32[]{:S(2)}, u32[]{:S(2)}) collective-permute-start(f32[200,256]{1,0:T(8,128)S(1)} %shard_map.60), channel_id=1, source_target_pairs={{4,0},{5,1},{6,2},{7,3},{8,4},{9,5},{10,6},{11,7},{12,8},{13,9},{1... | collective-permute-start | bytes 614408 | tf_op jit(solution)/shard_map/ppermute | solution.py:342
  24.3 0.4 fusion.2
  24.6 0.6 convolution_add_fusion
  25.3 1.1 %collective-permute-done.2.mine = f32[200,256]{1,0:T(8,128)S(1)} collective-permute-done((f32[200,256]{1,0:T(8,128)S(1)}, f32[200,256]{1,0:T(8,128)S(1)}, u32[]{:S(2)}, u32[]{:S(2)}) %collective-permute-start.2) | collective-permute-done | bytes 204832 | tf_op jit(solution)/shard_map/ppermute | solution.py:342
  26.5 0.4 fusion.4
  26.9 8.2 %collective-permute-done.1.got = f32[200,256]{1,0:T(8,128)S(1)} collective-permute-done((f32[200,256]{1,0:T(8,128)S(1)}, f32[200,256]{1,0:T(8,128)S(1)}, u32[]{:S(2)}, u32[]{:S(2)}) %collective-permute-start.1) | collective-permute-done | bytes 204832 | tf_op jit(solution)/shard_map/ppermute | solution.py:342
  35.4 1.9 %collective-permute-start.4 = (f32[200,256]{1,0:T(8,128)S(1)}, f32[200,256]{1,0:T(8,128)S(1)}, u32[]{:S(2)}, u32[]{:S(2)}) collective-permute-start(f32[200,256]{1,0:T(8,128)S(1)} %shard_map.61.mine), channel_id=1, source_target_pairs={{5,1},{7,3},{9,5},{11,7},{13,9},{15,11},{17,13},{19,15},{21,17},{2... | collective-permute-start | bytes 614408 | tf_op jit(solution)/shard_map/ppermute | solution.py:354
  37.6 0.6 convolution_add_fusion.1
  38.2 0.7 collective-permute-done.5.passed
  38.9 10.1 %collective-permute-done.4.got = f32[200,256]{1,0:T(8,128)S(1)} collective-permute-done((f32[200,256]{1,0:T(8,128)S(1)}, f32[200,256]{1,0:T(8,128)S(1)}, u32[]{:S(2)}, u32[]{:S(2)}) %collective-permute-start.4) | collective-permute-done | bytes 204832 | tf_op jit(solution)/shard_map/ppermute | solution.py:354
  49.3 1.9 %collective-permute-start.6 = (f32[200,256]{1,0:T(8,128)S(1)}, f32[200,256]{1,0:T(8,128)S(1)}, u32[]{:S(2)}, u32[]{:S(2)}) collective-permute-start(f32[200,256]{1,0:T(8,128)S(1)} %shard_map.62.mine), channel_id=1, source_target_pairs={{9,1},{11,3},{13,5},{15,7},{17,9},{19,11},{21,13},{23,15},{25,17},... | collective-permute-start | bytes 614408 | tf_op jit(solution)/shard_map/ppermute | solution.py:354
  51.3 0.4 convolution_select_fusion.turned1
  51.7 1.0 collective-permute-done.7.passed
  52.7 7.3 %collective-permute-done.6.got = f32[200,256]{1,0:T(8,128)S(1)} collective-permute-done((f32[200,256]{1,0:T(8,128)S(1)}, f32[200,256]{1,0:T(8,128)S(1)}, u32[]{:S(2)}, u32[]{:S(2)}) %collective-permute-start.6) | collective-permute-done | bytes 204832 | tf_op jit(solution)/shard_map/ppermute | solution.py:354
  60.3 1.9 %collective-permute-start.8 = (f32[200,256]{1,0:T(8,128)S(1)}, f32[200,256]{1,0:T(8,128)S(1)}, u32[]{:S(2)}, u32[]{:S(2)}) collective-permute-start(f32[200,256]{1,0:T(8,128)S(1)} %shard_map.63.mine), channel_id=1, source_target_pairs={{17,1},{19,3},{21,5},{23,7},{25,9},{27,11},{29,13},{31,15},{33,17}... | collective-permute-start | bytes 614408 | tf_op jit(solution)/shard_map/ppermute | solution.py:354
  62.7 1.0 collective-permute-done.9.passed
  63.8 9.7 %collective-permute-done.8.got = f32[200,256]{1,0:T(8,128)S(1)} collective-permute-done((f32[200,256]{1,0:T(8,128)S(1)}, f32[200,256]{1,0:T(8,128)S(1)}, u32[]{:S(2)}, u32[]{:S(2)}) %collective-permute-start.8) | collective-permute-done | bytes 204832 | tf_op jit(solution)/shard_map/ppermute | solution.py:354
  73.8 1.9 %collective-permute-start.10 = (f32[200,256]{1,0:T(8,128)S(1)}, f32[200,256]{1,0:T(8,128)S(1)}, u32[]{:S(2)}, u32[]{:S(2)}) collective-permute-start(f32[200,256]{1,0:T(8,128)S(1)} %shard_map.64.mine), channel_id=1, source_target_pairs={{33,1},{35,3},{37,5},{39,7},{41,9},{43,11},{45,13},{47,15},{49,17}... | collective-permute-start | bytes 614408 | tf_op jit(solution)/shard_map/ppermute | solution.py:354
  75.9 1.3 %collective-permute-done.11.passed = f32[192,256]{1,0:T(8,128)S(1)} collective-permute-done((f32[192,256]{1,0:T(8,128)S(1)}, f32[192,256]{1,0:T(8,128)S(1)}, u32[]{:S(2)}, u32[]{:S(2)}) %collective-permute-start.11) | collective-permute-done | bytes 196640 | tf_op jit(solution)/shard_map/ppermute | solution.py:330
  77.2 12.7 %collective-permute-done.10.got = f32[200,256]{1,0:T(8,128)S(1)} collective-permute-done((f32[200,256]{1,0:T(8,128)S(1)}, f32[200,256]{1,0:T(8,128)S(1)}, u32[]{:S(2)}, u32[]{:S(2)}) %collective-permute-start.10) | collective-permute-done | bytes 204832 | tf_op jit(solution)/shard_map/ppermute | solution.py:354
  90.2 1.3 %collective-permute-start.12 = (f32[200,256]{1,0:T(8,128)S(1)}, f32[200,256]{1,0:T(8,128)S(1)}, u32[]{:S(2)}, u32[]{:S(2)}) collective-permute-start(f32[200,256]{1,0:T(8,128)S(1)} %shard_map.65.mine), channel_id=1, source_target_pairs={{65,1},{67,3},{69,5},{71,7},{73,9},{75,11},{77,13},{79,15},{81,17}... | collective-permute-start | bytes 614408 | tf_op jit(solution)/shard_map/ppermute | solution.py:354
  91.5 0.5 collective-permute-start.13
  92.1 1.0 collective-permute-done.13.passed
  93.1 6.4 %collective-permute-done.12.got = f32[200,256]{1,0:T(8,128)S(1)} collective-permute-done((f32[200,256]{1,0:T(8,128)S(1)}, f32[200,256]{1,0:T(8,128)S(1)}, u32[]{:S(2)}, u32[]{:S(2)}) %collective-permute-start.12) | collective-permute-done | bytes 204832 | tf_op jit(solution)/shard_map/ppermute | solution.py:354
  99.9 0.7 collective-permute-start.14
  100.6 1.3 %collective-permute-start.15 = (f32[136,256]{1,0:T(8,128)S(1)}, f32[136,256]{1,0:T(8,128)S(1)}, u32[]{:S(2)}, u32[]{:S(2)}) collective-permute-start(f32[136,256]{1,0:T(8,128)S(1)} %slice.86), channel_id=1, source_target_pairs={{129,0},{131,2},{133,4},{135,6},{137,8},{139,10},{141,12},{143,14}... | collective-permute-start | bytes 417800 | tf_op jit(solution)/shard_map/ppermute | solution.py:360
  101.9 1.3 %shard_map.67 = (f32[256,256]{1,0:T(8,128)S(1)}, f32[264,256]{1,0:T(8,128)S(1)}, f32[256,256]{1,0:T(8,128)S(1)}, f32[264,256]{1,0:T(8,128)S(1)}) custom-call(s32[1]{0:T(128)} %bitcast.core, f32[200,256]{1,0:T(8,128)S(1)} %shard_map.66.mine, f32[200,256]{1,0:T(8,128)S(1)} %collective-permute-done.16.passed, f32[256,256]{1,0:T(8,128)S(1)} %convolution_select_fusion.1.turned0, ...), custom_call_target="tpu_custom_call" | custom-call | tf_op jit(solution)/shard_map/pallas_call | solution.py:286
  103.2 6.1 %collective-permute-done.15.to_first = f32[136,256]{1,0:T(8,128)S(1)} collective-permute-done((f32[136,256]{1,0:T(8,128)S(1)}, f32[136,256]{1,0:T(8,128)S(1)}, u32[]{:S(2)}, u32[]{:S(2)}) %collective-permute-start.15) | collective-permute-done | bytes 139296 | tf_op jit(solution)/shard_map/ppermute | solution.py:360
  109.4 2.1 %shard_map.68 = (f32[2,256,256]{2,1,0:T(8,128)}, f32[2,256]{1,0:T(2,128)}) custom-call(f32[136,256]{1,0:T(8,128)S(1)} %collective-permute-done.14.to_second, f32[136,256]{1,0:T(8,128)S(1)} %collective-permute-done.15.to_first, f32[256,256]{1,0:T(8,128)S(1)} %get-tuple-element.14.turned0, f32[264,256]{1,0:T(8,128)S(1)} %get-tuple-element.15.held0, ...), custom_call_target="tpu_custom_call" | custom-call | tf_op jit(solution)/shard_map/pallas_call | solution.py:286
  (28 shorter events, 3.3 us)
Async XLA Ops:
  14.3 2.0 %collective-permute-start = (f32[520,256]{1,0:T(8,128)S(1)}, f32[520,256]{1,0:T(8,128)S(1)}, u32[]{:S(2)}, u32[]{:S(2)}) collective-permute-start(f32[520,256]{1,0:T(8,128)S(1)} %get-tuple-element.11.own), channel_id=1, source_target_pairs={{0,1},{1,0},{2,3},{3,2},{4,5},{5,4},{6,7},{7,6},{8,9},{9,8},{10,11... | collective-permute-start | bytes 1597448 | tf_op jit(solution)/shard_map/ppermute | solution.py:330
  16.6 9.8 %collective-permute-start.2 = (f32[200,256]{1,0:T(8,128)S(1)}, f32[200,256]{1,0:T(8,128)S(1)}, u32[]{:S(2)}, u32[]{:S(2)}) collective-permute-start(f32[200,256]{1,0:T(8,128)S(1)} %shard_map.60), channel_id=1, source_target_pairs={{2,0},{3,1},{4,2},{5,3},{6,4},{7,5},{8,6},{9,7},{10,8},{11,9},{12,... | collective-permute-start | bytes 614408 | tf_op jit(solution)/shard_map/ppermute | solution.py:342
  19.0 16.1 %collective-permute-start.1 = (f32[200,256]{1,0:T(8,128)S(1)}, f32[200,256]{1,0:T(8,128)S(1)}, u32[]{:S(2)}, u32[]{:S(2)}) collective-permute-start(f32[200,256]{1,0:T(8,128)S(1)} %shard_map.60), channel_id=1, source_target_pairs={{4,0},{5,1},{6,2},{7,3},{8,4},{9,5},{10,6},{11,7},{12,8},{13,9},{1... | collective-permute-start | bytes 614408 | tf_op jit(solution)/shard_map/ppermute | solution.py:342
  26.4 8.7 %collective-permute-start.3 = (f32[192,256]{1,0:T(8,128)S(1)}, f32[192,256]{1,0:T(8,128)S(1)}, u32[]{:S(2)}, u32[]{:S(2)}) collective-permute-start(f32[192,256]{1,0:T(8,128)S(1)} %slice.80), channel_id=1, source_target_pairs={{0,1},{1,0},{2,3},{3,2},{4,5},{5,4},{6,7},{7,6},{8,9},{9,8},{10,11... | collective-permute-start | bytes 589832 | tf_op jit(solution)/shard_map/ppermute | solution.py:330
  35.4 13.6 %collective-permute-start.4 = (f32[200,256]{1,0:T(8,128)S(1)}, f32[200,256]{1,0:T(8,128)S(1)}, u32[]{:S(2)}, u32[]{:S(2)}) collective-permute-start(f32[200,256]{1,0:T(8,128)S(1)} %shard_map.61.mine), channel_id=1, source_target_pairs={{5,1},{7,3},{9,5},{11,7},{13,9},{15,11},{17,13},{19,15},{21,17},{2... | collective-permute-start | bytes 614408 | tf_op jit(solution)/shard_map/ppermute | solution.py:354
  37.3 1.5 %collective-permute-start.5 = (f32[192,256]{1,0:T(8,128)S(1)}, f32[192,256]{1,0:T(8,128)S(1)}, u32[]{:S(2)}, u32[]{:S(2)}) collective-permute-start(f32[192,256]{1,0:T(8,128)S(1)} %slice.81), channel_id=1, source_target_pairs={{0,1},{1,0},{2,3},{3,2},{4,5},{5,4},{6,7},{7,6},{8,9},{9,8},{10,11... | collective-permute-start | bytes 589832 | tf_op jit(solution)/shard_map/ppermute | solution.py:330
  49.3 10.8 %collective-permute-start.6 = (f32[200,256]{1,0:T(8,128)S(1)}, f32[200,256]{1,0:T(8,128)S(1)}, u32[]{:S(2)}, u32[]{:S(2)}) collective-permute-start(f32[200,256]{1,0:T(8,128)S(1)} %shard_map.62.mine), channel_id=1, source_target_pairs={{9,1},{11,3},{13,5},{15,7},{17,9},{19,11},{21,13},{23,15},{25,17},... | collective-permute-start | bytes 614408 | tf_op jit(solution)/shard_map/ppermute | solution.py:354
  51.2 1.5 %collective-permute-start.7 = (f32[192,256]{1,0:T(8,128)S(1)}, f32[192,256]{1,0:T(8,128)S(1)}, u32[]{:S(2)}, u32[]{:S(2)}) collective-permute-start(f32[192,256]{1,0:T(8,128)S(1)} %slice.82), channel_id=1, source_target_pairs={{0,1},{1,0},{2,3},{3,2},{4,5},{5,4},{6,7},{7,6},{8,9},{9,8},{10,11... | collective-permute-start | bytes 589832 | tf_op jit(solution)/shard_map/ppermute | solution.py:330
  60.3 13.2 %collective-permute-start.8 = (f32[200,256]{1,0:T(8,128)S(1)}, f32[200,256]{1,0:T(8,128)S(1)}, u32[]{:S(2)}, u32[]{:S(2)}) collective-permute-start(f32[200,256]{1,0:T(8,128)S(1)} %shard_map.63.mine), channel_id=1, source_target_pairs={{17,1},{19,3},{21,5},{23,7},{25,9},{27,11},{29,13},{31,15},{33,17}... | collective-permute-start | bytes 614408 | tf_op jit(solution)/shard_map/ppermute | solution.py:354
  62.2 1.5 %collective-permute-start.9 = (f32[192,256]{1,0:T(8,128)S(1)}, f32[192,256]{1,0:T(8,128)S(1)}, u32[]{:S(2)}, u32[]{:S(2)}) collective-permute-start(f32[192,256]{1,0:T(8,128)S(1)} %slice.83), channel_id=1, source_target_pairs={{0,1},{1,0},{2,3},{3,2},{4,5},{5,4},{6,7},{7,6},{8,9},{9,8},{10,11... | collective-permute-start | bytes 589832 | tf_op jit(solution)/shard_map/ppermute | solution.py:330
  73.8 16.1 %collective-permute-start.10 = (f32[200,256]{1,0:T(8,128)S(1)}, f32[200,256]{1,0:T(8,128)S(1)}, u32[]{:S(2)}, u32[]{:S(2)}) collective-permute-start(f32[200,256]{1,0:T(8,128)S(1)} %shard_map.64.mine), channel_id=1, source_target_pairs={{33,1},{35,3},{37,5},{39,7},{41,9},{43,11},{45,13},{47,15},{49,17}... | collective-permute-start | bytes 614408 | tf_op jit(solution)/shard_map/ppermute | solution.py:354
  75.7 1.5 %collective-permute-start.11 = (f32[192,256]{1,0:T(8,128)S(1)}, f32[192,256]{1,0:T(8,128)S(1)}, u32[]{:S(2)}, u32[]{:S(2)}) collective-permute-start(f32[192,256]{1,0:T(8,128)S(1)} %slice.84), channel_id=1, source_target_pairs={{0,1},{1,0},{2,3},{3,2},{4,5},{5,4},{6,7},{7,6},{8,9},{9,8},{10,11... | collective-permute-start | bytes 589832 | tf_op jit(solution)/shard_map/ppermute | solution.py:330
  90.2 9.3 %collective-permute-start.12 = (f32[200,256]{1,0:T(8,128)S(1)}, f32[200,256]{1,0:T(8,128)S(1)}, u32[]{:S(2)}, u32[]{:S(2)}) collective-permute-start(f32[200,256]{1,0:T(8,128)S(1)} %shard_map.65.mine), channel_id=1, source_target_pairs={{65,1},{67,3},{69,5},{71,7},{73,9},{75,11},{77,13},{79,15},{81,17}... | collective-permute-start | bytes 614408 | tf_op jit(solution)/shard_map/ppermute | solution.py:354
  91.5 1.6 %collective-permute-start.13 = (f32[192,256]{1,0:T(8,128)S(1)}, f32[192,256]{1,0:T(8,128)S(1)}, u32[]{:S(2)}, u32[]{:S(2)}) collective-permute-start(f32[192,256]{1,0:T(8,128)S(1)} %slice.85), channel_id=1, source_target_pairs={{0,1},{1,0},{2,3},{3,2},{4,5},{5,4},{6,7},{7,6},{8,9},{9,8},{10,11... | collective-permute-start | bytes 589832 | tf_op jit(solution)/shard_map/ppermute | solution.py:330
  99.8 2.1 %collective-permute-start.16 = (f32[200,256]{1,0:T(8,128)S(1)}, f32[200,256]{1,0:T(8,128)S(1)}, u32[]{:S(2)}, u32[]{:S(2)}) collective-permute-start(f32[200,256]{1,0:T(8,128)S(1)} %shard_map.66.mine), channel_id=1, source_target_pairs={{0,1},{1,0},{2,3},{3,2},{4,5},{5,4},{6,7},{7,6},{8,9},{9,8},{10,11... | collective-permute-start | bytes 614408 | tf_op jit(solution)/shard_map/ppermute | solution.py:330
  99.9 3.3 %collective-permute-start.14 = (f32[136,256]{1,0:T(8,128)S(1)}, f32[136,256]{1,0:T(8,128)S(1)}, u32[]{:S(2)}, u32[]{:S(2)}) collective-permute-start(f32[136,256]{1,0:T(8,128)S(1)} %slice.86), channel_id=1, source_target_pairs={{129,1},{131,3},{133,5},{135,7},{137,9},{139,11},{141,13},{143,15}... | collective-permute-start | bytes 417800 | tf_op jit(solution)/shard_map/ppermute | solution.py:360
  100.6 8.8 %collective-permute-start.15 = (f32[136,256]{1,0:T(8,128)S(1)}, f32[136,256]{1,0:T(8,128)S(1)}, u32[]{:S(2)}, u32[]{:S(2)}) collective-permute-start(f32[136,256]{1,0:T(8,128)S(1)} %slice.86), channel_id=1, source_target_pairs={{129,0},{131,2},{133,4},{135,6},{137,8},{139,10},{141,12},{143,14}... | collective-permute-start | bytes 417800 | tf_op jit(solution)/shard_map/ppermute | solution.py:360
